TPU v7x, 32 devices: a whole 2x2x4 slice. The times are simulated.
32 devices in a mesh: seq: 8 (over y, x, core), head: 4 (over z).
Axes of the slice: x: 2, y: 2, z: 4, core: 2. Of those that a mesh axis runs over, the one named last changes fastest.
Arguments:
- layer_input: bfloat16 [2, 2048, 1536], P(None, ('seq', 'head')), may hold values from -6 to 6
- segments: int32 [2, 2048], replicated, may hold values from 0 to 2, as said below
- routes: int32 [2, 2048, 8], P(None, ('seq', 'head')), may hold values from 0 to 39, all different within a row
- pair_rank: int32 [2, 2048, 8], P(None, ('seq', 'head')), may hold values from 0 to 1023, as said below
- query_key_value_weight: bfloat16 [1536, 2560], P(('seq', 'head')), may hold values from -0.15625 to 0.15625
- output_weight: bfloat16 [1536, 1536], P(('seq', 'head')), may hold values from -2 to 2
- router_weight: bfloat16 [1536, 40], P(('seq', 'head')), may hold values from -0.078125 to 0.078125
- norm_attn: bfloat16 [1536], P(('seq', 'head')), may hold values from 0.5 to 1.5
- norm_ffn: bfloat16 [1536], P(('seq', 'head')), may hold values from 0.5 to 1.5
- w_gate_up: bfloat16 [40, 1536, 1024], P('head', 'seq'), may hold values from -0.15625 to 0.15625
- w_down: bfloat16 [40, 512, 1536], P('head', 'seq'), may hold values from -1.5 to 1.5
- cotangent: bfloat16 [2, 2048, 1536], P(None, ('seq', 'head')), may hold values from -6 to 6
Outputs:
- mixed_out: bfloat16 [2, 2048, 1536], P(None, ('seq', 'head'))
- d_x: float32 [2, 2048, 1536], P(None, ('seq', 'head'))
- d_w_qkv: float32 [1536, 2560], P(('seq', 'head'))
- d_w_out: float32 [1536, 1536], P(('seq', 'head'))
- d_w_router: float32 [1536, 40], P(('seq', 'head'))
- d_norm_attn: float32 [1536], P(('seq', 'head'))
- d_norm_ffn: float32 [1536], P(('seq', 'head'))
- d_w_gate_up: float32 [40, 1536, 1024], P('head', 'seq')
- d_w_down: float32 [40, 512, 1536], P('head', 'seq')
Inputs may be any that keep to these rules, and one draw needn't show every extreme that they name: `segments`: segment numbers start at 0 and never fall along a sequence. In one sequence, drawn from the seed, all tokens share segment 0; the other holds 3 documents, each of 200 to 2000 tokens. `pair_rank`: over the pairs of one group (positions b * 64 to (b + 1) * 64 - 1 of every sequence, all 8 routes) the ranks are each number of 0 to 1023 once.
All inputs are finite; a program needn't handle non-finite values.
Results may differ from a plain program's by a relative error of at most 0.025.
Values may be sent and summed in bfloat16 or wider, within the bound.
A program may use at most 192 MiB of HBM per device.

v0:
```python
import jax
import jax.numpy as jnp
from jax import lax
from jax.sharding import PartitionSpec as P

MODEL_WIDTH = 1536
QUERY_HEADS = 24
KEY_VALUE_HEADS = 8
HEAD_WIDTH = 64
EXPERTS = 40
FF = 512
CAP = 25


epsilon = 1e-06
negative = -1e30
theta = 10000.0
HIGH_PRECISION = lax.Precision.HIGHEST


def rope_tables(token_positions, head_size):
    half = head_size // 2
    freq = theta ** (-jnp.arange(half, dtype=jnp.float32) / half)
    angle = token_positions.astype(jnp.float32)[:, None] * freq[None, :]
    return (jnp.cos(angle)[None, :, None, None, :], jnp.sin(angle)[None, :, None, None, :])


def rotate(value, cosine, sine):
    half = value.shape[-1] // 2
    first = value[..., :half]
    second = value[..., half:]
    return jnp.concatenate(
        [first * cosine - second * sine, second * cosine + first * sine], axis=-1
    )


def per_device(
    layer_input,
    segments,
    routes,
    pair_rank,
    query_key_value_weight,
    output_weight,
    router_weight,
    norm_attn,
    norm_ffn,
    w_gate_up,
    w_down,
    cotangent,
):
    head_number = lax.axis_size("head")
    sequence_batch, token_rows, width = layer_input.shape
    length = segments.shape[1]
    blk = token_rows * head_number
    query_group = QUERY_HEADS // KEY_VALUE_HEADS
    key_value_location = KEY_VALUE_HEADS // head_number
    loc_experts = w_gate_up.shape[0]
    top = routes.shape[2]
    tokens_present = sequence_batch * token_rows
    pairs = tokens_present * top
    scale = HEAD_WIDTH ** (-0.5)
    f32 = jnp.float32
    bf16 = jnp.bfloat16
    dense_qkv, dense_out, dense_router, gain_attn, gain_ffn = (
        lax.all_gather(query_key_value_weight, ("seq", "head"), axis=0, tiled=True),
        lax.all_gather(output_weight, ("seq", "head"), axis=0, tiled=True),
        lax.all_gather(router_weight, ("seq", "head"), axis=0, tiled=True),
        lax.all_gather(norm_attn, ("seq", "head"), axis=0, tiled=True),
        lax.all_gather(norm_ffn, ("seq", "head"), axis=0, tiled=True),
    )
    expert_up, expert_down = (
        lax.all_gather(w_gate_up, "seq", axis=1, tiled=True),
        lax.all_gather(w_down, "seq", axis=1, tiled=True),
    )
    seq_index = lax.axis_index("seq")
    device = seq_index * head_number + lax.axis_index("head")
    token_positions = device * token_rows + jnp.arange(token_rows, dtype=jnp.int32)
    cosine, sine = rope_tables(token_positions, HEAD_WIDTH)
    tokens = layer_input.reshape(tokens_present, MODEL_WIDTH).astype(f32)
    inverse_one = lax.rsqrt(jnp.mean(tokens * tokens, axis=1, keepdims=True) + epsilon)
    normed_one = tokens * inverse_one
    first_input = (normed_one * gain_attn.astype(f32)).astype(bf16)
    projected_rows = jnp.dot(first_input, dense_qkv, preferred_element_type=f32).reshape(
        sequence_batch, token_rows, KEY_VALUE_HEADS, query_group + 2, HEAD_WIDTH
    )
    turned = rotate(projected_rows[:, :, :, : query_group + 1], cosine, sine)
    packed = (
        jnp.concatenate([turned, projected_rows[:, :, :, query_group + 1 :]], axis=3)
        .astype(bf16)
        .reshape(sequence_batch, token_rows, KEY_VALUE_HEADS * (query_group + 2) * HEAD_WIDTH)
    )
    local = lax.all_to_all(packed, "head", split_axis=2, concat_axis=1, tiled=True).reshape(
        sequence_batch, blk, key_value_location, query_group + 2, HEAD_WIDTH
    )
    query_rows = local[:, :, :, :query_group]
    keys_values = local[:, :, :, query_group:].reshape(
        sequence_batch, blk, key_value_location * 2 * HEAD_WIDTH
    )
    q_start = seq_index * blk
    q_pos = q_start + jnp.arange(blk, dtype=jnp.int32)
    q_seg = lax.dynamic_slice_in_dim(segments, q_start, blk, 1)

    def key_view(piece, offset, token_count):
        portion = lax.dynamic_slice_in_dim(piece, offset, token_count, 1).reshape(
            sequence_batch, token_count, key_value_location, 2, HEAD_WIDTH
        )
        return (portion[:, :, :, 0], portion[:, :, :, 1])

    def key_mask(begin, token_count):
        k_pos = begin + jnp.arange(token_count, dtype=jnp.int32)
        k_seg = lax.dynamic_slice_in_dim(segments, begin, token_count, 1)
        same = q_seg[:, :, None] == k_seg[:, None, :]
        causal = k_pos[None, None, :] <= q_pos[None, :, None]
        return (same & causal)[:, None, None]

    def needed(begin):
        early = begin <= q_start + blk - 1
        return early

    def guarded(function, state, piece, start, offset, token_count):

        def work(inner):
            return function(inner, piece, start, offset, token_count)

        def leave(inner):
            return inner

        return lax.cond(needed(offset), work, leave, state)

    def sweep(function, state, piece, start):
        token_count = piece.shape[1]
        sub = 512

        def turn(index, inner):
            return guarded(function, inner, piece, start, index * sub, sub)

        return lax.fori_loop(0, token_count // sub, turn, state)

    def forward_block(state, piece, start, offset, token_count):
        top_now, total, accum = state
        keys, values = key_view(piece, offset, token_count)
        scores = (
            jnp.einsum("sqhgd,skhd->shgqk", query_rows, keys, preferred_element_type=f32) * scale
        )
        mask = key_mask(offset, token_count)
        scores = jnp.where(mask, scores, negative)
        top_new = jnp.maximum(top_now, jnp.max(scores, axis=-1))
        weights = jnp.where(mask, jnp.exp(scores - top_new[..., None]), 0.0)
        shrink = jnp.exp(top_now - top_new)
        total = total * shrink + jnp.sum(weights, axis=-1)
        accum = accum * shrink[..., None] + jnp.einsum(
            "shgqk,skhd->shgqd", weights.astype(bf16), values, preferred_element_type=f32
        )
        return (top_new, total, accum)

    state_zero = (
        jnp.full((sequence_batch, key_value_location, query_group, blk), negative, f32),
        jnp.zeros((sequence_batch, key_value_location, query_group, blk), f32),
        jnp.zeros((sequence_batch, key_value_location, query_group, blk, HEAD_WIDTH), f32),
    )
    folded = sweep(
        forward_block,
        state_zero,
        lax.all_gather(keys_values, "seq", axis=1, tiled=True),
        jnp.int32(0),
    )
    top_now, total, accum = folded
    lse = top_now + jnp.log(total)
    attended = accum / total[..., None]
    heads_local = (
        attended.transpose(0, 3, 1, 2, 4)
        .reshape(sequence_batch, blk, key_value_location * query_group * HEAD_WIDTH)
        .astype(bf16)
    )
    mixed_heads = lax.all_to_all(
        heads_local, "head", split_axis=1, concat_axis=2, tiled=True
    ).reshape(tokens_present, QUERY_HEADS * HEAD_WIDTH)
    attention_output = jnp.dot(mixed_heads, dense_out, preferred_element_type=f32)
    middle = tokens + attention_output
    inverse_two = lax.rsqrt(jnp.mean(middle * middle, axis=1, keepdims=True) + epsilon)
    normed_two = middle * inverse_two
    gain_ffn_f = gain_ffn.astype(f32)
    second_input = (normed_two * gain_ffn_f).astype(bf16)
    router_logits = jnp.dot(second_input, dense_router, preferred_element_type=f32)
    route_flat = routes.reshape(tokens_present, top)
    hot = route_flat[:, :, None] == jnp.arange(EXPERTS, dtype=jnp.int32)[None, None, :]
    chosen = jnp.sum(jnp.where(hot, router_logits[:, None, :], 0.0), axis=2)
    gates = jax.nn.softmax(chosen, axis=-1)
    expert_of = route_flat.reshape(pairs)
    rank = pair_rank.reshape(pairs)
    order = jnp.zeros((pairs,), jnp.int32).at[rank].set(jnp.arange(pairs, dtype=jnp.int32))
    flags = (expert_of[order][:, None] == jnp.arange(EXPERTS, dtype=jnp.int32)[None, :]).astype(
        jnp.int32
    )
    before = jnp.cumsum(flags, axis=0) - flags
    slot = jnp.sum(before * flags, axis=1)[rank]
    kept = slot < CAP
    spare = EXPERTS * CAP
    target = jnp.where(kept, expert_of * CAP + slot, spare)
    token_of = jnp.arange(pairs, dtype=jnp.int32) // top
    buffer = (
        jnp.zeros((spare + 1, MODEL_WIDTH), bf16)
        .at[target]
        .set(second_input[token_of])[:spare]
        .reshape(EXPERTS, 1, CAP, MODEL_WIDTH)
    )
    arrived = lax.all_to_all(buffer, "head", split_axis=0, concat_axis=1, tiled=True)
    expert_rows = arrived.reshape(loc_experts, head_number * CAP, MODEL_WIDTH)
    gate_up = jnp.einsum("erd,edf->erf", expert_rows, expert_up, preferred_element_type=f32)
    gate_part = gate_up[..., :FF]
    up_part = gate_up[..., FF:]
    activated = (jax.nn.silu(gate_part) * up_part).astype(bf16)
    expert_out = (
        jnp.einsum("erf,efd->erd", activated, expert_down, preferred_element_type=f32)
        .astype(bf16)
        .reshape(loc_experts, head_number, CAP, MODEL_WIDTH)
    )
    returned = lax.all_to_all(expert_out, "head", split_axis=1, concat_axis=0, tiled=True).reshape(
        spare, MODEL_WIDTH
    )
    returned = jnp.concatenate([returned, jnp.zeros((1, MODEL_WIDTH), bf16)], axis=0)
    picked = returned[target].astype(f32).reshape(tokens_present, top, MODEL_WIDTH)
    weights_pair = gates * kept.reshape(tokens_present, top).astype(f32)
    moe = jnp.sum(picked * weights_pair[..., None], axis=1)
    mixed_out = (middle + moe).astype(bf16).reshape(sequence_batch, token_rows, MODEL_WIDTH)
    grad_out = cotangent.reshape(tokens_present, MODEL_WIDTH).astype(f32)
    grad_gate = jnp.sum(picked * grad_out[:, None, :], axis=2) * kept.reshape(
        tokens_present, top
    ).astype(f32)
    grad_chosen = gates * (grad_gate - jnp.sum(gates * grad_gate, axis=1, keepdims=True))
    grad_logits = jnp.sum(jnp.where(hot, grad_chosen[:, :, None], 0.0), axis=1)
    grad_router = jnp.dot(second_input.astype(f32).T, grad_logits, precision=HIGH_PRECISION)
    grad_second = jnp.dot(grad_logits, dense_router.astype(f32).T, precision=HIGH_PRECISION)
    grad_pair = (
        (grad_out[:, None, :] * weights_pair[..., None]).reshape(pairs, MODEL_WIDTH).astype(bf16)
    )
    grad_slots = (
        jnp.zeros((spare + 1, MODEL_WIDTH), bf16)
        .at[target]
        .set(grad_pair)[:spare]
        .reshape(EXPERTS, 1, CAP, MODEL_WIDTH)
    )
    grad_arrived = lax.all_to_all(
        grad_slots, "head", split_axis=0, concat_axis=1, tiled=True
    ).reshape(loc_experts, head_number * CAP, MODEL_WIDTH)
    grad_act = jnp.einsum("erd,efd->erf", grad_arrived, expert_down, preferred_element_type=f32)
    sigma = jax.nn.sigmoid(gate_part)
    grad_upper = grad_act * gate_part * sigma
    grad_gating = grad_act * up_part * sigma * (1.0 + gate_part * (1.0 - sigma))
    grad_gate_up = jnp.concatenate([grad_gating, grad_upper], axis=-1).astype(bf16)
    down_grad = jnp.einsum("erf,erd->efd", activated, grad_arrived, preferred_element_type=f32)
    up_grad = jnp.einsum("erd,erf->edf", expert_rows, grad_gate_up, preferred_element_type=f32)
    grad_rows = (
        jnp.einsum("erf,edf->erd", grad_gate_up, expert_up, preferred_element_type=f32)
        .astype(bf16)
        .reshape(loc_experts, head_number, CAP, MODEL_WIDTH)
    )
    grad_back = lax.all_to_all(grad_rows, "head", split_axis=1, concat_axis=0, tiled=True).reshape(
        spare, MODEL_WIDTH
    )
    grad_back = jnp.concatenate([grad_back, jnp.zeros((1, MODEL_WIDTH), bf16)], axis=0)
    grad_second = grad_second + jnp.sum(
        grad_back[target].astype(f32).reshape(tokens_present, top, MODEL_WIDTH), axis=1
    )
    up_share, down_share = (
        lax.psum_scatter(
            up_grad.astype(jnp.bfloat16), "seq", scatter_dimension=1, tiled=True
        ).astype(jnp.float32),
        lax.psum_scatter(
            down_grad.astype(jnp.bfloat16), "seq", scatter_dimension=1, tiled=True
        ).astype(jnp.float32),
    )
    grad_gain_ffn = jnp.sum(grad_second * normed_two, axis=0)
    scaled_two = grad_second * gain_ffn_f
    grad_mid = grad_out + inverse_two * (
        scaled_two - normed_two * jnp.mean(scaled_two * normed_two, axis=1, keepdims=True)
    )
    grad_attn = grad_mid.astype(bf16)
    grad_dense_out = jnp.dot(mixed_heads.T, grad_attn, preferred_element_type=f32)
    grad_heads = (
        jnp.dot(grad_attn, dense_out.T, preferred_element_type=f32)
        .astype(bf16)
        .reshape(sequence_batch, token_rows, QUERY_HEADS * HEAD_WIDTH)
    )
    grad_local = lax.all_to_all(
        grad_heads, "head", split_axis=2, concat_axis=1, tiled=True
    ).reshape(sequence_batch, blk, key_value_location, query_group, HEAD_WIDTH)
    delta = jnp.sum(grad_local.transpose(0, 2, 3, 1, 4).astype(f32) * attended, axis=-1)

    def backward_block(state, piece, start, offset, token_count):
        grad_q, grad_store = state
        keys, values = key_view(piece, offset, token_count)
        scores = (
            jnp.einsum("sqhgd,skhd->shgqk", query_rows, keys, preferred_element_type=f32) * scale
        )
        mask = key_mask(offset, token_count)
        probs = jnp.where(mask, jnp.exp(scores - lse[..., None]), 0.0)
        grad_probs = jnp.einsum("sqhgd,skhd->shgqk", grad_local, values, preferred_element_type=f32)
        grad_scores = (probs * (grad_probs - delta[..., None])).astype(bf16)
        grad_q = (
            grad_q
            + jnp.einsum("shgqk,skhd->sqhgd", grad_scores, keys, preferred_element_type=f32) * scale
        )
        grad_k = (
            jnp.einsum("shgqk,sqhgd->skhd", grad_scores, query_rows, preferred_element_type=f32)
            * scale
        )
        grad_v = jnp.einsum(
            "shgqk,sqhgd->skhd", probs.astype(bf16), grad_local, preferred_element_type=f32
        )
        block_width = jnp.stack([grad_k, grad_v], axis=3).reshape(
            sequence_batch, token_count, key_value_location * 2 * HEAD_WIDTH
        )
        grad_store = lax.dynamic_update_slice_in_dim(grad_store, block_width, offset, 1)
        return (grad_q, grad_store)

    back_zero = (
        jnp.zeros((sequence_batch, blk, key_value_location, query_group, HEAD_WIDTH), f32),
        jnp.zeros((sequence_batch, length, key_value_location * 2 * HEAD_WIDTH), f32),
    )
    grad_q, grad_store = sweep(
        backward_block,
        back_zero,
        lax.all_gather(keys_values, "seq", axis=1, tiled=True),
        jnp.int32(0),
    )
    grad_kv = (
        lax.psum_scatter(grad_store.astype(jnp.bfloat16), "seq", scatter_dimension=1, tiled=True)
        .astype(jnp.float32)
        .reshape(sequence_batch, blk, key_value_location, 2, HEAD_WIDTH)
    )
    grad_pack = jnp.concatenate([grad_q.astype(bf16), grad_kv.astype(bf16)], axis=3).reshape(
        sequence_batch, blk, key_value_location * (query_group + 2) * HEAD_WIDTH
    )
    grad_proj = (
        lax.all_to_all(grad_pack, "head", split_axis=1, concat_axis=2, tiled=True)
        .reshape(sequence_batch, token_rows, KEY_VALUE_HEADS, query_group + 2, HEAD_WIDTH)
        .astype(f32)
    )
    unturned = rotate(grad_proj[:, :, :, : query_group + 1], cosine, -sine)
    grad_qkv = (
        jnp.concatenate([unturned, grad_proj[:, :, :, query_group + 1 :]], axis=3)
        .reshape(tokens_present, KEY_VALUE_HEADS * (query_group + 2) * HEAD_WIDTH)
        .astype(bf16)
    )
    grad_dense_qkv = jnp.dot(first_input.T, grad_qkv, preferred_element_type=f32)
    grad_first = jnp.dot(grad_qkv, dense_qkv.T, preferred_element_type=f32)
    grad_gain_attn = jnp.sum(grad_first * normed_one, axis=0)
    scaled_one = grad_first * gain_attn.astype(f32)
    grad_input = grad_mid + inverse_one * (
        scaled_one - normed_one * jnp.mean(scaled_one * normed_one, axis=1, keepdims=True)
    )
    qkv_share, out_share, router_share, attn_gain_share, ffn_gain_share = (
        lax.psum_scatter(grad_dense_qkv, ("seq", "head"), scatter_dimension=0, tiled=True),
        lax.psum_scatter(grad_dense_out, ("seq", "head"), scatter_dimension=0, tiled=True),
        lax.psum_scatter(grad_router, ("seq", "head"), scatter_dimension=0, tiled=True),
        lax.psum_scatter(grad_gain_attn, ("seq", "head"), scatter_dimension=0, tiled=True),
        lax.psum_scatter(grad_gain_ffn, ("seq", "head"), scatter_dimension=0, tiled=True),
    )
    return (
        mixed_out,
        grad_input.reshape(sequence_batch, token_rows, MODEL_WIDTH),
        qkv_share,
        out_share,
        router_share,
        attn_gain_share,
        ffn_gain_share,
        up_share,
        down_share,
    )


def solution(mesh):
    placed = (
        P(None, ("seq", "head"), None),
        P(),
        P(None, ("seq", "head"), None),
        P(None, ("seq", "head"), None),
        P(("seq", "head"), None),
        P(("seq", "head"), None),
        P(("seq", "head"), None),
        P(("seq", "head")),
        P(("seq", "head")),
        P("head", "seq", None),
        P("head", "seq", None),
        P(None, ("seq", "head"), None),
    )
    return jax.shard_map(
        per_device,
        mesh=mesh,
        in_specs=placed,
        out_specs=(
            P(None, ("seq", "head"), None),
            P(None, ("seq", "head"), None),
            P(("seq", "head"), None),
            P(("seq", "head"), None),
            P(("seq", "head"), None),
            P(("seq", "head")),
            P(("seq", "head")),
            P("head", "seq", None),
            P("head", "seq", None),
        ),
        check_vma=False,
    )
```

profile of v0, /device:TPU:0, one launch (start us, length us, event | category | flops | bytes accessed | tf_op | source)
XLA Modules:
  0.0 1638.9 jit_solution(926769261906299153)
XLA Ops:
  9.7 42.5 %all-reduce.7 = (bf16[1536]{0:T(1024)(128)(2,1)S(1)}, bf16[1536]{0:T(1024)(128)(2,1)S(1)}) all-reduce(bf16[1536]{0:T(1024)(128)(2,1)S(1)} %dynamic-update-slice, bf16[1536]{0:T(1024)(128)(2,1)S(1)} %dynamic-update-slice.1), channel_id=1, replica_groups=mesh['seq'=8,'head'=4] {'seq','head'}, use_global_device_ids=true, to_apply=%add.2 | all-reduce | flops 3072 | bytes 12288
  55.3 33.8 %all-gather.7.cloned.1.call-done = bf16[1536,2560]{1,0:T(8,128)(2,1)} async-done(((bf16[48,2560]{1,0:T(8,128)(2,1)}), bf16[1536,2560]{1,0:T(8,128)(2,1)}) %all-gather.7.cloned.1.call-update) | async-done | bytes 7864336 | tf_op jit(solution)/shard_map/all_gather | solution.py:65
  89.1 10.6 copy.179
  99.7 5.1 fusion.47
  105.6 11.2 copy.240
  117.8 20.7 %all_to_all.114 = bf16[4,2,40960]{2,1,0:T(2,128)(2,1)S(1)} all-to-all(bf16[4,2,40960]{2,1,0:T(2,128)(2,1)S(1)} %reshape.717), channel_id=1, replica_groups=mesh['seq'=8,'head'=4] {'head'}, dimensions={0} | all-to-all | bytes 1310720 | tf_op jit(solution)/shard_map/all_to_all | solution.py:92
  153.5 11.3 reduce-window.6
  168.6 7.1 while.38
  168.6 6.8 conditional.6
  186.3 9.5 all-to-all-done.1
  196.3 44.6 %all-gather.11.cloned.1.call-done = bf16[1536,1536]{1,0:T(8,128)(2,1)} async-done(((bf16[48,1536]{1,0:T(8,128)(2,1)}), bf16[1536,1536]{1,0:T(8,128)(2,1)}) %all-gather.11.cloned.1.call-update) | async-done | bytes 4718608 | tf_op jit(solution)/shard_map/all_gather | solution.py:66
  246.0 19.1 %scatter_custom_fusion.1 = bf16[1001,1536]{1,0:T(8,128)(2,1)S(1)} fusion(s32[1024]{0:T(1024)S(1)} %bitcast.293, bf16[128,1536]{1,0:T(8,128)(2,1)} %multiply_convert_fusion.3, s32[1024]{0:T(1024)S(1)} %broadcast_clamp_fusion.1, bf16[]{:T(256)} %constant.160.clone.1), kind=kCustom, calls=%fused_computation.73 | custom fusion | bytes 3075584 | tf_op jit(solution)/shard_map/scatter | solution.py:204
  266.9 5.5 reshape.607
  277.4 149.3 %all-gather = bf16[32,48,40]{1,2,0:T(8,128)(2,1)S(1)} all-gather(bf16[1,48,40]{1,2,0:T(8,128)(2,1)S(1)} %bitcast.300), channel_id=1, replica_groups=mesh['seq'=8,'head'=4] {'seq','head'}, dimensions={0}, use_global_device_ids=true | all-gather | bytes 126720 | tf_op jit(solution)/shard_map/all_gather | solution.py:67
  429.8 7.1 scatter_custom_fusion.2
  438.7 5.5 reshape.612
  453.5 5.7 reshape.608
  459.2 72.6 %all-to-all-done.4 = bf16[40,1,25,1536]{3,2,1,0:T(8,128)(2,1)} async-done(((bf16[40,1,25,1536]{3,2,1,0:T(8,128)(2,1)}), bf16[40,1,25,1536]{3,2,1,0:T(8,128)(2,1)}, u32[]{:S(2)}, u32[]{:S(2)}) %all-to-all-start.4) | async-done | bytes 3072032 | tf_op jit(solution)/shard_map/all_to_all | solution.py:243
  536.3 5.6 reshape.613
  542.0 17.6 %fusion.65 = f32[10,100,1024]{2,1,0:T(8,128)} fusion(bf16[10,100,1536]{2,1,0:T(8,128)(2,1)} %reshape.608, bf16[10,1536,1024]{2,1,0:T(8,128)(2,1)} %all-gather.13.cloned.1.call-done), kind=kOutput, calls=%fused_computation.169 | convolution fusion | flops 3145728000 | bytes 38625280 | tf_op jit(solution)/shard_map/erd,edf->erf/dot_general | solution.py:209
  559.6 11.1 multiply_convert_fusion.1
  570.7 17.2 %convolution_convert_fusion.2 = bf16[10,100,1536]{2,1,0:T(8,128)(2,1)} fusion(bf16[10,1536,1024]{2,1,0:T(8,128)(2,1)} %all-gather.13.cloned.1.call-done, bf16[10,100,512]{2,1,0:T(8,128)(2,1)} %get-tuple-element.746, bf16[10,100,512]{2,1,0:T(8,128)(2,1)S(1)} %get-tuple-element.745), kind=kOutput, calls=%fused_computation.70 | convolution fusion | flops 3151360000 | bytes 36577280 | tf_op jit(solution)/shard_map/erf,edf->erd/dot_general | solution.py:254
  587.9 5.5 reshape.614
  597.9 5.2 all-to-all-start.5
  603.1 9.7 convolution_convert_fusion.3
  612.8 5.5 reshape.609
  622.8 67.3 %all-to-all-done.5 = bf16[10,4,25,1536]{3,2,0,1:T(8,128)(2,1)} async-done(((bf16[10,4,25,1536]{3,2,0,1:T(8,128)(2,1)}), bf16[10,4,25,1536]{3,2,0,1:T(8,128)(2,1)}, u32[]{:S(2)}, u32[]{:S(2)}) %all-to-all-start.5) | async-done | bytes 3072032 | tf_op jit(solution)/shard_map/all_to_all | solution.py:258
  696.5 5.7 reshape.615
  704.3 5.6 gather_fusion.3
  714.7 67.4 %all-to-all-done.3 = bf16[10,4,25,1536]{3,2,0,1:T(8,128)(2,1)} async-done(((bf16[10,4,25,1536]{3,2,0,1:T(8,128)(2,1)}), bf16[10,4,25,1536]{3,2,0,1:T(8,128)(2,1)}, u32[]{:S(2)}, u32[]{:S(2)}) %all-to-all-start.3) | async-done | bytes 3072032 | tf_op jit(solution)/shard_map/all_to_all | solution.py:218
  782.0 5.7 reshape.610
  789.8 5.6 gather_fusion.2
  812.4 10.3 all-to-all-done.6
  826.1 9.5 while.39
  826.2 9.5 conditional.7
  837.3 9.6 convolution_convert_fusion.1
  848.1 15.4 convolution_convert_fusion
  869.7 34.7 %reduce-scatter.9.cloned.1.call-done = bf16[2,256,256]{1,2,0:T(8,128)(2,1)} async-done(((bf16[2,2048,256]{1,2,0:T(8,128)(2,1)}), bf16[2,256,256]{1,2,0:T(8,128)(2,1)}) %reduce-scatter.9.cloned.1.call-update) | async-done | bytes 262160 | tf_op jit(solution)/shard_map/reduce_scatter | solution.py:328
  906.6 21.7 %all_to_all.115 = bf16[2,256,640]{2,0,1:T(2,128)(2,1)S(1)} all-to-all(bf16[2,256,640]{2,0,1:T(2,128)(2,1)S(1)} %copy.207), channel_id=1, replica_groups=mesh['seq'=8,'head'=4] {'head'}, dimensions={1} | all-to-all | bytes 1310720 | tf_op jit(solution)/shard_map/all_to_all | solution.py:336
  935.9 7.6 fusion.67
  944.3 62.1 %reduce-scatter.19.cloned.1.call-done = f32[48,40]{1,0:T(8,128)} async-done(((f32[1536,40]{1,0:T(8,128)}), f32[48,40]{1,0:T(8,128)}) %reduce-scatter.19.cloned.1.call-update) | async-done | bytes 7696
  1007.8 6.0 multiply_reduce_fusion.1
  1013.9 40.5 %all-reduce.6 = (f32[1536]{0:T(1024)S(1)}, f32[1536]{0:T(1024)S(1)}) all-reduce(f32[1536]{0:T(1024)S(1)} %get-tuple-element.689, f32[1536]{0:T(1024)S(1)} %copy-done.33), channel_id=6, replica_groups=mesh['seq'=8,'head'=4] {'seq','head'}, use_global_device_ids=true, to_apply=%region_34.35.clone | all-reduce | flops 3072 | bytes 24576
  1056.7 62.5 %reduce-scatter.17.cloned.1.call-done = bf16[10,64,1536]{2,1,0:T(8,128)(2,1)} async-done(((bf16[10,512,1536]{2,1,0:T(8,128)(2,1)}), bf16[10,64,1536]{2,1,0:T(8,128)(2,1)}) %reduce-scatter.17.cloned.1.call-update) | async-done | bytes 1966096 | tf_op jit(solution)/shard_map/reduce_scatter | solution.py:269
  1123.2 189.9 %reduce-scatter.15.cloned.1.call-done = bf16[10,192,1024]{2,1,0:T(8,128)(2,1)} async-done(((bf16[10,1536,1024]{2,1,0:T(8,128)(2,1)}), bf16[10,192,1024]{2,1,0:T(8,128)(2,1)}) %reduce-scatter.15.cloned.1.call-update) | async-done | bytes 3932176 | tf_op jit(solution)/shard_map/reduce_scatter | solution.py:266
  1313.1 6.3 convert_element_type.231
  1319.4 136.6 %reduce-scatter.13.cloned.1.call-done = f32[48,1536]{1,0:T(8,128)} async-done(((f32[1536,1536]{1,0:T(8,128)}), f32[48,1536]{1,0:T(8,128)}) %reduce-scatter.13.cloned.1.call-update) | async-done | bytes 294928 | tf_op jit(solution)/shard_map/reduce_scatter | solution.py:355
  1456.0 176.2 %reduce-scatter.11.cloned.1.call-done = f32[48,2560]{1,0:T(8,128)} async-done(((f32[1536,2560]{1,0:T(8,128)}), f32[48,2560]{1,0:T(8,128)}) %reduce-scatter.11.cloned.1.call-update) | async-done | bytes 491536 | tf_op jit(solution)/shard_map/reduce_scatter | solution.py:354
  (298 shorter events, 155.4 us)
Async XLA Ops:
  7.2 81.9 %all-gather.7.cloned.1.call-start = ((), (), s32[]{:S(2)}) async-start(), calls=%async_computation.14 | async-start | bytes 8110080 | tf_op jit(solution)/shard_map/all_gather | solution.py:65
  7.9 160.6 %all-gather.9.cloned.1.call-start = ((), (), s32[]{:S(2)}) async-start(), calls=%async_computation.15 | async-start | bytes 2359296 | tf_op jit(solution)/shard_map/all_gather | solution.py:164
  52.2 47.5 %copy-start.27 = (f32[1536]{0:T(1024)}, f32[1536]{0:T(1024)S(1)}, u32[]{:S(2)}) copy-start(f32[1536]{0:T(1024)S(1)} %convert_element_type.194) | copy-start | bytes 18436
  54.2 50.7 %copy-start.25 = (f32[64,32]{0,1:T(8,128)}, f32[64,32]{0,1:T(8,128)S(1)}, u32[]{:S(2)}) copy-start(f32[64,32]{0,1:T(8,128)S(1)} %get-tuple-element.756) | copy-start | bytes 24580
  55.3 44.4 %copy-start.15 = (bf16[2,64,1536]{2,1,0:T(8,128)(2,1)}, bf16[2,64,1536]{2,1,0:T(8,128)(2,1)S(1)}, u32[]{:S(2)}) copy-start(bf16[2,64,1536]{2,1,0:T(8,128)(2,1)S(1)} %multiply_convert_fusion.4) | copy-start | bytes 1179652
  142.0 99.0 %all-gather.11.cloned.1.call-start = ((), (), s32[]{:S(2)}) async-start(), calls=%async_computation.16 | async-start | bytes 4866048 | tf_op jit(solution)/shard_map/all_gather | solution.py:66
  142.7 399.3 %all-gather.13.cloned.1.call-start = ((), (), s32[]{:S(2)}) async-start(), calls=%async_computation.17 | async-start | bytes 35389440 | tf_op jit(solution)/shard_map/all_gather | solution.py:72
  143.3 416.3 %all-gather.15.cloned.1.call-start = ((), (), s32[]{:S(2)}) async-start(), calls=%async_computation.18 | async-start | bytes 17694720 | tf_op jit(solution)/shard_map/all_gather | solution.py:73
  175.7 5.8 copy-start.4
  175.7 10.6 copy-start.21
  176.9 19.0 %all-to-all-start.1 = ((bf16[2,256,384]{2,0,1:T(2,128)(2,1)}), bf16[2,256,384]{2,0,1:T(2,128)(2,1)S(1)}, u32[]{:S(2)}, u32[]{:S(2)}) async-start(bf16[2,256,384]{2,0,1:T(2,128)(2,1)} %copy.183), calls=%async_computation.1 | async-start | bytes 786432 | tf_op jit(solution)/shard_map/all_to_all | solution.py:175
  181.7 59.2 %copy-start.2 = (bf16[2,64,1536]{2,1,0:T(8,128)(2,1)S(1)}, bf16[2,64,1536]{2,1,0:T(8,128)(2,1)}, u32[]{:S(2)}) copy-start(bf16[2,64,1536]{2,1,0:T(8,128)(2,1)} %param.20) | copy-start | bytes 1179652
  186.3 59.6 %copy-start.38 = (s32[1024,1]{0,1:T(1,128)}, s32[1024,1]{0,1:T(1,128)S(1)}, u32[]{:S(2)}) copy-start(s32[1024,1]{0,1:T(1,128)S(1)} %compare_select_fusion.1) | copy-start | bytes 12292
  196.3 47.9 %copy-start.8 = (bf16[16,8,4,384]{3,1,2,0:T(8,128)(2,1)}, bf16[16,8,4,384]{3,1,2,0:T(8,128)(2,1)S(1)}, u32[]{:S(2)}) copy-start(bf16[16,8,4,384]{3,1,2,0:T(8,128)(2,1)S(1)} %copy.232) | copy-start | bytes 1179652
  244.2 22.7 %copy-start.47 = (f32[128]{0:T(128)}, f32[128]{0:T(128)S(1)}, u32[]{:S(2)}) copy-start(f32[128]{0:T(128)S(1)} %add_rsqrt_fusion.1) | copy-start | bytes 1540
  272.4 5.0 copy-start.30
  272.4 5.0 copy-start.45
  272.4 154.8 %copy-start.17 = (bf16[2,64,1536]{2,1,0:T(8,128)(2,1)S(1)}, bf16[2,64,1536]{2,1,0:T(8,128)(2,1)}, u32[]{:S(2)}) copy-start(bf16[2,64,1536]{2,1,0:T(8,128)(2,1)} %param.31) | copy-start | bytes 1179652
  272.4 155.8 %copy-start.12 = (bf16[128,1536]{1,0:T(8,128)(2,1)S(1)}, bf16[128,1536]{1,0:T(8,128)(2,1)}, u32[]{:S(2)}) copy-start(bf16[128,1536]{1,0:T(8,128)(2,1)} %multiply_convert_fusion.3) | copy-start | bytes 1179652
  272.4 171.8 %all-to-all-start.2 = ((bf16[40,1,25,1536]{3,2,1,0:T(8,128)(2,1)}), bf16[40,1,25,1536]{3,2,1,0:T(8,128)(2,1)}, u32[]{:S(2)}, u32[]{:S(2)}) async-start(bf16[40,1,25,1536]{3,2,1,0:T(8,128)(2,1)} %bitcast.263), calls=%async_computation.2 | async-start | bytes 7864320 | tf_op jit(solution)/shard_map/all_to_all | solution.py:207
  428.5 10.3 copy-start.34
  444.2 87.6 %all-to-all-start.4 = ((bf16[40,1,25,1536]{3,2,1,0:T(8,128)(2,1)}), bf16[40,1,25,1536]{3,2,1,0:T(8,128)(2,1)}, u32[]{:S(2)}, u32[]{:S(2)}) async-start(bf16[40,1,25,1536]{3,2,1,0:T(8,128)(2,1)} %bitcast.264), calls=%async_computation.4 | async-start | bytes 7864320 | tf_op jit(solution)/shard_map/all_to_all | solution.py:243
  570.7 17.2 %copy-start.10 = (bf16[10,100,512]{2,1,0:T(8,128)(2,1)}, bf16[10,100,512]{2,1,0:T(8,128)(2,1)S(1)}, u32[]{:S(2)}) copy-start(bf16[10,100,512]{2,1,0:T(8,128)(2,1)S(1)} %get-tuple-element.745) | copy-start | bytes 3072004
  570.7 32.3 %copy-start.6 = (bf16[10,100,512]{2,1,0:T(8,128)(2,1)}, bf16[10,100,512]{2,1,0:T(8,128)(2,1)S(1)}, u32[]{:S(2)}) copy-start(bf16[10,100,512]{2,1,0:T(8,128)(2,1)S(1)} %get-tuple-element.747) | copy-start | bytes 3072004
  597.9 92.3 %all-to-all-start.5 = ((bf16[10,4,25,1536]{3,2,0,1:T(8,128)(2,1)}), bf16[10,4,25,1536]{3,2,0,1:T(8,128)(2,1)}, u32[]{:S(2)}, u32[]{:S(2)}) async-start(bf16[10,4,25,1536]{3,2,0,1:T(8,128)(2,1)} %copy.203), calls=%async_computation.5 | async-start | bytes 7864320 | tf_op jit(solution)/shard_map/all_to_all | solution.py:258
  622.8 72.2 %copy-start.39 = (s32[1024,1]{0,1:T(1,128)S(1)}, s32[1024,1]{0,1:T(1,128)}, u32[]{:S(2)}) copy-start(s32[1024,1]{0,1:T(1,128)} %copy-done.38) | copy-start | bytes 12292
  622.8 72.8 %copy-start.51 = (pred[1024]{0:T(1024)(128)(4,1)S(1)}, pred[1024]{0:T(1024)(128)(4,1)}, u32[]{:S(2)}) copy-start(pred[1024]{0:T(1024)(128)(4,1)} %get-tuple-element.742) | copy-start | bytes 3076
  622.8 72.9 %copy-start.35 = (f32[128]{0:T(128)S(1)}, f32[128]{0:T(128)}, u32[]{:S(2)}) copy-start(f32[128]{0:T(128)} %copy-done.34) | copy-start | bytes 1540
  622.8 72.9 %copy-start.43 = (f32[128]{0:T(128)S(1)}, f32[128]{0:T(128)}, u32[]{:S(2)}) copy-start(f32[128]{0:T(128)} %copy-done.42) | copy-start | bytes 1540
  690.1 91.9 %all-to-all-start.3 = ((bf16[10,4,25,1536]{3,2,0,1:T(8,128)(2,1)}), bf16[10,4,25,1536]{3,2,0,1:T(8,128)(2,1)}, u32[]{:S(2)}, u32[]{:S(2)}) async-start(bf16[10,4,25,1536]{3,2,0,1:T(8,128)(2,1)} %copy.193), calls=%async_computation.3 | async-start | bytes 7864320 | tf_op jit(solution)/shard_map/all_to_all | solution.py:218
  795.3 4.4 copy-start.1
  795.4 4.4 copy-start.14
  795.4 4.4 copy-start.20
  795.4 4.4 copy-start.48
  795.4 5.7 copy-start.18
  806.8 17.5 %copy-start.5 = (f32[2,2,3,256,64]{3,4,2,1,0:T(8,128)S(1)}, f32[2,2,3,256,64]{3,4,2,1,0:T(8,128)}, u32[]{:S(2)}) copy-start(f32[2,2,3,256,64]{3,4,2,1,0:T(8,128)} %copy-done.4) | copy-start | bytes 2359300
  808.1 14.6 all-to-all-start.6
  811.5 92.9 %reduce-scatter.9.cloned.1.call-start = ((), (), s32[]{:S(2)}) async-start(), calls=%async_computation.19 | async-start | bytes 2359296 | tf_op jit(solution)/shard_map/reduce_scatter | solution.py:328
  826.1 9.6 copy-start.13
  826.1 9.6 copy-start.24
  835.7 170.7 %reduce-scatter.19.cloned.1.call-start = ((), (), s32[]{:S(2)}) async-start(), calls=%async_computation.24 | async-start | bytes 811008
  837.2 282.0 %reduce-scatter.17.cloned.1.call-start = ((), (), s32[]{:S(2)}) async-start(), calls=%async_computation.23 | async-start | bytes 17694720 | tf_op jit(solution)/shard_map/reduce_scatter | solution.py:269
  846.9 466.1 %reduce-scatter.15.cloned.1.call-start = ((), (), s32[]{:S(2)}) async-start(), calls=%async_computation.22 | async-start | bytes 35389440 | tf_op jit(solution)/shard_map/reduce_scatter | solution.py:266
  863.6 592.4 %reduce-scatter.13.cloned.1.call-start = ((), (), s32[]{:S(2)}) async-start(), calls=%async_computation.21 | async-start | bytes 9732096 | tf_op jit(solution)/shard_map/reduce_scatter | solution.py:355
  869.6 762.6 %reduce-scatter.11.cloned.1.call-start = ((), (), s32[]{:S(2)}) async-start(), calls=%async_computation.20 | async-start | bytes 16220160 | tf_op jit(solution)/shard_map/reduce_scatter | solution.py:354
  943.5 64.3 %copy-start.3 = (bf16[2,64,1536]{2,1,0:T(8,128)(2,1)S(1)}, bf16[2,64,1536]{2,1,0:T(8,128)(2,1)}, u32[]{:S(2)}) copy-start(bf16[2,64,1536]{2,1,0:T(8,128)(2,1)} %param.20) | copy-start | bytes 1179652
  943.5 64.3 %copy-start.28 = (f32[1536]{0:T(1024)S(1)}, f32[1536]{0:T(1024)}, u32[]{:S(2)}) copy-start(f32[1536]{0:T(1024)} %copy-done.27) | copy-start | bytes 18436
  1007.8 6.1 copy-start.33
  (21 other events, 45.1 us)
Sparse Core Ops, SparseCore 0:
  10.8 78.2 all-gather.6
  142.1 26.4 all-gather.8
  171.3 69.5 all-gather.10
  242.7 151.5 all-gather.12
  396.0 85.7 all-gather.14
  835.8 68.5 reduce-scatter.8
  910.9 95.4 reduce-scatter.18
  1010.3 108.7 reduce-scatter.16
  1123.2 189.7 reduce-scatter.14
  1320.4 135.5 reduce-scatter.12
  1462.6 169.5 reduce-scatter.10
where the time goes:
time: 1650 us; the launch traced here: 1640 us
  waiting for transfers between devices  973 us (59%)
  blocking collectives  275 us (17%)
  local copies, waits for them, and re-layouts  170 us (10%)
  matrix products  124 us (8%)
  other arithmetic  53.8 us (3%)
  starting transfers between devices  28.7 us (2%)
    reduce_scatter x1, waiting for transfers between devices, per_device(): lax.psum_scatter(up_grad.astype(jnp.bfloat16), 'seq', scatter_dimension=1...  190 us
    reduce_scatter x1, waiting for transfers between devices, per_device(): lax.psum_scatter(grad_dense_qkv, ('seq', 'head'), scatter_dimension=0, ti...  176 us
    all_gather x1, blocking collectives, per_device(): lax.all_gather(router_weight, ('seq', 'head'), axis=0, tiled=True)  149 us
    reduce_scatter x1, waiting for transfers between devices, per_device(): lax.psum_scatter(grad_dense_out, ('seq', 'head'), scatter_dimension=0, ti...  137 us
    unnamed x2, blocking collectives  83 us
    all_to_all x1, waiting for transfers between devices, per_device(): lax.all_to_all(grad_slots, 'head', split_axis=0, concat_axis=1, tiled=True)  72.6 us
    all_to_all x1, waiting for transfers between devices, per_device(): lax.all_to_all(expert_out, 'head', split_axis=1, concat_axis=0, tiled=True)  67.4 us
    all_to_all x1, waiting for transfers between devices, per_device(): lax.all_to_all(grad_rows, 'head', split_axis=1, concat_axis=0, tiled=True)  67.3 us
  transfers between devices with their start and end apart: 17, of which 14 were waited for; matrix products, arithmetic and copies ran while one was open for 14% of the time, Pallas kernels for 0%

commit v1 on v0

v1 whole, which is shorter than its diff:
```python
import functools

import jax
import jax.numpy as jnp
from jax import lax
from jax.experimental import pallas as pl
from jax.experimental.pallas import tpu as pltpu
from jax.sharding import Mesh, PartitionSpec as P

MODEL_WIDTH = 1536
QUERY_HEADS = 24
KEY_VALUE_HEADS = 8
HEAD_WIDTH = 64
EXPERTS = 40
FF = 512
CAP = 25
LANES = 128
LOW = 64

epsilon = 1e-06
negative = -1e30
theta = 10000.0
HIGH_PRECISION = lax.Precision.HIGHEST
MESH = pl.DeviceIdType.MESH
f32 = jnp.float32
bf16 = jnp.bfloat16
ANY = pl.BlockSpec(memory_space=pl.ANY)
WHOLE = pl.BlockSpec(memory_space=pltpu.VMEM)
DMA = pltpu.SemaphoreType.DMA


def rope_tables(token_positions, head_size):
    half = head_size // 2
    freq = theta ** (-jnp.arange(half, dtype=jnp.float32) / half)
    angle = token_positions.astype(jnp.float32)[:, None] * freq[None, :]
    return (jnp.cos(angle)[None, :, None, None, :], jnp.sin(angle)[None, :, None, None, :])


def rotate(value, cosine, sine):
    half = value.shape[-1] // 2
    first = value[..., :half]
    second = value[..., half:]
    return jnp.concatenate(
        [first * cosine - second * sine, second * cosine + first * sine], axis=-1
    )


def digits(count):
    number = count.bit_length() - 1
    assert 1 << number == count
    return number


def flip(index, mask):
    out = index
    bit = 0
    while (1 << bit) <= mask:
        if (mask >> bit) & 1:
            out = out + (1 - 2 * ((index // (1 << bit)) % 2)) * (1 << bit)
        bit += 1
    return out


def subsets(bits):
    out = [0]
    for bit in bits:
        out = out + [mask | (1 << bit) for mask in out]
    return out


def near(count):
    return sorted(range(1, count), key=lambda step: min(step, count - step))


def meet(peers):
    sem = pltpu.get_barrier_semaphore()
    for peer in peers:
        pl.semaphore_signal(sem, inc=1, device_id=peer, device_id_type=MESH)
    pl.semaphore_wait(sem, len(peers))


class Cube:
    def __init__(self, chips, with_core):
        self.chips = chips
        self.chip_digits = digits(chips)
        self.number = self.chip_digits + int(with_core)
        self.with_core = with_core
        up = tuple(range(self.chip_digits))
        core = (self.chip_digits,) if with_core else ()
        self.gather_orders = (up + core, up[::-1] + core)
        self.scatter_orders = (core + up, core + up[::-1])

    def place(self, mask):
        chip = flip(lax.axis_index("chip"), mask & (self.chips - 1))
        if not self.with_core:
            return (chip,)
        return (chip, flip(lax.axis_index("core"), mask >> self.chip_digits))

    def peer(self, digit):
        if digit < self.chip_digits:
            return {"chip": flip(lax.axis_index("chip"), 1 << digit)}
        return {"core": flip(lax.axis_index("core"), 1)}


def gather_kernel(cube, heads, in_ref, out_ref, local, line_send, line_recv, send, recv):
    hz = lax.axis_index("head")
    rows = in_ref.shape[0]
    half = rows // 2
    others = near(heads) if heads > 1 else []
    meet(
        [cube.peer(digit) for digit in range(cube.number)]
        + [{"head": (hz + d) % heads} for d in others]
    )

    def at(mask, d):
        index = cube.place(mask)
        return index + ((hz + heads - d) % heads,) if heads > 1 else index

    own = pltpu.make_async_copy(in_ref, out_ref.at[at(0, 0)], local)
    own.start()
    line = {}
    for d in others:
        line[d] = pltpu.make_async_remote_copy(
            src_ref=in_ref,
            dst_ref=out_ref.at[at(0, 0)],
            send_sem=line_send.at[d - 1],
            recv_sem=line_recv.at[d - 1],
            device_id={"head": (hz + d) % heads},
            device_id_type=MESH,
        )
        line[d].start()
    copies = {}

    def forward(side, mask, d):
        order = cube.gather_orders[side]
        last = max([k for k in range(cube.number) if (mask >> order[k]) & 1], default=-1)
        for k in range(last + 1, cube.number):
            later = mask | (1 << order[k])
            part = pl.ds(side * half, half)
            place = out_ref.at[at(mask, d) + (part,)]
            copy = pltpu.make_async_remote_copy(
                src_ref=in_ref.at[part] if mask == 0 and d == 0 else place,
                dst_ref=place,
                send_sem=send.at[side, later, d],
                recv_sem=recv.at[side, later, d],
                device_id=cube.peer(order[k]),
                device_id_type=MESH,
            )
            copy.start()
            copies[(side, later, d)] = copy

    for side in range(2):
        forward(side, 0, 0)
    for d in others:
        line[d].wait_recv()
        for side in range(2):
            forward(side, 0, d)
    for mask in sorted(range(1, 1 << cube.number), key=lambda m: bin(m).count("1")):
        for d in [0] + others:
            for side in range(2):
                copies[(side, mask, d)].wait_recv()
                forward(side, mask, d)
    own.wait()
    for copy in list(line.values()) + list(copies.values()):
        copy.wait_send()


def gather(value, chips, heads, with_core, number):
    rows, columns = value.shape
    cube = Cube(chips, with_core)
    lead = (chips,) + ((2,) if with_core else ()) + ((heads,) if heads > 1 else ())
    steps = max(heads - 1, 1)
    return pl.pallas_call(
        functools.partial(gather_kernel, cube, heads),
        out_shape=jax.ShapeDtypeStruct(lead + (rows, columns), value.dtype),
        in_specs=[ANY],
        out_specs=ANY,
        scratch_shapes=[
            DMA,
            DMA((steps,)),
            DMA((steps,)),
            DMA((2, 1 << cube.number, heads)),
            DMA((2, 1 << cube.number, heads)),
        ],
        compiler_params=pltpu.CompilerParams(collective_id=number, has_side_effects=True),
        name="gather",
    )(value)


def scatter_kernel(cube, heads, in_ref, out_ref, *refs):
    count = cube.number
    arrived, parts = refs[:count], refs[count : 2 * count - 1]
    line_out, line_in, line_send, line_recv, send, recv = refs[2 * count - 1 :]
    hz = lax.axis_index("head")
    half = in_ref.shape[-2] // 2
    others = near(heads) if heads > 1 else []
    order_of_lines = others[::-1] + [0]
    meet(
        [cube.peer(digit) for digit in range(count)] + [{"head": (hz + d) % heads} for d in others]
    )
    copies = {}

    def slot(side, k, mask):
        return subsets(cube.scatter_orders[side][k + 1 :]).index(mask)

    def mine(side, mask, d):
        index = cube.place(mask)
        if heads > 1:
            index = index + ((hz + d) % heads,)
        return in_ref.at[index + (pl.ds(side * half, half),)]

    def pass_on(side, k, mask, d, source):
        where = slot(side, k, mask)
        copy = pltpu.make_async_remote_copy(
            src_ref=source,
            dst_ref=arrived[k].at[side, where, d],
            send_sem=send.at[side, k, where, d],
            recv_sem=recv.at[side, k, where, d],
            device_id=cube.peer(cube.scatter_orders[side][k]),
            device_id_type=MESH,
        )
        copy.start()
        copies[(side, k, mask, d)] = copy

    def total(side, steps, mask, d):
        value = mine(side, mask, d)[...].astype(f32)
        for j in range(steps):
            copies[(side, j, mask, d)].wait_recv()
            value = value + arrived[j][side, slot(side, j, mask), d].astype(f32)
        return value

    for k in range(count):
        for d in order_of_lines:
            for side in range(2):
                order = cube.scatter_orders[side]
                for mask in subsets(order[k + 1 :])[::-1]:
                    full = mask | (1 << order[k])
                    if k == 0:
                        source = mine(side, full, d)
                    else:
                        source = parts[k - 1].at[side, slot(side, k, mask), d]
                        source[...] = total(side, k, full, d).astype(bf16)
                    pass_on(side, k, mask, d, source)
    line = {}
    for d in order_of_lines:
        for side in range(2):
            value = total(side, count, 0, d)
            if d:
                line_out[d - 1, pl.ds(side * half, half)] = value.astype(bf16)
            else:
                out_ref[pl.ds(side * half, half)] = value
        if d:
            line[d] = pltpu.make_async_remote_copy(
                src_ref=line_out.at[d - 1],
                dst_ref=line_in.at[d - 1],
                send_sem=line_send.at[d - 1],
                recv_sem=line_recv.at[d - 1],
                device_id={"head": (hz + d) % heads},
                device_id_type=MESH,
            )
            line[d].start()
    for d in others:
        line[d].wait_recv()
        out_ref[...] += line_in[d - 1].astype(f32)
    for copy in list(line.values()) + list(copies.values()):
        copy.wait_send()


def scatter_sum(value, chips, heads, with_core, number):
    rows, columns = value.shape[-2:]
    cube = Cube(chips, with_core)
    half = rows // 2
    steps = max(heads - 1, 1)
    line_rows = rows if heads > 1 else 16
    slots = [(1 << cube.number) >> (k + 1) for k in range(cube.number)]
    if 2 * value.size + 4 * heads * half * columns * (sum(slots) + sum(slots[1:])) > 40 << 20:
        names = ("chip", "core") if with_core else ("chip",)
        names = names + (("head",) if heads > 1 else ())
        flat = value.reshape(-1, columns)
        return lax.psum_scatter(flat, names, scatter_dimension=0, tiled=True).astype(f32)
    return pl.pallas_call(
        functools.partial(scatter_kernel, cube, heads),
        out_shape=jax.ShapeDtypeStruct((rows, columns), f32),
        in_specs=[WHOLE],
        out_specs=WHOLE,
        scratch_shapes=[pltpu.VMEM((2, s, heads, half, columns), bf16) for s in slots]
        + [pltpu.VMEM((2, s, heads, half, columns), bf16) for s in slots[1:]]
        + [
            pltpu.VMEM((steps, line_rows, columns), bf16),
            pltpu.VMEM((steps, line_rows, columns), bf16),
            DMA((steps,)),
            DMA((steps,)),
            DMA((2, cube.number, slots[0], heads)),
            DMA((2, cube.number, slots[0], heads)),
        ],
        compiler_params=pltpu.CompilerParams(
            collective_id=number, has_side_effects=True, vmem_limit_bytes=56 << 20
        ),
        name="scatter_sum",
    )(value)


def line_kernel(heads, same, in_ref, out_ref, local, send, recv):
    hz = lax.axis_index("head")
    others = near(heads)[::-1]
    meet([{"head": (hz + d) % heads} for d in others])

    def source(place):
        return in_ref if same else in_ref.at[place]

    own = pltpu.make_async_copy(source(hz), out_ref.at[hz], local)
    own.start()
    copies = []
    for d in others:
        place = (hz + d) % heads
        copy = pltpu.make_async_remote_copy(
            src_ref=source(place),
            dst_ref=out_ref.at[hz],
            send_sem=send.at[d - 1],
            recv_sem=recv.at[d - 1],
            device_id={"head": place},
            device_id_type=MESH,
        )
        copy.start()
        copies.append(copy)
    own.wait()
    for copy in copies:
        copy.wait()


def line_exchange(value, heads, number, same=False):
    return pl.pallas_call(
        functools.partial(line_kernel, heads, same),
        out_shape=jax.ShapeDtypeStruct((heads,) + value.shape if same else value.shape, value.dtype),
        in_specs=[ANY],
        out_specs=ANY,
        scratch_shapes=[DMA, DMA((heads - 1,)), DMA((heads - 1,))],
        compiler_params=pltpu.CompilerParams(collective_id=number, has_side_effects=True),
        name="line_exchange",
    )(value)


NT = (((1,), (1,)), ((), ()))


def experts_kernel(
    tile,
    hidden,
    x_ref,
    c_ref,
    gate_hbm,
    up_hbm,
    down_hbm,
    moe_ref,
    back_ref,
    d_gate_hbm,
    d_up_hbm,
    d_down_hbm,
    w_gate,
    w_up,
    w_down,
    d_gate_w,
    d_up_w,
    d_down_w,
    acts,
    back_gate,
    back_up,
    stage_wide,
    stage_down,
    load,
    store,
):
    step = pl.program_id(0)
    width, total = w_gate.shape

    @pl.when(step == 0)
    def _():
        loads = [
            pltpu.make_async_copy(gate_hbm, w_gate, load.at[0]),
            pltpu.make_async_copy(up_hbm, w_up, load.at[1]),
            pltpu.make_async_copy(down_hbm, w_down, load.at[2]),
        ]
        for copy in loads:
            copy.start()
        d_gate_w[...] = jnp.zeros_like(d_gate_w)
        d_up_w[...] = jnp.zeros_like(d_up_w)
        d_down_w[...] = jnp.zeros_like(d_down_w)
        for copy in loads:
            copy.wait()

    x = x_ref[:, :width]
    c = c_ref[...]
    routed = x_ref[:, width:]
    first_expert = lax.axis_index("head") * (total // hidden)
    d_gates = jnp.zeros((x.shape[0], LANES), f32)
    for begin in range(0, total, tile):
        js = pl.ds(begin, tile)
        column = begin + lax.broadcasted_iota(jnp.int32, (LANES, tile), 1)
        line = lax.broadcasted_iota(jnp.int32, (LANES, tile), 0)
        expert = first_expert + column // hidden
        here = (line == expert).astype(f32)
        both = (here + (line == expert + LOW).astype(f32)).astype(bf16)
        weight = jnp.dot(routed, both, preferred_element_type=f32)
        gate = jnp.dot(x, w_gate[:, js], preferred_element_type=f32)
        up = jnp.dot(x, w_up[:, js], preferred_element_type=f32)
        d_act = lax.dot_general(c, w_down[js, :], NT, preferred_element_type=f32)
        sigma = 1.0 / (1.0 + jnp.exp(-gate))
        silu = gate * sigma
        act = (silu * up).astype(bf16).astype(f32)
        d_gates = d_gates + lax.dot_general(
            (act * d_act).astype(bf16), here.astype(bf16), NT, preferred_element_type=f32
        )
        acts[:, js] = (act * weight).astype(bf16)
        d_act = d_act * weight
        back_up[:, js] = (d_act * silu).astype(bf16)
        back_gate[:, js] = (d_act * up * sigma * (1.0 + gate * (1.0 - sigma))).astype(bf16)
    back_ref[:, width:] = d_gates.astype(bf16)
    x_turned = x.T
    for begin in range(0, total, tile):
        js = pl.ds(begin, tile)
        d_gate_w[:, js] += jnp.dot(x_turned, back_gate[:, js], preferred_element_type=f32)
        d_up_w[:, js] += jnp.dot(x_turned, back_up[:, js], preferred_element_type=f32)
        d_down_w[js, :] += jnp.dot(acts[:, js].T, c, preferred_element_type=f32)
    for begin in range(0, width, 512):
        cs = pl.ds(begin, 512)
        moe_ref[:, cs] = jnp.dot(acts[...], w_down[:, cs], preferred_element_type=f32).astype(bf16)
        back_ref[:, cs] = (
            lax.dot_general(back_gate[...], w_gate[cs, :], NT, preferred_element_type=f32)
            + lax.dot_general(back_up[...], w_up[cs, :], NT, preferred_element_type=f32)
        ).astype(bf16)

    @pl.when(step == pl.num_programs(0) - 1)
    def _():
        rows = stage_wide.shape[1]
        jobs = [
            (source, target, stage, begin)
            for source, target, stage in (
                (d_gate_w, d_gate_hbm, stage_wide),
                (d_up_w, d_up_hbm, stage_wide),
                (d_down_w, d_down_hbm, stage_down),
            )
            for begin in range(0, source.shape[0], rows)
        ]
        flight = {}
        for index, (source, target, stage, begin) in enumerate(jobs):
            now = index % 2
            if now in flight:
                flight[now].wait()
            stage[now] = source[pl.ds(begin, rows), :].astype(bf16)
            flight[now] = pltpu.make_async_copy(
                stage.at[now], target.at[pl.ds(begin, rows), :], store.at[now]
            )
            flight[now].start()
        for copy in flight.values():
            copy.wait()


def experts(x, c, w_gate, w_up, w_down, hidden):
    tokens, columns = x.shape
    width, total = w_gate.shape
    block = min(256, tokens)
    tile = 256 if total % 256 == 0 else hidden
    return pl.pallas_call(
        functools.partial(experts_kernel, tile, hidden),
        grid=(tokens // block,),
        out_shape=(
            jax.ShapeDtypeStruct((tokens, width), bf16),
            jax.ShapeDtypeStruct((tokens, columns), bf16),
            jax.ShapeDtypeStruct((width, total), bf16),
            jax.ShapeDtypeStruct((width, total), bf16),
            jax.ShapeDtypeStruct((total, width), bf16),
        ),
        in_specs=[
            pl.BlockSpec((block, columns), lambda i: (i, 0)),
            pl.BlockSpec((block, width), lambda i: (i, 0)),
            ANY,
            ANY,
            ANY,
        ],
        out_specs=(
            pl.BlockSpec((block, width), lambda i: (i, 0)),
            pl.BlockSpec((block, columns), lambda i: (i, 0)),
            ANY,
            ANY,
            ANY,
        ),
        scratch_shapes=[
            pltpu.VMEM((width, total), bf16),
            pltpu.VMEM((width, total), bf16),
            pltpu.VMEM((total, width), bf16),
            pltpu.VMEM((width, total), f32),
            pltpu.VMEM((width, total), f32),
            pltpu.VMEM((total, width), f32),
            pltpu.VMEM((block, total), bf16),
            pltpu.VMEM((block, total), bf16),
            pltpu.VMEM((block, total), bf16),
            pltpu.VMEM((2, 64, total), bf16),
            pltpu.VMEM((2, 64, width), bf16),
            DMA((3,)),
            DMA((2,)),
        ],
        compiler_params=pltpu.CompilerParams(vmem_limit_bytes=60 << 20),
        name="experts",
    )(x, c, w_gate, w_up, w_down)


def across(value, chips, mask):
    if mask == 0:
        return value
    return lax.ppermute(value, "chip", [(i, i ^ mask) for i in range(chips)])


def sibling(value):
    return lax.ppermute(value, "core", [(0, 1), (1, 0)])


def per_device(
    layer_input,
    segments,
    routes,
    pair_rank,
    query_key_value_weight,
    output_weight,
    router_weight,
    norm_attn,
    norm_ffn,
    w_gate_up,
    w_down,
    cotangent,
):
    chips = lax.axis_size("chip")
    head_number = lax.axis_size("head")
    sequence_batch, token_rows, width = layer_input.shape
    length = segments.shape[1]
    blk = token_rows * head_number
    query_group = QUERY_HEADS // KEY_VALUE_HEADS
    key_value_location = KEY_VALUE_HEADS // head_number
    loc_experts, slice_rows = w_gate_up.shape[:2]
    top = routes.shape[2]
    tokens_present = sequence_batch * token_rows
    pairs = tokens_present * top
    line_tokens = tokens_present * head_number
    scale = HEAD_WIDTH ** (-0.5)
    hidden = FF // chips
    loc_columns = key_value_location * (query_group + 2) * HEAD_WIDTH
    chip = lax.axis_index("chip")
    core = lax.axis_index("core")
    head = lax.axis_index("head")
    seq_index = chip * 2 + core
    dense_rows = query_key_value_weight.shape[0]

    parts = w_gate_up.reshape(loc_experts, slice_rows, 2, chips, hidden).transpose(3, 2, 1, 0, 4)
    parts = parts.reshape(chips, 2, slice_rows, loc_experts * hidden)
    piled = jnp.zeros((chips, 2, 2, slice_rows, loc_experts * hidden), bf16)
    for mask in range(chips):
        piece = lax.dynamic_index_in_dim(parts, chip ^ mask, 0, keepdims=False)
        piece = across(piece, chips, mask)
        other = sibling(piece)
        piled = lax.dynamic_update_slice(piled, piece[None, None], (chip ^ mask, core, 0, 0, 0))
        piled = lax.dynamic_update_slice(piled, other[None, None], (chip ^ mask, 1 - core, 0, 0, 0))
    piled = piled.transpose(2, 0, 1, 3, 4).reshape(2, width, loc_experts * hidden)
    expert_gate, expert_up = piled[0], piled[1]
    down_other = sibling(w_down)
    expert_down = (
        jnp.where(
            core == 0,
            jnp.concatenate([w_down, down_other], axis=1),
            jnp.concatenate([down_other, w_down], axis=1),
        )
    ).reshape(loc_experts * hidden, width)

    grad_all = lax.all_gather(
        cotangent.reshape(tokens_present, width), ("chip", "head"), axis=0, tiled=True
    )
    dense_out = lax.all_gather(output_weight, ("chip", "core", "head"), axis=0, tiled=True)

    extras = jnp.concatenate([router_weight, norm_attn[:, None], norm_ffn[:, None]], axis=1)
    extras = jnp.pad(extras, ((0, 0), (0, LANES - extras.shape[1])))
    slices = query_key_value_weight.reshape(dense_rows, head_number, loc_columns).transpose(1, 0, 2)
    slices = jnp.concatenate(
        [slices, jnp.broadcast_to(extras, (head_number,) + extras.shape)], axis=2
    )
    lined = line_exchange(slices, head_number, 1)
    dense = gather(
        lined.reshape(head_number * dense_rows, loc_columns + LANES), chips, 1, True, 2
    ).reshape(width, loc_columns + LANES)
    dense_qkv = dense[:, :loc_columns]
    dense_router = dense[:, loc_columns : loc_columns + EXPERTS]
    gain_attn = dense[:, loc_columns + EXPERTS].astype(f32)
    gain_ffn = dense[:, loc_columns + EXPERTS + 1].astype(f32)

    x_line = line_exchange(layer_input.reshape(tokens_present, width), head_number, 3, True)
    x_line = x_line.reshape(line_tokens, width).astype(f32)
    normed_line = x_line * lax.rsqrt(jnp.mean(x_line * x_line, axis=1, keepdims=True) + epsilon)
    first_line = (normed_line * gain_attn).astype(bf16)

    def to_blocks(value):
        columns = value.shape[1:]
        return (
            value.reshape((head_number, sequence_batch, token_rows) + columns)
            .swapaxes(0, 1)
            .reshape((sequence_batch, blk) + columns)
        )

    def to_lines(value):
        columns = value.shape[2:]
        return (
            value.reshape((sequence_batch, head_number, token_rows) + columns)
            .swapaxes(0, 1)
            .reshape((line_tokens,) + columns)
        )

    q_start = seq_index * blk
    q_pos = q_start + jnp.arange(blk, dtype=jnp.int32)
    cosine, sine = rope_tables(q_pos, HEAD_WIDTH)
    projected = to_blocks(jnp.dot(first_line, dense_qkv, preferred_element_type=f32)).reshape(
        sequence_batch, blk, key_value_location, query_group + 2, HEAD_WIDTH
    )
    turned = rotate(projected[:, :, :, : query_group + 1], cosine, sine)
    query_rows = turned[:, :, :, :query_group].astype(bf16)
    keys_values = (
        jnp.stack([turned[:, :, :, query_group], projected[:, :, :, query_group + 1]], axis=3)
        .astype(bf16)
        .reshape(sequence_batch * blk, key_value_location * 2 * HEAD_WIDTH)
    )
    kv_columns = key_value_location * 2 * HEAD_WIDTH
    kv_all = (
        gather(keys_values, chips, 1, True, 4)
        .reshape(2 * chips, sequence_batch, blk, kv_columns)
        .transpose(1, 0, 2, 3)
        .reshape(sequence_batch, length, kv_columns)
    )
    q_seg = lax.dynamic_slice_in_dim(segments, q_start, blk, 1)

    def key_view(piece, offset, token_count):
        portion = lax.dynamic_slice_in_dim(piece, offset, token_count, 1).reshape(
            sequence_batch, token_count, key_value_location, 2, HEAD_WIDTH
        )
        return (portion[:, :, :, 0], portion[:, :, :, 1])

    def key_mask(begin, token_count):
        k_pos = begin + jnp.arange(token_count, dtype=jnp.int32)
        k_seg = lax.dynamic_slice_in_dim(segments, begin, token_count, 1)
        same = q_seg[:, :, None] == k_seg[:, None, :]
        causal = k_pos[None, None, :] <= q_pos[None, :, None]
        return (same & causal)[:, None, None]

    def sweep(function, state):
        sub = 512

        def turn(index, inner):
            offset = index * sub
            return lax.cond(
                offset <= q_start + blk - 1,
                lambda now: function(now, kv_all, offset, sub),
                lambda now: now,
                inner,
            )

        return lax.fori_loop(0, length // sub, turn, state)

    def forward_block(state, piece, offset, token_count):
        top_now, total, accum = state
        keys, values = key_view(piece, offset, token_count)
        scores = (
            jnp.einsum("sqhgd,skhd->shgqk", query_rows, keys, preferred_element_type=f32) * scale
        )
        mask = key_mask(offset, token_count)
        scores = jnp.where(mask, scores, negative)
        top_new = jnp.maximum(top_now, jnp.max(scores, axis=-1))
        weights = jnp.where(mask, jnp.exp(scores - top_new[..., None]), 0.0)
        shrink = jnp.exp(top_now - top_new)
        total = total * shrink + jnp.sum(weights, axis=-1)
        accum = accum * shrink[..., None] + jnp.einsum(
            "shgqk,skhd->shgqd", weights.astype(bf16), values, preferred_element_type=f32
        )
        return (top_new, total, accum)

    state_zero = (
        jnp.full((sequence_batch, key_value_location, query_group, blk), negative, f32),
        jnp.zeros((sequence_batch, key_value_location, query_group, blk), f32),
        jnp.zeros((sequence_batch, key_value_location, query_group, blk, HEAD_WIDTH), f32),
    )
    top_now, total, accum = sweep(forward_block, state_zero)
    lse = top_now + jnp.log(total)
    attended = accum / total[..., None]
    group_columns = key_value_location * query_group * HEAD_WIDTH
    heads_local = to_lines(
        attended.transpose(0, 3, 1, 2, 4).reshape(sequence_batch, blk, group_columns).astype(bf16)
    )
    mixed_heads = (
        line_exchange(
            heads_local.reshape(head_number, tokens_present, group_columns), head_number, 5
        )
        .transpose(1, 0, 2)
        .reshape(tokens_present, QUERY_HEADS * HEAD_WIDTH)
    )
    tokens = layer_input.reshape(tokens_present, width).astype(f32)
    middle = tokens + jnp.dot(mixed_heads, dense_out, preferred_element_type=f32)
    inverse_two = lax.rsqrt(jnp.mean(middle * middle, axis=1, keepdims=True) + epsilon)
    normed_two = middle * inverse_two
    second_input = (normed_two * gain_ffn).astype(bf16)
    router_logits = jnp.dot(second_input, dense_router, preferred_element_type=f32)
    route_flat = routes.reshape(tokens_present, top)
    hot = route_flat[:, :, None] == jnp.arange(EXPERTS, dtype=jnp.int32)[None, None, :]
    chosen = jnp.sum(jnp.where(hot, router_logits[:, None, :], 0.0), axis=2)
    gates = jax.nn.softmax(chosen, axis=-1)
    expert_of = route_flat.reshape(pairs)
    rank = pair_rank.reshape(pairs)
    slot = jnp.sum(
        (expert_of[None, :] == expert_of[:, None]) & (rank[None, :] < rank[:, None]),
        axis=1,
        dtype=jnp.int32,
    )
    kept = (slot < CAP).reshape(tokens_present, top).astype(f32)
    weights_pair = gates * kept
    spread = jnp.sum(jnp.where(hot, weights_pair[:, :, None], 0.0), axis=1)
    spread_high = spread.astype(bf16)
    spread_low = (spread - spread_high.astype(f32)).astype(bf16)
    pad = jnp.zeros((tokens_present, LOW - EXPERTS), bf16)
    payload = jnp.concatenate([second_input, spread_high, pad, spread_low, pad], axis=1)
    columns = width + LANES
    group_tokens = chips * head_number * tokens_present
    x_all = gather(payload, chips, head_number, False, 6).reshape(group_tokens, columns)
    moe_part, back_part, d_gate_w, d_up_w, d_down_w = experts(
        x_all, grad_all, expert_gate, expert_up, expert_down, hidden
    )
    back = scatter_sum(
        back_part.reshape(chips, head_number, tokens_present, columns), chips, head_number, False, 7
    )
    moe = lax.psum_scatter(moe_part, ("chip", "head"), scatter_dimension=0, tiled=True)
    mixed_out = (middle + moe.astype(f32)).astype(bf16)
    mixed_out = mixed_out.reshape(sequence_batch, token_rows, width)

    grads = jnp.stack([d_gate_w, d_up_w]).reshape(2, chips, 2, slice_rows, loc_experts * hidden)
    keep = lax.dynamic_index_in_dim(grads, core, 2, keepdims=False)
    give = lax.dynamic_index_in_dim(grads, 1 - core, 2, keepdims=False)
    shared = (keep.astype(f32) + sibling(give).astype(f32)).astype(bf16)
    piled = jnp.zeros((chips, 2, slice_rows, loc_experts * hidden), bf16)
    for mask in range(chips):
        piece = across(lax.dynamic_index_in_dim(shared, chip ^ mask, 1, keepdims=False), chips, mask)
        piled = lax.dynamic_update_slice(piled, piece[None], (chip ^ mask, 0, 0, 0))
    up_share = (
        piled.reshape(chips, 2, slice_rows, loc_experts, hidden)
        .transpose(3, 2, 1, 0, 4)
        .astype(f32)
        .reshape(loc_experts, slice_rows, 2 * FF)
    )
    d_down_w = d_down_w.reshape(loc_experts, 2, hidden // 2, width)
    keep = lax.dynamic_index_in_dim(d_down_w, core, 1, keepdims=False)
    give = lax.dynamic_index_in_dim(d_down_w, 1 - core, 1, keepdims=False)
    down_share = keep.astype(f32) + sibling(give).astype(f32)

    grad_out = cotangent.reshape(tokens_present, width).astype(f32)
    d_kept = back[:, width : width + EXPERTS]
    grad_gate = jnp.sum(jnp.where(hot, d_kept[:, None, :], 0.0), axis=2) * kept
    grad_chosen = gates * (grad_gate - jnp.sum(gates * grad_gate, axis=1, keepdims=True))
    grad_logits = jnp.sum(jnp.where(hot, grad_chosen[:, :, None], 0.0), axis=1)
    grad_router = jnp.dot(second_input.astype(f32).T, grad_logits, precision=HIGH_PRECISION)
    grad_second = back[:, :width] + jnp.dot(
        grad_logits, dense_router.astype(f32).T, precision=HIGH_PRECISION
    )
    grad_gain_ffn = jnp.sum(grad_second * normed_two, axis=0)
    scaled_two = grad_second * gain_ffn
    grad_mid = grad_out + inverse_two * (
        scaled_two - normed_two * jnp.mean(scaled_two * normed_two, axis=1, keepdims=True)
    )
    grad_attn = grad_mid.astype(bf16)
    grad_dense_out = jnp.dot(mixed_heads.T, grad_attn, preferred_element_type=f32)
    out_share = lax.psum_scatter(
        grad_dense_out.astype(bf16), ("chip", "core", "head"), scatter_dimension=0, tiled=True
    ).astype(f32)
    grad_heads = (
        jnp.dot(grad_attn, dense_out.T, preferred_element_type=f32)
        .astype(bf16)
        .reshape(tokens_present, head_number, group_columns)
        .transpose(1, 0, 2)
    )
    grad_local = to_blocks(
        line_exchange(grad_heads, head_number, 8).reshape(line_tokens, group_columns)
    ).reshape(sequence_batch, blk, key_value_location, query_group, HEAD_WIDTH)
    delta = jnp.sum(grad_local.transpose(0, 2, 3, 1, 4).astype(f32) * attended, axis=-1)

    def backward_block(state, piece, offset, token_count):
        grad_q, grad_store = state
        keys, values = key_view(piece, offset, token_count)
        scores = (
            jnp.einsum("sqhgd,skhd->shgqk", query_rows, keys, preferred_element_type=f32) * scale
        )
        mask = key_mask(offset, token_count)
        probs = jnp.where(mask, jnp.exp(scores - lse[..., None]), 0.0)
        grad_probs = jnp.einsum("sqhgd,skhd->shgqk", grad_local, values, preferred_element_type=f32)
        grad_scores = (probs * (grad_probs - delta[..., None])).astype(bf16)
        grad_q = (
            grad_q
            + jnp.einsum("shgqk,skhd->sqhgd", grad_scores, keys, preferred_element_type=f32) * scale
        )
        grad_k = (
            jnp.einsum("shgqk,sqhgd->skhd", grad_scores, query_rows, preferred_element_type=f32)
            * scale
        )
        grad_v = jnp.einsum(
            "shgqk,sqhgd->skhd", probs.astype(bf16), grad_local, preferred_element_type=f32
        )
        block_width = jnp.stack([grad_k, grad_v], axis=3).reshape(
            sequence_batch, token_count, kv_columns
        )
        grad_store = lax.dynamic_update_slice_in_dim(
            grad_store, block_width.astype(bf16), offset, 1
        )
        return (grad_q, grad_store)

    back_zero = (
        jnp.zeros((sequence_batch, blk, key_value_location, query_group, HEAD_WIDTH), f32),
        jnp.zeros((sequence_batch, length, kv_columns), bf16),
    )
    grad_q, grad_store = sweep(backward_block, back_zero)
    grad_store = (
        grad_store.reshape(sequence_batch, 2 * chips, blk, kv_columns)
        .transpose(1, 0, 2, 3)
        .reshape(chips, 2, sequence_batch * blk, kv_columns)
    )
    grad_kv = scatter_sum(grad_store, chips, 1, True, 9).reshape(
        sequence_batch, blk, key_value_location, 2, HEAD_WIDTH
    )
    grad_proj = jnp.concatenate([grad_q.astype(bf16), grad_kv.astype(bf16)], axis=3).astype(f32)
    unturned = rotate(grad_proj[:, :, :, : query_group + 1], cosine, -sine)
    grad_qkv = to_lines(
        jnp.concatenate([unturned, grad_proj[:, :, :, query_group + 1 :]], axis=3)
        .reshape(sequence_batch, blk, loc_columns)
        .astype(bf16)
    )
    grad_first_part = jnp.dot(grad_qkv, dense_qkv.T, preferred_element_type=f32)
    grad_first = jnp.sum(
        line_exchange(
            grad_first_part.astype(bf16).reshape(head_number, tokens_present, width),
            head_number,
            10,
        ).astype(f32),
        axis=0,
    )
    grad_gain_attn = jnp.sum(grad_first_part * normed_line, axis=0)
    inverse_one = lax.rsqrt(jnp.mean(tokens * tokens, axis=1, keepdims=True) + epsilon)
    normed_one = tokens * inverse_one
    scaled_one = grad_first * gain_attn
    grad_input = grad_mid + inverse_one * (
        scaled_one - normed_one * jnp.mean(scaled_one * normed_one, axis=1, keepdims=True)
    )
    grad_dense_qkv = jnp.dot(first_line.T, grad_qkv, preferred_element_type=f32)
    sums = jnp.concatenate(
        [
            grad_dense_qkv,
            grad_router,
            grad_gain_attn[:, None],
            grad_gain_ffn[:, None],
            jnp.zeros((width, LANES - EXPERTS - 2), f32),
        ],
        axis=1,
    ).astype(bf16)
    sums = scatter_sum(
        sums.reshape(chips, 2, head_number * dense_rows, loc_columns + LANES), chips, 1, True, 11
    )
    sums = line_exchange(
        sums.reshape(head_number, dense_rows, loc_columns + LANES), head_number, 12
    )
    qkv_share = sums[:, :, :loc_columns].transpose(1, 0, 2).reshape(dense_rows, -1)
    extra = jnp.sum(sums[:, :, loc_columns:], axis=0)
    return (
        mixed_out,
        grad_input.reshape(sequence_batch, token_rows, width),
        qkv_share,
        out_share,
        extra[:, :EXPERTS],
        extra[:, EXPERTS],
        extra[:, EXPERTS + 1],
        up_share,
        down_share,
    )


def solution(mesh):
    grid = mesh.devices
    seq, heads = grid.shape
    split = Mesh(grid.reshape(seq // 2, 2, heads), ("chip", "core", "head"))
    places = ("chip", "core", "head")
    inner = ("chip", "core")
    placed = (
        P(None, places, None),
        P(),
        P(None, places, None),
        P(None, places, None),
        P(places, None),
        P(places, None),
        P(places, None),
        P(places),
        P(places),
        P("head", inner, None),
        P("head", inner, None),
        P(None, places, None),
    )
    return jax.shard_map(
        per_device,
        mesh=split,
        in_specs=placed,
        out_specs=(
            P(None, places, None),
            P(None, places, None),
            P(places, None),
            P(places, None),
            P(places, None),
            P(places),
            P(places),
            P("head", inner, None),
            P("head", inner, None),
        ),
        check_vma=False,
    )
```

time: 1650 us -> 909 us (0.55)
  waiting for transfers between devices: 973 us -> 52.5 us
  Pallas kernels: 0 us -> 568 us
  blocking collectives: 275 us -> 0 us
  matrix products: 124 us -> 38.5 us
  starting transfers between devices: 28.7 us -> 9.43 us
    reduce_scatter x5 -> x2, waiting for transfers between devices: 600 us -> 21.6 us  [the longest x1 21.6 us: per_device(): lax.psum_scatter(moe_part, ('chip', 'head'), scatter_dimension=0, tiled=T...]
    pallas_call x0 -> x13, Pallas kernels: none -> 568 us  [the longest x3 160 us: scatter_sum(): pl.pallas_call(functools.partial(scatter_kernel, cube, heads), out_shape=...]
    all_to_all x6 -> x0, waiting for transfers between devices: 227 us -> none  [the longest x1 72.6 us: per_device(): lax.all_to_all(grad_slots, 'head', split_axis=0, concat_axis=1, tiled=True)]
    all_gather x1 -> x0, blocking collectives: 149 us -> none  [per_device(): lax.all_gather(router_weight, ('seq', 'head'), axis=0, tiled=True)]
    dot_general x9 -> x4, matrix products: 99.5 us -> 13.4 us  [the longest x1 4.52 us: per_device(): jnp.dot(first_line, dense_qkv, preferred_element_type=f32)]
    unnamed x2 -> x0, blocking collectives: 83 us -> none
    all_gather x5 -> x2, waiting for transfers between devices: 81 us -> 0.02 us  [the longest x1 0.02 us: per_device(): lax.all_gather(cotangent.reshape(tokens_present, width), ('chip', 'head')...]
    unnamed x12 -> x4, waiting for transfers between devices: 64.6 us -> 1.41 us
  transfers between devices with their start and end apart: 17 -> 17, of which waited for: 14 -> 3; matrix products, arithmetic and copies ran while one was open for 14% -> 27% of each run, Pallas kernels for 0% -> 51%
where the time goes in v1:
time: 909 us; the launch traced here: 895 us
  Pallas kernels  568 us (62%)
  local copies, waits for them, and re-layouts  157 us (17%)
  waiting for transfers between devices  52.5 us (6%)
  other arithmetic  52.5 us (6%)
  matrix products  38.5 us (4%)
  between operations  15.1 us (2%)
  starting transfers between devices  9.43 us (1%)
    pallas_call x3, Pallas kernels, scatter_sum(): pl.pallas_call(functools.partial(scatter_kernel, cube, heads), out_shape=...  160 us
    pallas_call x3, Pallas kernels, gather(): pl.pallas_call(functools.partial(gather_kernel, cube, heads), out_shape=j...  155 us
    pallas_call x6, Pallas kernels, line_exchange(): pl.pallas_call(functools.partial(line_kernel, heads, same), out_shape=jax...  140 us
    pallas_call x1, Pallas kernels, experts(): pl.pallas_call(functools.partial(experts_kernel, tile, hidden), grid=(tok...  114 us
    ppermute x6, waiting for transfers between devices, across(): return lax.ppermute(value, 'chip', [(i, i ^ mask) for i in range(chips)])  29.5 us
    reshape x2, local copies, waits for them, and re-layouts, per_device(): up_share = piled.reshape(chips, 2, slice_rows, loc_experts, hidden).trans...  21.7 us
    reduce_scatter x1, waiting for transfers between devices, per_device(): lax.psum_scatter(moe_part, ('chip', 'head'), scatter_dimension=0, tiled=T...  21.6 us
  transfers between devices with their start and end apart: 17, of which 3 were waited for; matrix products, arithmetic and copies ran while one was open for 27% of the time, Pallas kernels for 51%

profile of v1, /device:TPU:0, one launch (start us, length us, event | category | flops | bytes accessed | tf_op | source)
XLA Modules:
  0.0 894.5 jit_solution(10159233438448062485)
XLA Ops:
  8.7 8.1 reshape.551
  16.8 8.6 copy.341
  25.4 4.5 constant_dynamic-slice_fusion.5
  44.0 13.2 %line_exchange.7 = bf16[4,48,768]{2,1,0:T(8,128)(2,1)} custom-call(bf16[4,48,768]{2,1,0:T(8,128)(2,1)} %pad_maximum_fusion.3.in_ref), custom_call_target="tpu_custom_call" | custom-call | tf_op jit(solution)/shard_map/line_exchange/pallas_call | solution.py:332
  57.2 49.7 %gather.3 = bf16[4,2,192,768]{3,2,1,0:T(8,128)(2,1)} custom-call(bf16[192,768]{1,0:T(8,128)(2,1)} %bitcast.348), custom_call_target="tpu_custom_call" | custom-call | tf_op jit(solution)/shard_map/gather/pallas_call | solution.py:173
  106.9 39.4 %line_exchange.6 = bf16[4,128,1536]{2,1,0:T(8,128)(2,1)} custom-call(bf16[128,1536]{1,0:T(8,128)(2,1)} %bitcast.317), custom_call_target="tpu_custom_call" | custom-call | tf_op jit(solution)/shard_map/line_exchange/pallas_call | solution.py:332
  150.4 4.5 fusion.56
  154.9 3.7 copy.328
  158.6 3.6 reshape_reshape.12
  168.4 18.7 %gather.4 = bf16[4,2,512,256]{3,2,1,0:T(8,128)(2,1)} custom-call(bf16[512,256]{1,0:T(8,128)(2,1)} %reshape.586.in_ref), custom_call_target="tpu_custom_call" | custom-call | tf_op jit(solution)/shard_map/gather/pallas_call | solution.py:173
  187.2 4.5 copy.331
  191.7 2.9 reshape.547
  194.7 5.6 while.38
  194.9 5.1 conditional.6
  205.8 32.3 %line_exchange.8 = bf16[4,128,384]{2,1,0:T(8,128)(2,1)} custom-call(bf16[4,128,384]{2,1,0:T(8,128)(2,1)} %bitcast.345), custom_call_target="tpu_custom_call" | custom-call | tf_op jit(solution)/shard_map/line_exchange/pallas_call | solution.py:332
  249.2 4.6 maximum_select_fusion
  253.8 3.5 fusion.82
  257.3 3.4 multiply_reduce_fusion.3
  265.2 86.5 %gather.5 = bf16[4,4,128,1664]{3,2,1,0:T(8,128)(2,1)} custom-call(bf16[128,1664]{1,0:T(8,128)(2,1)} %concatenate.42.in_ref), custom_call_target="tpu_custom_call" | custom-call | tf_op jit(solution)/shard_map/gather/pallas_call | solution.py:173
  351.7 114.0 %experts.1 = (bf16[2048,1536]{1,0:T(8,128)(2,1)}, bf16[2048,1664]{1,0:T(8,128)(2,1)}, bf16[1536,1280]{1,0:T(8,128)(2,1)}, bf16[1536,1280]{1,0:T(8,128)(2,1)}, bf16[1280,1536]{1,0:T(8,128)(2,1)}) custom-call(bf16[2048,1664]{1,0:T(8,128)(2,1)} %bitcast.306, bf16[2048,1536]{1,0:T(8,128)(2,1)} %all-gather.5.cloned.1.call-done.c_ref, ...), custom_call_target="tpu_custom_call" | custom-call | tf_op jit(solution)/shard_map/experts/pallas_call | solution.py:463
  465.8 4.5 fusion.44
  479.2 3.0 dynamic-slice_bitcast_fusion
  482.6 103.4 %scatter_sum.3 = f32[128,1664]{1,0:T(8,128)} custom-call(bf16[4,4,128,1664]{3,2,1,0:T(8,128)(2,1)} %bitcast.324), custom_call_target="tpu_custom_call" | custom-call | tf_op jit(solution)/shard_map/scatter_sum/pallas_call | solution.py:281
  589.8 2.9 multiply_reduce_fusion.1
  594.2 5.0 fusion.42
  599.2 21.6 %reduce-scatter.3.cloned.1.call-done = bf16[128,1536]{1,0:T(8,128)(2,1)} async-done(((bf16[2048,1536]{1,0:T(8,128)(2,1)}), bf16[128,1536]{1,0:T(8,128)(2,1)}) %reduce-scatter.3.cloned.1.call-update) | async-done | bytes 393232 | tf_op jit(solution)/shard_map/reduce_scatter | solution.py:731
  624.2 3.6 convolution_convert_fusion
  627.8 4.0 dynamic-slice_bitcast_fusion.1
  635.2 4.1 convert_add_fusion.1
  640.8 2.7 broadcast_in_dim.194
  644.6 12.1 %collective-permute-done.9 = bf16[2,192,1280]{2,1,0:T(8,128)(2,1)} collective-permute-done((bf16[2,192,1280]{2,1,0:T(8,128)(2,1)}, bf16[2,192,1280]{2,1,0:T(8,128)(2,1)}, u32[]{:S(2)}, u32[]{:S(2)}) %collective-permute-start.9) | collective-permute-done | bytes 983072 | tf_op jit(solution)/shard_map/ppermute | solution.py:510
  659.1 17.4 %collective-permute-done.10 = bf16[2,192,1280]{2,1,0:T(8,128)(2,1)} collective-permute-done((bf16[2,192,1280]{2,1,0:T(8,128)(2,1)}, bf16[2,192,1280]{2,1,0:T(8,128)(2,1)}, u32[]{:S(2)}, u32[]{:S(2)}) %collective-permute-start.10) | collective-permute-done | bytes 983072 | tf_op jit(solution)/shard_map/ppermute | solution.py:510
  687.5 8.1 convert_bitcast_fusion
  695.6 11.3 %copy.375 = f32[10,192,2,4,128]{4,3,2,1,0:T(4,128)} copy(f32[10,192,2,4,128]{1,4,0,2,3:T(8,128)} %convert_bitcast_fusion) | data formatting | bytes 15728640 | tf_op jit(solution)/shard_map/reshape | solution.py:747
  706.9 10.3 %reshape.572 = f32[10,192,1024]{2,1,0:T(8,128)} reshape(f32[10,192,2,4,128]{4,3,2,1,0:T(4,128)} %copy.375) | data formatting | bytes 15728640 | tf_op jit(solution)/shard_map/reshape | solution.py:747
  717.3 4.7 convolution_convert_fusion.1
  725.9 9.8 %line_exchange.9 = bf16[4,128,384]{2,1,0:T(8,128)(2,1)} custom-call(bf16[4,128,384]{2,1,0:T(8,128)(2,1)} %bitcast.344), custom_call_target="tpu_custom_call" | custom-call | tf_op jit(solution)/shard_map/line_exchange/pallas_call | solution.py:332
  743.2 8.0 while.39
  743.2 7.8 conditional.7
  753.5 2.8 copy.360
  756.3 38.5 %scatter_sum.4 = f32[512,256]{1,0:T(8,128)} custom-call(bf16[4,2,512,256]{3,2,1,0:T(8,128)(2,1)} %bitcast.319), custom_call_target="tpu_custom_call" | custom-call | tf_op jit(solution)/shard_map/scatter_sum/pallas_call | solution.py:281
  798.4 2.8 copy.364
  802.1 4.1 fusion.48
  807.0 2.9 convolution_convert_fusion.2
  810.7 4.7 concatenate.50.in_ref
  815.5 17.6 %scatter_sum.5 = f32[192,768]{1,0:T(8,128)} custom-call(bf16[4,2,192,768]{3,2,1,0:T(8,128)(2,1)} %concatenate.50.in_ref), custom_call_target="tpu_custom_call" | custom-call | tf_op jit(solution)/shard_map/scatter_sum/pallas_call | solution.py:281
  833.1 14.6 %line_exchange.11 = f32[4,48,768]{2,1,0:T(8,128)} custom-call(f32[4,48,768]{2,1,0:T(8,128)} %bitcast.338), custom_call_target="tpu_custom_call" | custom-call | tf_op jit(solution)/shard_map/line_exchange/pallas_call | solution.py:332
  851.2 30.7 %line_exchange.10 = bf16[4,128,1536]{2,1,0:T(8,128)(2,1)} custom-call(bf16[4,128,1536]{2,1,0:T(8,128)(2,1)} %bitcast.340), custom_call_target="tpu_custom_call" | custom-call | tf_op jit(solution)/shard_map/line_exchange/pallas_call | solution.py:332
  (259 shorter events, 125.6 us)
Async XLA Ops:
  7.2 250.2 %all-gather.3.cloned.1.call-start = ((), (), s32[]{:S(2)}) async-start(), calls=%async_computation.2 | async-start | bytes 4866048 | tf_op jit(solution)/shard_map/all_gather | solution.py:575
  7.9 343.8 %all-gather.5.cloned.1.call-start = ((), (), s32[]{:S(2)}) async-start(), calls=%async_computation.3 | async-start | bytes 6684672 | tf_op jit(solution)/shard_map/all_gather | solution.py:572
  8.7 612.2 %reduce-scatter.3.cloned.1.call-start = ((), (), s32[]{:S(2)}) async-start(), calls=%async_computation.4 | async-start | bytes 6684672 | tf_op jit(solution)/shard_map/reduce_scatter | solution.py:731
  31.3 11.7 %copy-start.21 = (bf16[48,2560]{1,0:T(8,128)(2,1)S(1)}, bf16[48,2560]{1,0:T(8,128)(2,1)}, u32[]{:S(2)}) copy-start(bf16[48,2560]{1,0:T(8,128)(2,1)} %param.24) | copy-start | bytes 737284
  31.3 11.7 %copy-start.25 = (bf16[48,40]{0,1:T(8,128)(2,1)S(1)}, bf16[48,40]{0,1:T(8,128)(2,1)}, u32[]{:S(2)}) copy-start(bf16[48,40]{0,1:T(8,128)(2,1)} %param.26) | copy-start | bytes 11524
  31.3 11.7 %copy-start.29 = (bf16[48]{0:T(256)(128)(2,1)S(1)}, bf16[48]{0:T(256)(128)(2,1)}, u32[]{:S(2)}) copy-start(bf16[48]{0:T(256)(128)(2,1)} %param.28) | copy-start | bytes 292
  31.3 11.7 %copy-start.30 = (bf16[48]{0:T(256)(128)(2,1)S(1)}, bf16[48]{0:T(256)(128)(2,1)}, u32[]{:S(2)}) copy-start(bf16[48]{0:T(256)(128)(2,1)} %param.27) | copy-start | bytes 292
  31.3 212.2 %collective-permute-start = (bf16[2,192,1280]{2,1,0:T(8,128)(2,1)}, bf16[2,192,1280]{2,1,0:T(8,128)(2,1)}, u32[]{:S(2)}, u32[]{:S(2)}) collective-permute-start(bf16[2,192,1280]{2,1,0:T(8,128)(2,1)} %bitcast.50), channel_id=1, source_target_pairs={{0,4},{4,0},{1,5},{5,1},{2,6},{6,2},{3,7},{7,3},{8,12},{12,8},{9,1... | collective-permute-start | bytes 2949128 | tf_op jit(solution)/shard_map/ppermute | solution.py:514
  34.2 208.7 %collective-permute-start.1 = (bf16[2,192,1280]{2,1,0:T(8,128)(2,1)}, bf16[2,192,1280]{2,1,0:T(8,128)(2,1)}, u32[]{:S(2)}, u32[]{:S(2)}) collective-permute-start(bf16[2,192,1280]{2,1,0:T(8,128)(2,1)} %bitcast.54), channel_id=1, source_target_pairs={{0,8},{8,0},{16,24},{24,16},{1,9},{9,1},{17,25},{25,17},{2,10},{10... | collective-permute-start | bytes 2949128 | tf_op jit(solution)/shard_map/ppermute | solution.py:510
  39.1 203.8 %collective-permute-start.3 = (bf16[2,192,1280]{2,1,0:T(8,128)(2,1)}, bf16[2,192,1280]{2,1,0:T(8,128)(2,1)}, u32[]{:S(2)}, u32[]{:S(2)}) collective-permute-start(bf16[2,192,1280]{2,1,0:T(8,128)(2,1)} %bitcast.59), channel_id=1, source_target_pairs={{0,16},{8,24},{16,0},{24,8},{1,17},{9,25},{17,1},{25,9},{2,18},{10... | collective-permute-start | bytes 2949128 | tf_op jit(solution)/shard_map/ppermute | solution.py:510
  43.0 200.4 %collective-permute-start.5 = (bf16[2,192,1280]{2,1,0:T(8,128)(2,1)}, bf16[2,192,1280]{2,1,0:T(8,128)(2,1)}, u32[]{:S(2)}, u32[]{:S(2)}) collective-permute-start(bf16[2,192,1280]{2,1,0:T(8,128)(2,1)} %bitcast.64), channel_id=1, source_target_pairs={{0,24},{8,16},{16,8},{24,0},{1,25},{9,17},{17,9},{25,1},{2,26},{10... | collective-permute-start | bytes 2949128 | tf_op jit(solution)/shard_map/ppermute | solution.py:510
  43.0 206.2 %collective-permute-start.7 = (bf16[10,64,1536]{2,1,0:T(8,128)(2,1)}, bf16[10,64,1536]{2,1,0:T(8,128)(2,1)}, u32[]{:S(2)}, u32[]{:S(2)}) collective-permute-start(bf16[10,64,1536]{2,1,0:T(8,128)(2,1)} %param.30), channel_id=1, source_target_pairs={{0,4},{4,0},{1,5},{5,1},{2,6},{6,2},{3,7},{7,3},{8,12},{12,8},{9,1... | collective-permute-start | bytes 5898248 | tf_op jit(solution)/shard_map/ppermute | solution.py:514
  158.6 6.9 copy-start.23
  158.6 6.9 copy-start.24
  164.0 1.4 copy-start.19
  200.2 42.1 %copy-start.6 = (f32[2,2,3,256,64]{3,4,2,1,0:T(8,128)}, f32[2,2,3,256,64]{3,4,2,1,0:T(8,128)S(1)}, u32[]{:S(2)}) copy-start(f32[2,2,3,256,64]{3,4,2,1,0:T(8,128)S(1)} %get-tuple-element.624) | copy-start | bytes 2359300
  200.2 39.9 %copy-start.26 = (s32[2,64,8]{1,2,0:T(8,128)S(1)}, s32[2,64,8]{1,2,0:T(8,128)}, u32[]{:S(2)}) copy-start(s32[2,64,8]{1,2,0:T(8,128)} %param.23) | copy-start | bytes 12292
  241.6 1.2 copy-start.11
  242.9 3.3 collective-permute-start.2
  243.0 4.7 collective-permute-start.4
  243.5 5.6 collective-permute-start.6
  246.2 3.0 copy-start.14
  260.9 0.7 copy-start.13
  465.8 420.1 %reduce-scatter.5.cloned.1.call-start = ((), (), s32[]{:S(2)}) async-start(), calls=%async_computation.5 | async-start | bytes 4866048 | tf_op jit(solution)/shard_map/reduce_scatter | solution.py:770
  465.8 4.6 copy-start
  470.4 123.8 %collective-permute-start.8 = (bf16[2,4,192,1280]{3,2,1,0:T(8,128)(2,1)}, bf16[2,4,192,1280]{3,2,1,0:T(8,128)(2,1)}, u32[]{:S(2)}, u32[]{:S(2)}) collective-permute-start(bf16[2,4,192,1280]{3,2,1,0:T(8,128)(2,1)} %fusion.44), channel_id=1, source_target_pairs={{0,4},{4,0},{1,5},{5,1},{2,6},{6,2},{3,7},{7,3},{8,12},{12,8},{9,1... | collective-permute-start | bytes 11796488 | tf_op jit(solution)/shard_map/ppermute | solution.py:514
  482.1 153.1 %collective-permute-start.12 = (bf16[10,64,1536]{2,1,0:T(8,128)(2,1)}, bf16[10,64,1536]{2,1,0:T(8,128)(2,1)}, u32[]{:S(2)}, u32[]{:S(2)}) collective-permute-start(bf16[10,64,1536]{2,1,0:T(8,128)(2,1)} %dynamic-slice_bitcast_fusion), channel_id=1, source_target_pairs={{0,4},{4,0},{1,5},{5,1},{2,6},{6,2},{3,7},{7,3},{8,12},{12,8},{9,1... | collective-permute-start | bytes 5898248 | tf_op jit(solution)/shard_map/ppermute | solution.py:514
  620.8 3.3 copy-start.8
  623.3 0.9 copy-start.2
  627.7 7.5 copy-start.12
  631.7 25.0 %collective-permute-start.9 = (bf16[2,192,1280]{2,1,0:T(8,128)(2,1)}, bf16[2,192,1280]{2,1,0:T(8,128)(2,1)}, u32[]{:S(2)}, u32[]{:S(2)}) collective-permute-start(bf16[2,192,1280]{2,1,0:T(8,128)(2,1)} %get-tuple-element.793), channel_id=1, source_target_pairs={{0,8},{8,0},{16,24},{24,16},{1,9},{9,1},{17,25},{25,17},{2,10},{10... | collective-permute-start | bytes 2949128 | tf_op jit(solution)/shard_map/ppermute | solution.py:510
  633.2 43.3 %collective-permute-start.10 = (bf16[2,192,1280]{2,1,0:T(8,128)(2,1)}, bf16[2,192,1280]{2,1,0:T(8,128)(2,1)}, u32[]{:S(2)}, u32[]{:S(2)}) collective-permute-start(bf16[2,192,1280]{2,1,0:T(8,128)(2,1)} %get-tuple-element.792), channel_id=1, source_target_pairs={{0,16},{8,24},{16,0},{24,8},{1,17},{9,25},{17,1},{25,9},{2,18},{10... | collective-permute-start | bytes 2949128 | tf_op jit(solution)/shard_map/ppermute | solution.py:510
  634.2 44.7 %collective-permute-start.11 = (bf16[2,192,1280]{2,1,0:T(8,128)(2,1)}, bf16[2,192,1280]{2,1,0:T(8,128)(2,1)}, u32[]{:S(2)}, u32[]{:S(2)}) collective-permute-start(bf16[2,192,1280]{2,1,0:T(8,128)(2,1)} %get-tuple-element.791), channel_id=1, source_target_pairs={{0,24},{8,16},{16,8},{24,0},{1,25},{9,17},{17,9},{25,1},{2,26},{10... | collective-permute-start | bytes 2949128 | tf_op jit(solution)/shard_map/ppermute | solution.py:510
  640.8 2.7 copy-start.10
  681.3 5.0 copy-start.9
  706.9 10.4 %copy-start.3 = (f32[128,1536]{1,0:T(8,128)S(1)}, f32[128,1536]{1,0:T(8,128)}, u32[]{:S(2)}) copy-start(f32[128,1536]{1,0:T(8,128)} %copy-done.2) | copy-start | bytes 2359300
  722.0 18.3 %copy-start.7 = (f32[2,2,3,256,64]{3,4,2,1,0:T(8,128)S(1)}, f32[2,2,3,256,64]{3,4,2,1,0:T(8,128)}, u32[]{:S(2)}) copy-start(f32[2,2,3,256,64]{3,4,2,1,0:T(8,128)} %copy-done.6) | copy-start | bytes 2359300
  743.3 1.5 copy-start.17
  756.3 40.3 %copy-start.20 = (f32[256,32]{0,1:T(8,128)S(1)}, f32[256,32]{0,1:T(8,128)}, u32[]{:S(2)}) copy-start(f32[256,32]{0,1:T(8,128)} %copy-done.19) | copy-start | bytes 98308
  756.3 40.3 %copy-start.22 = (f32[256,32]{0,1:T(8,128)S(1)}, f32[256,32]{0,1:T(8,128)}, u32[]{:S(2)}) copy-start(f32[256,32]{0,1:T(8,128)} %get-tuple-element.805) | copy-start | bytes 98308
  796.5 5.6 copy-start.1
  796.5 5.6 copy-start.27
  801.3 0.8 copy-start.18
  806.3 4.5 copy-start.15
  806.3 4.5 copy-start.16
  847.7 36.0 %copy-start.5 = (bf16[2,64,1536]{2,1,0:T(8,128)(2,1)S(1)}, bf16[2,64,1536]{2,1,0:T(8,128)(2,1)}, u32[]{:S(2)}) copy-start(bf16[2,64,1536]{2,1,0:T(8,128)(2,1)} %param.20) | copy-start | bytes 1179652
  848.8 35.9 %copy-start.4 = (f32[128,1536]{1,0:T(8,128)S(1)}, f32[128,1536]{1,0:T(8,128)}, u32[]{:S(2)}) copy-start(f32[128,1536]{1,0:T(8,128)} %copy-done.2) | copy-start | bytes 2359300
  848.8 35.9 %copy-start.28 = (f32[128]{0:T(128)S(1)}, f32[128]{0:T(128)}, u32[]{:S(2)}) copy-start(f32[128]{0:T(128)} %rsqrt.40) | copy-start | bytes 1540
Sparse Core Ops, SparseCore 0:
  10.8 98.8 all-gather.2
  112.5 111.9 all-gather.4
  465.9 154.9 reduce-scatter.2
  627.9 107.2 reduce-scatter.4

commit v2 on v1

--- a/solution.py
+++ b/solution.py
@@ -504,6 +504,343 @@
     )(x, c, w_gate, w_up, w_down)
 
 
+def turn_kernel(cube, heads, tile, hidden, own_ref, c_hbm, gate_hbm, up_hbm, down_hbm, out_ref, moe_hbm, d_gate_hbm, d_up_hbm, d_down_hbm, *refs):
+    chips, count = cube.chips, cube.number
+    tokens, turned, cots, w_gate, w_up, w_down, acts, back_gate, back_up, d_gates, moe_stage, line_in = refs[:12]
+    arrived = refs[12 : 12 + count]
+    load, store, own_sem, line_send, line_recv, send, recv, back_send, back_recv, end_send, end_recv = refs[12 + count :]
+    hz = lax.axis_index("head")
+    rows, columns = own_ref.shape
+    width, total = w_gate.shape
+    half = rows // 2
+    line = heads * rows
+    others = near(heads)
+    masks = sorted(range(chips), key=lambda m: bin(m).count("1"))
+
+    loads = [
+        pltpu.make_async_copy(source, target, load.at[index])
+        for index, (source, target) in enumerate(
+            ((gate_hbm, w_gate), (up_hbm, w_up), (down_hbm, w_down), (c_hbm, cots))
+        )
+    ]
+    for copy in loads:
+        copy.start()
+    meet([cube.peer(digit) for digit in range(count)] + [{"head": (hz + d) % heads} for d in others])
+
+    def part(side):
+        return pl.ds(side * half, half)
+
+    def line_copy(d):
+        return pltpu.make_async_remote_copy(
+            src_ref=own_ref,
+            dst_ref=tokens.at[cube.place(0) + (hz,)],
+            send_sem=line_send.at[d - 1],
+            recv_sem=line_recv.at[d - 1],
+            device_id={"head": (hz + d) % heads},
+            device_id_type=MESH,
+        )
+
+    def plane_copy(side, mask, k, d):
+        digit = cube.gather_orders[side][k]
+        later = mask | (1 << digit)
+        place = tokens.at[cube.place(mask) + ((hz + heads - d) % heads, part(side))]
+        return pltpu.make_async_remote_copy(
+            src_ref=own_ref.at[part(side)] if mask == 0 and d == 0 else place,
+            dst_ref=place,
+            send_sem=send.at[side, later, d],
+            recv_sem=recv.at[side, later, d],
+            device_id=cube.peer(digit),
+            device_id_type=MESH,
+        )
+
+    def steps_after(side, mask):
+        order = cube.gather_orders[side]
+        last = max([k for k in range(count) if (mask >> order[k]) & 1], default=-1)
+        return range(last + 1, count)
+
+    def arrival(side, mask, d):
+        order = cube.gather_orders[side]
+        k = max(k for k in range(count) if (mask >> order[k]) & 1)
+        return plane_copy(side, mask & ~(1 << order[k]), k, d)
+
+    def receive(mask):
+        for d in [0] + others:
+            if mask == 0 and d:
+                line_copy(d).wait_recv()
+            for side in range(2):
+                if mask:
+                    arrival(side, mask, d).wait_recv()
+                for k in steps_after(side, mask):
+                    plane_copy(side, mask, k, d).start()
+
+    def sent(mask):
+        for d in [0] + others:
+            for side in range(2):
+                for k in steps_after(side, mask):
+                    plane_copy(side, mask, k, d).wait_send()
+
+    def slot(side, k, mask):
+        return subsets(cube.scatter_orders[side][k + 1 :]).index(mask)
+
+    def back_place(side, mask, d):
+        return tokens.at[cube.place(mask) + ((hz + d) % heads, part(side))]
+
+    def back_copy(side, k, mask, d):
+        order = cube.scatter_orders[side]
+        where = slot(side, k, mask)
+        return pltpu.make_async_remote_copy(
+            src_ref=back_place(side, mask | (1 << order[k]), d),
+            dst_ref=arrived[k].at[side, where, d],
+            send_sem=back_send.at[side, k, where, d],
+            recv_sem=back_recv.at[side, k, where, d],
+            device_id=cube.peer(order[k]),
+            device_id_type=MESH,
+        )
+
+    def end_copy(d):
+        return pltpu.make_async_remote_copy(
+            src_ref=tokens.at[cube.place(0) + ((hz + d) % heads,)],
+            dst_ref=line_in.at[d - 1],
+            send_sem=end_send.at[d - 1],
+            recv_sem=end_recv.at[d - 1],
+            device_id={"head": (hz + d) % heads},
+            device_id_type=MESH,
+        )
+
+    outward = others[::-1] + [0]
+
+    def give(mask):
+        for d in outward:
+            for side in range(2):
+                first = 1 << cube.scatter_orders[side][0]
+                if mask & first:
+                    back_copy(side, 0, mask & ~first, d).start()
+
+    own = pltpu.make_async_copy(own_ref, tokens.at[cube.place(0) + (hz,)], own_sem)
+    own.start()
+    for d in others:
+        line_copy(d).start()
+    for copy in loads:
+        copy.wait()
+    own.wait()
+
+    first_expert = hz * (total // hidden)
+    span = min(512, width)
+
+    def compute(place):
+        here = pl.ds(place * line, line)
+        x = tokens[place, :, :, pl.ds(0, width)].reshape(line, width)
+        c = cots[here, :]
+        routed = tokens[place, :, :, pl.ds(width, LANES)].reshape(line, LANES)
+        turned[:, here] = x.T
+        d_gates[...] = jnp.zeros_like(d_gates)
+
+        @pl.loop(0, total // tile)
+        def _(j):
+            js = pl.ds(pl.multiple_of(j * tile, tile), tile)
+            column = j * tile + lax.broadcasted_iota(jnp.int32, (LANES, tile), 1)
+            lane = lax.broadcasted_iota(jnp.int32, (LANES, tile), 0)
+            expert = first_expert + column // hidden
+            high = (lane == expert).astype(f32)
+            both = (high + (lane == expert + LOW).astype(f32)).astype(bf16)
+            weight = jnp.dot(routed, both, preferred_element_type=f32)
+            gate = jnp.dot(x, w_gate[:, js], preferred_element_type=f32)
+            up = jnp.dot(x, w_up[:, js], preferred_element_type=f32)
+            d_act = lax.dot_general(c, w_down[js, :], NT, preferred_element_type=f32)
+            sigma = 1.0 / (1.0 + jnp.exp(-gate))
+            silu = gate * sigma
+            act = (silu * up).astype(bf16).astype(f32)
+            d_gates[...] += lax.dot_general(
+                (act * d_act).astype(bf16), high.astype(bf16), NT, preferred_element_type=f32
+            )
+            acts[here, js] = (act * weight).astype(bf16)
+            d_act = d_act * weight
+            back_up[here, js] = (d_act * silu).astype(bf16)
+            back_gate[here, js] = (d_act * up * sigma * (1.0 + gate * (1.0 - sigma))).astype(bf16)
+
+    def results(place, step):
+        here = pl.ds(place * line, line)
+
+        @pl.loop(0, width // span)
+        def _(j):
+            cs = pl.ds(pl.multiple_of(j * span, span), span)
+            value = lax.dot_general(
+                back_gate[here, :], w_gate[cs, :], NT, preferred_element_type=f32
+            ) + lax.dot_general(back_up[here, :], w_up[cs, :], NT, preferred_element_type=f32)
+            tokens[place, :, :, cs] = value.astype(bf16).reshape(heads, rows, span)
+
+        tokens[place, :, :, pl.ds(width, LANES)] = (
+            d_gates[...].astype(bf16).reshape(heads, rows, LANES)
+        )
+
+    def moe_copy(place):
+        return pltpu.make_async_copy(
+            moe_stage, moe_hbm.at[pl.ds(place * line, line)], store.at[3]
+        )
+
+    def mixed(place, step):
+        here = pl.ds(place * line, line)
+
+        @pl.when(step > 0)
+        def _():
+            moe_copy(place).wait()
+
+        @pl.loop(0, width // span)
+        def _(j):
+            cs = pl.ds(pl.multiple_of(j * span, span), span)
+            moe_stage[:, cs] = jnp.dot(
+                acts[here, :], w_down[:, cs], preferred_element_type=f32
+            ).astype(bf16)
+
+        moe_copy(place).start()
+
+    @pl.loop(0, chips)
+    def _(step):
+        seen = -1
+        for index, mask in enumerate(masks):
+            level = bin(mask).count("1")
+            if level > seen:
+                seen = level
+
+                @pl.when(step == index)
+                def _():
+                    for other in masks:
+                        if bin(other).count("1") == level:
+                            receive(other)
+
+        place = cube.place(0)[0] * 0
+        for index, mask in enumerate(masks):
+            place = jnp.where(step == index, cube.place(mask)[0], place)
+        compute(place)
+        for index, mask in enumerate(masks):
+
+            @pl.when(step == index)
+            def _():
+                sent(mask)
+
+        results(place, step)
+        for index, mask in enumerate(masks):
+            if mask:
+
+                @pl.when(step == index)
+                def _():
+                    give(mask)
+
+        mixed(place, step)
+
+    def sums(side, steps, mask, d):
+        value = back_place(side, mask, d)[...].astype(f32)
+        for j in range(steps):
+            back_copy(side, j, mask, d).wait_recv()
+            value = value + arrived[j][side, slot(side, j, mask), d].astype(f32)
+        return value
+
+    def weights_grad(left, right, target, hbm, index, by_rows):
+        @pl.loop(0, total // tile)
+        def _(j):
+            js = pl.ds(pl.multiple_of(j * tile, tile), tile)
+            if by_rows:
+                value = jnp.dot(left[:, js].T, right[...], preferred_element_type=f32)
+                target[js, :] = value.astype(bf16)
+            else:
+                value = jnp.dot(left[...], right[:, js], preferred_element_type=f32)
+                target[:, js] = value.astype(bf16)
+
+        pltpu.make_async_copy(target, hbm, store.at[index]).start()
+
+    weights_grad(turned, back_gate, w_gate, d_gate_hbm, 0, False)
+    for k in range(1, count):
+        for d in outward:
+            for side in range(2):
+                order = cube.scatter_orders[side]
+                for mask in subsets(order[k + 1 :])[::-1]:
+                    full = mask | (1 << order[k])
+                    back_place(side, full, d)[...] = sums(side, k, full, d).astype(bf16)
+                    back_copy(side, k, mask, d).start()
+    weights_grad(turned, back_up, w_up, d_up_hbm, 1, False)
+    for d in outward:
+        for side in range(2):
+            value = sums(side, count, 0, d)
+            if d:
+                back_place(side, 0, d)[...] = value.astype(bf16)
+            else:
+                out_ref[part(side)] = value
+        if d:
+            end_copy(d).start()
+    moe_copy(0).wait()
+    weights_grad(acts, cots, w_down, d_down_hbm, 2, True)
+    for d in others:
+        end_copy(d).wait_recv()
+        out_ref[...] += line_in[d - 1].astype(f32)
+    for d in others:
+        line_copy(d).wait_send()
+        end_copy(d).wait_send()
+    for side in range(2):
+        for k in range(count):
+            for mask in subsets(cube.scatter_orders[side][k + 1 :]):
+                for d in outward:
+                    back_copy(side, k, mask, d).wait_send()
+    for index, (source, hbm) in enumerate(
+        ((w_gate, d_gate_hbm), (w_up, d_up_hbm), (w_down, d_down_hbm))
+    ):
+        pltpu.make_async_copy(source, hbm, store.at[index]).wait()
+
+
+def expert_turn(payload, c, w_gate, w_up, w_down, hidden, chips, heads, number):
+    rows, columns = payload.shape
+    width, total = w_gate.shape
+    cube = Cube(chips, False)
+    count = cube.number
+    tokens = chips * heads * rows
+    half = rows // 2
+    tile = 256 if total % 256 == 0 else hidden
+    slots = [chips >> (k + 1) for k in range(count)]
+    return pl.pallas_call(
+        functools.partial(turn_kernel, cube, heads, tile, hidden),
+        out_shape=(
+            jax.ShapeDtypeStruct((rows, columns), f32),
+            jax.ShapeDtypeStruct((tokens, width), bf16),
+            jax.ShapeDtypeStruct((width, total), bf16),
+            jax.ShapeDtypeStruct((width, total), bf16),
+            jax.ShapeDtypeStruct((total, width), bf16),
+        ),
+        in_specs=[WHOLE, ANY, ANY, ANY, ANY],
+        out_specs=(WHOLE, ANY, ANY, ANY, ANY),
+        scratch_shapes=[
+            pltpu.VMEM((chips, heads, rows, columns), bf16),
+            pltpu.VMEM((width, tokens), bf16),
+            pltpu.VMEM((tokens, width), bf16),
+            pltpu.VMEM((width, total), bf16),
+            pltpu.VMEM((width, total), bf16),
+            pltpu.VMEM((total, width), bf16),
+            pltpu.VMEM((tokens, total), bf16),
+            pltpu.VMEM((tokens, total), bf16),
+            pltpu.VMEM((tokens, total), bf16),
+            pltpu.VMEM((heads * rows, LANES), f32),
+            pltpu.VMEM((heads * rows, width), bf16),
+            pltpu.VMEM((heads - 1, rows, columns), bf16),
+        ]
+        + [pltpu.VMEM((2, s, heads, half, columns), bf16) for s in slots]
+        + [
+            DMA((4,)),
+            DMA((4,)),
+            DMA,
+            DMA((heads - 1,)),
+            DMA((heads - 1,)),
+            DMA((2, chips, heads)),
+            DMA((2, chips, heads)),
+            DMA((2, count, slots[0], heads)),
+            DMA((2, count, slots[0], heads)),
+            DMA((heads - 1,)),
+            DMA((heads - 1,)),
+        ],
+        compiler_params=pltpu.CompilerParams(
+            collective_id=number, has_side_effects=True, vmem_limit_bytes=63 << 20
+        ),
+        name="expert_turn",
+    )(payload, c, w_gate, w_up, w_down)
+
+
 def across(value, chips, mask):
     if mask == 0:
         return value
@@ -721,13 +1058,18 @@
     payload = jnp.concatenate([second_input, spread_high, pad, spread_low, pad], axis=1)
     columns = width + LANES
     group_tokens = chips * head_number * tokens_present
-    x_all = gather(payload, chips, head_number, False, 6).reshape(group_tokens, columns)
-    moe_part, back_part, d_gate_w, d_up_w, d_down_w = experts(
-        x_all, grad_all, expert_gate, expert_up, expert_down, hidden
-    )
-    back = scatter_sum(
-        back_part.reshape(chips, head_number, tokens_present, columns), chips, head_number, False, 7
-    )
+    needs = 10 * group_tokens * width + 6 * width * expert_gate.shape[1]
+    if needs + 6 * group_tokens * expert_gate.shape[1] <= 60 << 20:
+        back, moe_part, d_gate_w, d_up_w, d_down_w = expert_turn(
+            payload, grad_all, expert_gate, expert_up, expert_down, hidden, chips, head_number, 6
+        )
+    else:
+        x_all = gather(payload, chips, head_number, False, 6).reshape(group_tokens, columns)
+        moe_part, back_part, d_gate_w, d_up_w, d_down_w = experts(
+            x_all, grad_all, expert_gate, expert_up, expert_down, hidden
+        )
+        back_part = back_part.reshape(chips, head_number, tokens_present, columns)
+        back = scatter_sum(back_part, chips, head_number, False, 7)
     moe = lax.psum_scatter(moe_part, ("chip", "head"), scatter_dimension=0, tiled=True)
     mixed_out = (middle + moe.astype(f32)).astype(bf16)
     mixed_out = mixed_out.reshape(sequence_batch, token_rows, width)

time: 909 us -> 902 us (level)
  Pallas kernels: 568 us -> 463 us
  waiting for transfers between devices: 52.5 us -> 150 us
    reduce_scatter x1, waiting for transfers between devices: 21.6 us -> 120 us  [per_device(): lax.psum_scatter(moe_part, ('chip', 'head'), scatter_dimension=0, tiled=T...]
    pallas_call x3 -> x2, Pallas kernels: 160 us -> 61.6 us  [scatter_sum(): pl.pallas_call(functools.partial(scatter_kernel, cube, heads), out_shape=...]
    pallas_call x3 -> x2, Pallas kernels: 155 us -> 67 us  [gather(): pl.pallas_call(functools.partial(gather_kernel, cube, heads), out_shape=j...]
    pallas_call x1, Pallas kernels: 114 us -> 193 us  [expert_turn(): pl.pallas_call(functools.partial(turn_kernel, cube, heads, tile, hidden),...]
  transfers between devices with their start and end apart: 17 -> 17, of which waited for: 3 -> 3; matrix products, arithmetic and copies ran while one was open for 27% -> 28% of each run, Pallas kernels for 51% -> 30%
where the time goes in v2:
time: 902 us; the launch traced here: 887 us
  Pallas kernels  463 us (51%)
  local copies, waits for them, and re-layouts  160 us (18%)
  waiting for transfers between devices  150 us (17%)
  other arithmetic  52.3 us (6%)
  matrix products  36.6 us (4%)
  between operations  15 us (2%)
  starting transfers between devices  9.4 us (1%)
    pallas_call x1, Pallas kernels, expert_turn(): pl.pallas_call(functools.partial(turn_kernel, cube, heads, tile, hidden),...  193 us
    pallas_call x6, Pallas kernels, line_exchange(): pl.pallas_call(functools.partial(line_kernel, heads, same), out_shape=jax...  141 us
    reduce_scatter x1, waiting for transfers between devices, per_device(): lax.psum_scatter(moe_part, ('chip', 'head'), scatter_dimension=0, tiled=T...  120 us
    pallas_call x2, Pallas kernels, gather(): pl.pallas_call(functools.partial(gather_kernel, cube, heads), out_shape=j...  67 us
    pallas_call x2, Pallas kernels, scatter_sum(): pl.pallas_call(functools.partial(scatter_kernel, cube, heads), out_shape=...  61.6 us
    ppermute x6, waiting for transfers between devices, across(): return lax.ppermute(value, 'chip', [(i, i ^ mask) for i in range(chips)])  28.5 us
    reshape x2, local copies, waits for them, and re-layouts, per_device(): up_share = piled.reshape(chips, 2, slice_rows, loc_experts, hidden).trans...  21.6 us
  transfers between devices with their start and end apart: 17, of which 3 were waited for; matrix products, arithmetic and copies ran while one was open for 28% of the time, Pallas kernels for 30%

profile of v2, /device:TPU:0, one launch (start us, length us, event | category | flops | bytes accessed | tf_op | source)
XLA Modules:
  0.0 887.1 jit_solution(5013119028743848665)
XLA Ops:
  8.7 8.1 reshape.544
  16.8 8.6 copy.341
  25.4 4.3 constant_dynamic-slice_fusion.5
  42.7 12.5 %line_exchange.7 = bf16[4,48,768]{2,1,0:T(8,128)(2,1)} custom-call(bf16[4,48,768]{2,1,0:T(8,128)(2,1)} %pad_maximum_fusion.3.in_ref), custom_call_target="tpu_custom_call" | custom-call | tf_op jit(solution)/shard_map/line_exchange/pallas_call | solution.py:332
  55.2 51.4 %gather.2 = bf16[4,2,192,768]{3,2,1,0:T(8,128)(2,1)} custom-call(bf16[192,768]{1,0:T(8,128)(2,1)} %bitcast.344), custom_call_target="tpu_custom_call" | custom-call | tf_op jit(solution)/shard_map/gather/pallas_call | solution.py:173
  106.7 39.2 %line_exchange.6 = bf16[4,128,1536]{2,1,0:T(8,128)(2,1)} custom-call(bf16[128,1536]{1,0:T(8,128)(2,1)} %bitcast.314), custom_call_target="tpu_custom_call" | custom-call | tf_op jit(solution)/shard_map/line_exchange/pallas_call | solution.py:332
  150.1 3.5 fusion.56
  156.2 2.8 reshape_reshape.12
  164.1 15.6 %gather.3 = bf16[4,2,512,256]{3,2,1,0:T(8,128)(2,1)} custom-call(bf16[512,256]{1,0:T(8,128)(2,1)} %reshape.578.in_ref), custom_call_target="tpu_custom_call" | custom-call | tf_op jit(solution)/shard_map/gather/pallas_call | solution.py:173
  179.7 4.5 copy.331
  184.2 2.9 reshape.541
  187.2 6.5 while.38
  187.7 5.8 conditional.6
  194.6 2.7 convert_element_type.217
  199.4 34.5 %line_exchange.8 = bf16[4,128,384]{2,1,0:T(8,128)(2,1)} custom-call(bf16[4,128,384]{2,1,0:T(8,128)(2,1)} %bitcast.341), custom_call_target="tpu_custom_call" | custom-call | tf_op jit(solution)/shard_map/line_exchange/pallas_call | solution.py:332
  245.1 4.6 maximum_select_fusion
  249.7 3.5 fusion.85
  253.2 3.2 multiply_reduce_fusion.3
  261.0 193.3 %expert_turn.1 = (f32[128,1664]{1,0:T(8,128)}, bf16[2048,1536]{1,0:T(8,128)(2,1)}, bf16[1536,1280]{1,0:T(8,128)(2,1)}, bf16[1536,1280]{1,0:T(8,128)(2,1)}, bf16[1280,1536]{1,0:T(8,128)(2,1)}) custom-call(bf16[128,1664]{1,0:T(8,128)(2,1)} %concatenate.42.own_ref, bf16[2048,1536]{1,0:T(8,128)(2,1)} %all-gather.5.cloned.1.call-done.c_hbm, ...), custom_call_target="tpu_custom_call" | custom-call | tf_op jit(solution)/shard_map/expert_turn/pallas_call | solution.py:798
  454.5 4.5 fusion.44
  460.6 3.0 copy.365
  465.5 3.0 dynamic-slice_bitcast_fusion
  471.7 2.8 multiply_reduce_fusion.1
  476.5 5.2 fusion.42
  481.7 119.6 %reduce-scatter.3.cloned.1.call-done = bf16[128,1536]{1,0:T(8,128)(2,1)} async-done(((bf16[2048,1536]{1,0:T(8,128)(2,1)}), bf16[128,1536]{1,0:T(8,128)(2,1)}) %reduce-scatter.3.cloned.1.call-update) | async-done | bytes 393232 | tf_op jit(solution)/shard_map/reduce_scatter | solution.py:1073
  603.9 3.6 convolution_convert_fusion
  607.5 4.3 dynamic-slice_bitcast_fusion.1
  615.2 4.1 convert_add_fusion.1
  621.7 2.7 broadcast_in_dim.194
  625.6 11.2 %collective-permute-done.9 = bf16[2,192,1280]{2,1,0:T(8,128)(2,1)} collective-permute-done((bf16[2,192,1280]{2,1,0:T(8,128)(2,1)}, bf16[2,192,1280]{2,1,0:T(8,128)(2,1)}, u32[]{:S(2)}, u32[]{:S(2)}) %collective-permute-start.9) | collective-permute-done | bytes 983072 | tf_op jit(solution)/shard_map/ppermute | solution.py:847
  639.1 17.3 %collective-permute-done.10 = bf16[2,192,1280]{2,1,0:T(8,128)(2,1)} collective-permute-done((bf16[2,192,1280]{2,1,0:T(8,128)(2,1)}, bf16[2,192,1280]{2,1,0:T(8,128)(2,1)}, u32[]{:S(2)}, u32[]{:S(2)}) %collective-permute-start.10) | collective-permute-done | bytes 983072 | tf_op jit(solution)/shard_map/ppermute | solution.py:847
  667.3 8.2 convert_bitcast_fusion
  675.5 11.5 %copy.375 = f32[10,192,2,4,128]{4,3,2,1,0:T(4,128)} copy(f32[10,192,2,4,128]{1,4,0,2,3:T(8,128)} %convert_bitcast_fusion) | data formatting | bytes 15728640 | tf_op jit(solution)/shard_map/reshape | solution.py:1089
  687.1 10.1 %reshape.564 = f32[10,192,1024]{2,1,0:T(8,128)} reshape(f32[10,192,2,4,128]{4,3,2,1,0:T(4,128)} %copy.375) | data formatting | bytes 15728640 | tf_op jit(solution)/shard_map/reshape | solution.py:1089
  697.2 4.8 convolution_convert_fusion.1
  705.8 9.7 %line_exchange.9 = bf16[4,128,384]{2,1,0:T(8,128)(2,1)} custom-call(bf16[4,128,384]{2,1,0:T(8,128)(2,1)} %bitcast.340), custom_call_target="tpu_custom_call" | custom-call | tf_op jit(solution)/shard_map/line_exchange/pallas_call | solution.py:332
  717.6 2.6 reshape_reshape.15
  723.6 9.7 %while.39 = (s32[]{:T(128)}, f32[2,256,2,3,64]{1,4,3,2,0:T(8,128)S(1)}, bf16[2,2048,256]{1,2,0:T(8,128)(2,1)}, s32[]{:T(128)}, bf16[2,2048,256]{1,2,0:T(8,128)(2...) while((s32[]{:T(128)}, ...), condition=%wide.region_23.24_spmd.clone, body=%wide.region_20.23_spmd.clone.sunk | while | flops 1024066304 | bytes 39758280 | solution.py:997
  723.7 9.5 %conditional.7 = ((f32[2,256,2,3,64]{1,4,3,2,0:T(8,128)S(1)}, bf16[2,2048,256]{1,2,0:T(8,128)(2,1)})) conditional(s32[]{:T(128)} %convert_element_type.348, (f32[2,256,2,3,64]{1,4,3,2,0:T(8,128)S(1)}, bf16[2,2048,256]{1,2,0:T(8,128)(2,1)}) %tuple.126, (s32[]{:T(128)}, bf16[2,2048,256]{1,2,0:T(8,128)(2,1)}, s32[2,256]{1,0:T(2,128)}, ...), branch_computations={%region_21.21_spmd, %region_22.22_spmd} | conditional | flops 1024066304 | bytes 39756988 | solution.py:990
  733.4 3.7 copy.405
  737.1 4.3 copy.360
  741.3 43.9 %scatter_sum.2 = f32[512,256]{1,0:T(8,128)} custom-call(bf16[4,2,512,256]{3,2,1,0:T(8,128)(2,1)} %bitcast.316), custom_call_target="tpu_custom_call" | custom-call | tf_op jit(solution)/shard_map/scatter_sum/pallas_call | solution.py:281
  793.9 4.3 fusion.48
  799.7 2.9 convolution_convert_fusion.2
  803.5 4.8 concatenate.50.in_ref
  808.3 17.6 %scatter_sum.3 = f32[192,768]{1,0:T(8,128)} custom-call(bf16[4,2,192,768]{3,2,1,0:T(8,128)(2,1)} %concatenate.50.in_ref), custom_call_target="tpu_custom_call" | custom-call | tf_op jit(solution)/shard_map/scatter_sum/pallas_call | solution.py:281
  825.9 14.6 %line_exchange.11 = f32[4,48,768]{2,1,0:T(8,128)} custom-call(f32[4,48,768]{2,1,0:T(8,128)} %bitcast.334), custom_call_target="tpu_custom_call" | custom-call | tf_op jit(solution)/shard_map/line_exchange/pallas_call | solution.py:332
  844.1 30.7 %line_exchange.10 = bf16[4,128,1536]{2,1,0:T(8,128)(2,1)} custom-call(bf16[4,128,1536]{2,1,0:T(8,128)(2,1)} %bitcast.336), custom_call_target="tpu_custom_call" | custom-call | tf_op jit(solution)/shard_map/line_exchange/pallas_call | solution.py:332
  (299 shorter events, 120.8 us)
Async XLA Ops:
  7.2 246.0 %all-gather.3.cloned.1.call-start = ((), (), s32[]{:S(2)}) async-start(), calls=%async_computation.2 | async-start | bytes 4866048 | tf_op jit(solution)/shard_map/all_gather | solution.py:912
  7.9 253.1 %all-gather.5.cloned.1.call-start = ((), (), s32[]{:S(2)}) async-start(), calls=%async_computation.3 | async-start | bytes 6684672 | tf_op jit(solution)/shard_map/all_gather | solution.py:909
  8.7 592.7 %reduce-scatter.3.cloned.1.call-start = ((), (), s32[]{:S(2)}) async-start(), calls=%async_computation.4 | async-start | bytes 6684672 | tf_op jit(solution)/shard_map/reduce_scatter | solution.py:1073
  31.1 10.6 %copy-start.22 = (bf16[48,2560]{1,0:T(8,128)(2,1)S(1)}, bf16[48,2560]{1,0:T(8,128)(2,1)}, u32[]{:S(2)}) copy-start(bf16[48,2560]{1,0:T(8,128)(2,1)} %param.24) | copy-start | bytes 737284
  31.1 10.7 %copy-start.39 = (bf16[48,40]{0,1:T(8,128)(2,1)S(1)}, bf16[48,40]{0,1:T(8,128)(2,1)}, u32[]{:S(2)}) copy-start(bf16[48,40]{0,1:T(8,128)(2,1)} %param.26) | copy-start | bytes 11524
  31.1 10.7 %copy-start.50 = (bf16[48]{0:T(256)(128)(2,1)S(1)}, bf16[48]{0:T(256)(128)(2,1)}, u32[]{:S(2)}) copy-start(bf16[48]{0:T(256)(128)(2,1)} %param.28) | copy-start | bytes 292
  31.1 10.7 %copy-start.51 = (bf16[48]{0:T(256)(128)(2,1)S(1)}, bf16[48]{0:T(256)(128)(2,1)}, u32[]{:S(2)}) copy-start(bf16[48]{0:T(256)(128)(2,1)} %param.27) | copy-start | bytes 292
  31.1 208.3 %collective-permute-start = (bf16[2,192,1280]{2,1,0:T(8,128)(2,1)}, bf16[2,192,1280]{2,1,0:T(8,128)(2,1)}, u32[]{:S(2)}, u32[]{:S(2)}) collective-permute-start(bf16[2,192,1280]{2,1,0:T(8,128)(2,1)} %bitcast.346), channel_id=1, source_target_pairs={{0,4},{4,0},{1,5},{5,1},{2,6},{6,2},{3,7},{7,3},{8,12},{12,8},{9,1... | collective-permute-start | bytes 2949128 | tf_op jit(solution)/shard_map/ppermute | solution.py:851
  34.0 204.7 %collective-permute-start.1 = (bf16[2,192,1280]{2,1,0:T(8,128)(2,1)}, bf16[2,192,1280]{2,1,0:T(8,128)(2,1)}, u32[]{:S(2)}, u32[]{:S(2)}) collective-permute-start(bf16[2,192,1280]{2,1,0:T(8,128)(2,1)} %bitcast.349), channel_id=1, source_target_pairs={{0,8},{8,0},{16,24},{24,16},{1,9},{9,1},{17,25},{25,17},{2,10},{10... | collective-permute-start | bytes 2949128 | tf_op jit(solution)/shard_map/ppermute | solution.py:847
  38.9 199.9 %collective-permute-start.3 = (bf16[2,192,1280]{2,1,0:T(8,128)(2,1)}, bf16[2,192,1280]{2,1,0:T(8,128)(2,1)}, u32[]{:S(2)}, u32[]{:S(2)}) collective-permute-start(bf16[2,192,1280]{2,1,0:T(8,128)(2,1)} %bitcast.348), channel_id=1, source_target_pairs={{0,16},{8,24},{16,0},{24,8},{1,17},{9,25},{17,1},{25,9},{2,18},{10... | collective-permute-start | bytes 2949128 | tf_op jit(solution)/shard_map/ppermute | solution.py:847
  41.8 197.6 %collective-permute-start.5 = (bf16[2,192,1280]{2,1,0:T(8,128)(2,1)}, bf16[2,192,1280]{2,1,0:T(8,128)(2,1)}, u32[]{:S(2)}, u32[]{:S(2)}) collective-permute-start(bf16[2,192,1280]{2,1,0:T(8,128)(2,1)} %bitcast.347), channel_id=1, source_target_pairs={{0,24},{8,16},{16,8},{24,0},{1,25},{9,17},{17,9},{25,1},{2,26},{10... | collective-permute-start | bytes 2949128 | tf_op jit(solution)/shard_map/ppermute | solution.py:847
  41.8 203.3 %collective-permute-start.7 = (bf16[10,64,1536]{2,1,0:T(8,128)(2,1)}, bf16[10,64,1536]{2,1,0:T(8,128)(2,1)}, u32[]{:S(2)}, u32[]{:S(2)}) collective-permute-start(bf16[10,64,1536]{2,1,0:T(8,128)(2,1)} %param.30), channel_id=1, source_target_pairs={{0,4},{4,0},{1,5},{5,1},{2,6},{6,2},{3,7},{7,3},{8,12},{12,8},{9,1... | collective-permute-start | bytes 5898248 | tf_op jit(solution)/shard_map/ppermute | solution.py:851
  150.1 106.4 %copy-start.23 = (f32[1536]{0:T(1024)}, f32[1536]{0:T(1024)S(1)}, u32[]{:S(2)}) copy-start(f32[1536]{0:T(1024)S(1)} %get-tuple-element.731) | copy-start | bytes 18436
  150.1 309.0 %copy-start.28 = (f32[1536]{0:T(1024)}, f32[1536]{0:T(1024)S(1)}, u32[]{:S(2)}) copy-start(f32[1536]{0:T(1024)S(1)} %get-tuple-element.732) | copy-start | bytes 18436
  156.2 5.0 copy-start.32
  193.6 42.3 %copy-start.20 = (s32[2,256]{1,0:T(2,128)}, s32[2,256]{1,0:T(2,128)S(1)}, u32[]{:S(2)}) copy-start(s32[2,256]{1,0:T(2,128)S(1)} %get-tuple-element.1074) | copy-start | bytes 6148
  193.7 44.6 %copy-start = (bf16[2,2048,256]{1,2,0:T(8,128)(2,1)}, bf16[2,2048,256]{1,2,0:T(8,128)(2,1)S(1)}, u32[]{:S(2)}) copy-start(bf16[2,2048,256]{1,2,0:T(8,128)(2,1)S(1)} %get-tuple-element.1054) | copy-start | bytes 6291460
  193.7 44.6 %copy-start.6 = (f32[2,2,3,256,64]{3,4,2,1,0:T(8,128)}, f32[2,2,3,256,64]{3,4,2,1,0:T(8,128)S(1)}, u32[]{:S(2)}) copy-start(f32[2,2,3,256,64]{3,4,2,1,0:T(8,128)S(1)} %get-tuple-element.624) | copy-start | bytes 2359300
  193.7 42.3 %copy-start.43 = (s32[2,64,8]{1,2,0:T(8,128)S(1)}, s32[2,64,8]{1,2,0:T(8,128)}, u32[]{:S(2)}) copy-start(s32[2,64,8]{1,2,0:T(8,128)} %param.23) | copy-start | bytes 12292
  235.9 23.4 %copy-start.30 = (s32[128,8]{0,1:T(8,128)}, s32[128,8]{0,1:T(8,128)S(1)}, u32[]{:S(2)}) copy-start(s32[128,8]{0,1:T(8,128)S(1)} %eq.67) | copy-start | bytes 12292
  237.4 21.4 %copy-start.35 = (pred[128,8]{0,1:T(8,128)(4,1)}, pred[128,8]{0,1:T(8,128)(4,1)S(1)}, u32[]{:S(2)}) copy-start(pred[128,8]{0,1:T(8,128)(4,1)S(1)} %copy.337) | copy-start | bytes 3076
  238.8 3.3 collective-permute-start.2
  238.8 4.7 collective-permute-start.4
  239.3 5.6 collective-permute-start.6
  256.4 198.0 %copy-start.40 = (f32[128]{0:T(128)}, f32[128]{0:T(128)S(1)}, u32[]{:S(2)}) copy-start(f32[128]{0:T(128)S(1)} %add_rsqrt_fusion.2) | copy-start | bytes 1540
  454.4 424.3 %reduce-scatter.5.cloned.1.call-start = ((), (), s32[]{:S(2)}) async-start(), calls=%async_computation.5 | async-start | bytes 4866048 | tf_op jit(solution)/shard_map/reduce_scatter | solution.py:1112
  454.5 4.6 copy-start.3
  459.0 6.0 copy-start.2
  459.0 6.0 copy-start.24
  459.0 6.0 copy-start.41
  459.0 17.5 %collective-permute-start.8 = (bf16[2,4,192,1280]{3,2,1,0:T(8,128)(2,1)}, bf16[2,4,192,1280]{3,2,1,0:T(8,128)(2,1)}, u32[]{:S(2)}, u32[]{:S(2)}) collective-permute-start(bf16[2,4,192,1280]{3,2,1,0:T(8,128)(2,1)} %fusion.44), channel_id=1, source_target_pairs={{0,4},{4,0},{1,5},{5,1},{2,6},{6,2},{3,7},{7,3},{8,12},{12,8},{9,1... | collective-permute-start | bytes 11796488 | tf_op jit(solution)/shard_map/ppermute | solution.py:851
  465.4 4.5 copy-start.27
  465.4 6.3 copy-start.25
  465.4 6.3 copy-start.42
  468.4 146.8 %collective-permute-start.12 = (bf16[10,64,1536]{2,1,0:T(8,128)(2,1)}, bf16[10,64,1536]{2,1,0:T(8,128)(2,1)}, u32[]{:S(2)}, u32[]{:S(2)}) collective-permute-start(bf16[10,64,1536]{2,1,0:T(8,128)(2,1)} %dynamic-slice_bitcast_fusion), channel_id=1, source_target_pairs={{0,4},{4,0},{1,5},{5,1},{2,6},{6,2},{3,7},{7,3},{8,12},{12,8},{9,1... | collective-permute-start | bytes 5898248 | tf_op jit(solution)/shard_map/ppermute | solution.py:851
  607.5 7.8 copy-start.13
  611.7 25.0 %collective-permute-start.9 = (bf16[2,192,1280]{2,1,0:T(8,128)(2,1)}, bf16[2,192,1280]{2,1,0:T(8,128)(2,1)}, u32[]{:S(2)}, u32[]{:S(2)}) collective-permute-start(bf16[2,192,1280]{2,1,0:T(8,128)(2,1)} %get-tuple-element.793), channel_id=1, source_target_pairs={{0,8},{8,0},{16,24},{24,16},{1,9},{9,1},{17,25},{25,17},{2,10},{10... | collective-permute-start | bytes 2949128 | tf_op jit(solution)/shard_map/ppermute | solution.py:847
  613.1 43.3 %collective-permute-start.10 = (bf16[2,192,1280]{2,1,0:T(8,128)(2,1)}, bf16[2,192,1280]{2,1,0:T(8,128)(2,1)}, u32[]{:S(2)}, u32[]{:S(2)}) collective-permute-start(bf16[2,192,1280]{2,1,0:T(8,128)(2,1)} %get-tuple-element.792), channel_id=1, source_target_pairs={{0,16},{8,24},{16,0},{24,8},{1,17},{9,25},{17,1},{25,9},{2,18},{10... | collective-permute-start | bytes 2949128 | tf_op jit(solution)/shard_map/ppermute | solution.py:847
  614.3 44.4 %collective-permute-start.11 = (bf16[2,192,1280]{2,1,0:T(8,128)(2,1)}, bf16[2,192,1280]{2,1,0:T(8,128)(2,1)}, u32[]{:S(2)}, u32[]{:S(2)}) collective-permute-start(bf16[2,192,1280]{2,1,0:T(8,128)(2,1)} %get-tuple-element.791), channel_id=1, source_target_pairs={{0,24},{8,16},{16,8},{24,0},{1,25},{9,17},{17,9},{25,1},{2,26},{10... | collective-permute-start | bytes 2949128 | tf_op jit(solution)/shard_map/ppermute | solution.py:847
  661.1 5.0 copy-start.10
  697.2 23.1 %copy-start.7 = (f32[2,2,3,256,64]{3,4,2,1,0:T(8,128)S(1)}, f32[2,2,3,256,64]{3,4,2,1,0:T(8,128)}, u32[]{:S(2)}) copy-start(f32[2,2,3,256,64]{3,4,2,1,0:T(8,128)} %copy-done.6) | copy-start | bytes 2359300
  788.6 5.3 copy-start.48
  798.2 5.2 copy-start.15
  798.2 5.2 copy-start.16
  840.5 36.0 %copy-start.5 = (bf16[2,64,1536]{2,1,0:T(8,128)(2,1)S(1)}, bf16[2,64,1536]{2,1,0:T(8,128)(2,1)}, u32[]{:S(2)}) copy-start(bf16[2,64,1536]{2,1,0:T(8,128)(2,1)} %param.20) | copy-start | bytes 1179652
  840.5 36.0 %copy-start.29 = (f32[1536]{0:T(1024)S(1)}, f32[1536]{0:T(1024)}, u32[]{:S(2)}) copy-start(f32[1536]{0:T(1024)} %copy-done.28) | copy-start | bytes 18436
  840.5 36.0 %copy-start.47 = (f32[2,64]{1,0:T(2,128)S(1)}, f32[2,64]{1,0:T(2,128)}, u32[]{:S(2)}) copy-start(f32[2,64]{1,0:T(2,128)} %copy-done.46) | copy-start | bytes 1540
  841.6 35.9 %copy-start.49 = (f32[128]{0:T(128)S(1)}, f32[128]{0:T(128)}, u32[]{:S(2)}) copy-start(f32[128]{0:T(128)} %rsqrt.40) | copy-start | bytes 1540
  (21 other events, 52.0 us)
Sparse Core Ops, SparseCore 0:
  10.8 99.0 all-gather.2
  112.7 111.6 all-gather.4
  454.6 146.7 reduce-scatter.2
  607.6 107.0 reduce-scatter.4

commit v3 on v2

--- a/solution.py
+++ b/solution.py
@@ -504,14 +504,20 @@
     )(x, c, w_gate, w_up, w_down)
 
 
-def turn_kernel(cube, heads, tile, hidden, own_ref, c_hbm, gate_hbm, up_hbm, down_hbm, out_ref, moe_hbm, d_gate_hbm, d_up_hbm, d_down_hbm, *refs):
+def turn_kernel(cube, heads, hidden, *refs):
     chips, count = cube.chips, cube.number
-    tokens, turned, cots, w_gate, w_up, w_down, acts, back_gate, back_up, d_gates, moe_stage, line_in = refs[:12]
-    arrived = refs[12 : 12 + count]
-    load, store, own_sem, line_send, line_recv, send, recv, back_send, back_recv, end_send, end_recv = refs[12 + count :]
+    own_ref, c_hbm, up_hbm, down_hbm = refs[:4]
+    out_ref, moe_hbm, keep_up_hbm, other_up_hbm, keep_down_hbm, other_down_hbm = refs[4:10]
+    tokens, turned, cots, w_up, w_down, acts, backs, d_gates, moe_stage, line_in = refs[10:20]
+    arrived = refs[20 : 20 + count]
+    load, store, own_sem, line_send, line_recv, send, recv, back_send, back_recv = refs[
+        20 + count : 29 + count
+    ]
+    end_send, end_recv, twin_send, twin_recv = refs[29 + count :]
     hz = lax.axis_index("head")
     rows, columns = own_ref.shape
-    width, total = w_gate.shape
+    experts_here, width, _ = w_up.shape
+    total = experts_here * hidden
     half = rows // 2
     line = heads * rows
     others = near(heads)
@@ -520,35 +526,72 @@
     loads = [
         pltpu.make_async_copy(source, target, load.at[index])
         for index, (source, target) in enumerate(
-            ((gate_hbm, w_gate), (up_hbm, w_up), (down_hbm, w_down), (c_hbm, cots))
+            ((up_hbm, w_up), (down_hbm, w_down), (c_hbm, cots))
         )
     ]
     for copy in loads:
         copy.start()
-    meet([cube.peer(digit) for digit in range(count)] + [{"head": (hz + d) % heads} for d in others])
+    core = lax.axis_index("core")
+    twin = {"core": 1 - core}
+    meet(
+        [cube.peer(digit) for digit in range(count)]
+        + [{"head": (hz + d) % heads} for d in others]
+        + [twin]
+    )
 
     def part(side):
         return pl.ds(side * half, half)
 
-    def line_copy(d):
+    middle = jnp.minimum(hz, heads - 1 - hz)
+
+    def source(rank):
+        if rank == 0:
+            return hz
+        far = (rank + 1) // 2
+        near_one = hz - far if rank % 2 else hz + far
+        far_one = jnp.where(
+            hz < heads - 1 - hz, hz + (rank - middle), hz - (rank - middle)
+        )
+        return jnp.where(rank <= 2 * middle, near_one, far_one)
+
+    def line_copy(rank, step):
+        head = source(rank)
+        place = tokens.at[cube.place(0) + (head,)]
         return pltpu.make_async_remote_copy(
-            src_ref=own_ref,
-            dst_ref=tokens.at[cube.place(0) + (hz,)],
-            send_sem=line_send.at[d - 1],
-            recv_sem=line_recv.at[d - 1],
-            device_id={"head": (hz + d) % heads},
+            src_ref=own_ref if rank == 0 else place,
+            dst_ref=place,
+            send_sem=line_send.at[heads if rank == 0 and step < 0 else head],
+            recv_sem=line_recv.at[head],
+            device_id={"head": (hz + step + heads) % heads},
             device_id_type=MESH,
         )
 
-    def plane_copy(side, mask, k, d):
+    def along(rank, act):
+        head = source(rank)
+        goes_up = hz + 1 < heads
+        goes_down = hz > 0
+        if rank:
+            goes_up = goes_up & (head < hz)
+            goes_down = goes_down & (head > hz)
+
+        @pl.when(goes_up)
+        def _():
+            act(line_copy(rank, 1))
+
+        @pl.when(goes_down)
+        def _():
+            act(line_copy(rank, -1))
+
+    def plane_copy(side, mask, k, rank):
         digit = cube.gather_orders[side][k]
         later = mask | (1 << digit)
-        place = tokens.at[cube.place(mask) + ((hz + heads - d) % heads, part(side))]
+        head = source(rank)
+        place = tokens.at[cube.place(mask) + (head, part(side))]
         return pltpu.make_async_remote_copy(
-            src_ref=own_ref.at[part(side)] if mask == 0 and d == 0 else place,
+            src_ref=own_ref.at[part(side)] if mask == 0 and rank == 0 else place,
             dst_ref=place,
-            send_sem=send.at[side, later, d],
-            recv_sem=recv.at[side, later, d],
+            send_sem=send.at[side, later, head],
+            recv_sem=recv.at[side, later, head],
             device_id=cube.peer(digit),
             device_id_type=MESH,
         )
@@ -558,26 +601,30 @@
         last = max([k for k in range(count) if (mask >> order[k]) & 1], default=-1)
         return range(last + 1, count)
 
-    def arrival(side, mask, d):
+    def arrival(side, mask, rank):
         order = cube.gather_orders[side]
         k = max(k for k in range(count) if (mask >> order[k]) & 1)
-        return plane_copy(side, mask & ~(1 << order[k]), k, d)
+        return plane_copy(side, mask & ~(1 << order[k]), k, rank)
 
     def receive(mask):
-        for d in [0] + others:
-            if mask == 0 and d:
-                line_copy(d).wait_recv()
+        for rank in range(heads):
+            if mask == 0:
+                if rank:
+                    line_copy(rank, 1).wait_recv()
+                along(rank, lambda copy: copy.start())
             for side in range(2):
                 if mask:
-                    arrival(side, mask, d).wait_recv()
+                    arrival(side, mask, rank).wait_recv()
                 for k in steps_after(side, mask):
-                    plane_copy(side, mask, k, d).start()
+                    plane_copy(side, mask, k, rank).start()
 
     def sent(mask):
-        for d in [0] + others:
+        for rank in range(heads):
+            if mask == 0:
+                along(rank, lambda copy: copy.wait_send())
             for side in range(2):
                 for k in steps_after(side, mask):
-                    plane_copy(side, mask, k, d).wait_send()
+                    plane_copy(side, mask, k, rank).wait_send()
 
     def slot(side, k, mask):
         return subsets(cube.scatter_orders[side][k + 1 :]).index(mask)
@@ -609,23 +656,19 @@
 
     outward = others[::-1] + [0]
 
-    def give(mask):
-        for d in outward:
-            for side in range(2):
-                first = 1 << cube.scatter_orders[side][0]
-                if mask & first:
-                    back_copy(side, 0, mask & ~first, d).start()
+    def give(mask, d):
+        for side in range(2):
+            first = 1 << cube.scatter_orders[side][0]
+            if mask & first:
+                back_copy(side, 0, mask & ~first, d).start()
 
     own = pltpu.make_async_copy(own_ref, tokens.at[cube.place(0) + (hz,)], own_sem)
     own.start()
-    for d in others:
-        line_copy(d).start()
-    for copy in loads:
-        copy.wait()
-    own.wait()
-
-    first_expert = hz * (total // hidden)
+
+    first_expert = hz * experts_here
     span = min(512, width)
+    group = 2 if experts_here % 2 == 0 else 1
+    tile = group * hidden
 
     def compute(place):
         here = pl.ds(place * line, line)
@@ -644,8 +687,11 @@
             high = (lane == expert).astype(f32)
             both = (high + (lane == expert + LOW).astype(f32)).astype(bf16)
             weight = jnp.dot(routed, both, preferred_element_type=f32)
-            gate = jnp.dot(x, w_gate[:, js], preferred_element_type=f32)
-            up = jnp.dot(x, w_up[:, js], preferred_element_type=f32)
+            both_parts = [
+                jnp.dot(x, w_up[j * group + i], preferred_element_type=f32) for i in range(group)
+            ]
+            gate = jnp.concatenate([value[:, :hidden] for value in both_parts], axis=1)
+            up = jnp.concatenate([value[:, hidden:] for value in both_parts], axis=1)
             d_act = lax.dot_general(c, w_down[js, :], NT, preferred_element_type=f32)
             sigma = 1.0 / (1.0 + jnp.exp(-gate))
             silu = gate * sigma
@@ -655,8 +701,12 @@
             )
             acts[here, js] = (act * weight).astype(bf16)
             d_act = d_act * weight
-            back_up[here, js] = (d_act * silu).astype(bf16)
-            back_gate[here, js] = (d_act * up * sigma * (1.0 + gate * (1.0 - sigma))).astype(bf16)
+            d_up = (d_act * silu).astype(bf16)
+            d_gate = (d_act * up * sigma * (1.0 + gate * (1.0 - sigma))).astype(bf16)
+            for i in range(group):
+                one = slice(i * hidden, (i + 1) * hidden)
+                backs[j * group + i, here, pl.ds(0, hidden)] = d_gate[:, one]
+                backs[j * group + i, here, pl.ds(hidden, hidden)] = d_up[:, one]
 
     def results(place, step):
         here = pl.ds(place * line, line)
@@ -664,9 +714,12 @@
         @pl.loop(0, width // span)
         def _(j):
             cs = pl.ds(pl.multiple_of(j * span, span), span)
-            value = lax.dot_general(
-                back_gate[here, :], w_gate[cs, :], NT, preferred_element_type=f32
-            ) + lax.dot_general(back_up[here, :], w_up[cs, :], NT, preferred_element_type=f32)
+            value = sum(
+                lax.dot_general(
+                    backs[e, here, :], w_up[e, cs, :], NT, preferred_element_type=f32
+                )
+                for e in range(experts_here)
+            )
             tokens[place, :, :, cs] = value.astype(bf16).reshape(heads, rows, span)
 
         tokens[place, :, :, pl.ds(width, LANES)] = (
@@ -675,7 +728,7 @@
 
     def moe_copy(place):
         return pltpu.make_async_copy(
-            moe_stage, moe_hbm.at[pl.ds(place * line, line)], store.at[3]
+            moe_stage, moe_hbm.at[pl.ds(place * line, line)], store.at[chips + 1]
         )
 
     def mixed(place, step):
@@ -711,6 +764,13 @@
         place = cube.place(0)[0] * 0
         for index, mask in enumerate(masks):
             place = jnp.where(step == index, cube.place(mask)[0], place)
+
+        @pl.when(step == 0)
+        def _():
+            own.wait()
+            for copy in loads:
+                copy.wait()
+
         compute(place)
         for index, mask in enumerate(masks):
 
@@ -720,13 +780,18 @@
 
         results(place, step)
         for index, mask in enumerate(masks):
-            if mask:
+            if mask and mask != chips - 1:
 
                 @pl.when(step == index)
                 def _():
-                    give(mask)
-
-        mixed(place, step)
+                    for d in outward:
+                        give(mask, d)
+
+        for index, mask in enumerate(masks[:-1]):
+
+            @pl.when(step == index)
+            def _():
+                mixed(place, step)
 
     def sums(side, steps, mask, d):
         value = back_place(side, mask, d)[...].astype(f32)
@@ -735,116 +800,596 @@
             value = value + arrived[j][side, slot(side, j, mask), d].astype(f32)
         return value
 
-    def weights_grad(left, right, target, hbm, index, by_rows):
+    slices = 2 * chips
+    slice_rows = width // slices
+
+    def up_rows(ref, chip, which):
+        return ref.at[:, pl.ds((chip * 2 + which) * slice_rows, slice_rows), :]
+
+    def keep_up(chip):
+        return pltpu.make_async_copy(up_rows(w_up, chip, core), keep_up_hbm.at[chip], store.at[chip])
+
+    def give_up(chip):
+        return pltpu.make_async_remote_copy(
+            src_ref=up_rows(w_up, chip, 1 - core),
+            dst_ref=other_up_hbm.at[chip],
+            send_sem=twin_send.at[chip],
+            recv_sem=twin_recv.at[chip],
+            device_id=twin,
+            device_id_type=MESH,
+        )
+
+    def keep_down():
+        return pltpu.make_async_copy(w_down_parts(core), keep_down_hbm, store.at[chips])
+
+    def give_down():
+        return pltpu.make_async_remote_copy(
+            src_ref=w_down_parts(1 - core),
+            dst_ref=other_down_hbm,
+            send_sem=twin_send.at[chips],
+            recv_sem=twin_recv.at[chips],
+            device_id=twin,
+            device_id_type=MESH,
+        )
+
+    def w_down_parts(which):
+        return w_down.reshape(experts_here, 2, hidden // 2, width).at[:, which]
+
+    def up_grad(begin, end):
+        @pl.loop(begin, end)
+        def _(e):
+            w_up[e] = jnp.dot(turned[...], backs[e], preferred_element_type=f32).astype(bf16)
+
+        if end == experts_here:
+            for chip in range(chips):
+                give_up(chip).start()
+                keep_up(chip).start()
+
+    def down_grad():
         @pl.loop(0, total // tile)
         def _(j):
             js = pl.ds(pl.multiple_of(j * tile, tile), tile)
-            if by_rows:
-                value = jnp.dot(left[:, js].T, right[...], preferred_element_type=f32)
-                target[js, :] = value.astype(bf16)
-            else:
-                value = jnp.dot(left[...], right[:, js], preferred_element_type=f32)
-                target[:, js] = value.astype(bf16)
-
-        pltpu.make_async_copy(target, hbm, store.at[index]).start()
-
-    weights_grad(turned, back_gate, w_gate, d_gate_hbm, 0, False)
-    for k in range(1, count):
-        for d in outward:
+            value = jnp.dot(acts[:, js].T, cots[...], preferred_element_type=f32)
+            w_down[js, :] = value.astype(bf16)
+
+        give_down().start()
+        keep_down().start()
+
+    def last_mix():
+        mixed(cube.place(chips - 1)[0], 1)
+
+    cuts = [experts_here * i // 4 for i in range(5)]
+    work = [
+        last_mix,
+        lambda: up_grad(cuts[0], cuts[1]),
+        lambda: up_grad(cuts[1], cuts[2]),
+        lambda: up_grad(cuts[2], cuts[3]),
+        lambda: up_grad(cuts[3], cuts[4]),
+        down_grad,
+    ]
+    turns = heads + count
+    for turn in range(turns):
+        if turn < heads:
+            give(chips - 1, outward[turn])
+        for piece in work[len(work) * turn // turns : len(work) * (turn + 1) // turns]:
+            piece()
+        for k in range(1, count):
+            if 0 <= turn - k < heads:
+                d = outward[turn - k]
+                for side in range(2):
+                    order = cube.scatter_orders[side]
+                    for mask in subsets(order[k + 1 :])[::-1]:
+                        full = mask | (1 << order[k])
+                        back_place(side, full, d)[...] = sums(side, k, full, d).astype(bf16)
+                        back_copy(side, k, mask, d).start()
+        if 0 <= turn - count < heads:
+            d = outward[turn - count]
             for side in range(2):
-                order = cube.scatter_orders[side]
-                for mask in subsets(order[k + 1 :])[::-1]:
-                    full = mask | (1 << order[k])
-                    back_place(side, full, d)[...] = sums(side, k, full, d).astype(bf16)
-                    back_copy(side, k, mask, d).start()
-    weights_grad(turned, back_up, w_up, d_up_hbm, 1, False)
-    for d in outward:
-        for side in range(2):
-            value = sums(side, count, 0, d)
+                value = sums(side, count, 0, d)
+                if d:
+                    back_place(side, 0, d)[...] = value.astype(bf16)
+                else:
+                    out_ref[part(side)] = value
             if d:
-                back_place(side, 0, d)[...] = value.astype(bf16)
-            else:
-                out_ref[part(side)] = value
-        if d:
-            end_copy(d).start()
-    moe_copy(0).wait()
-    weights_grad(acts, cots, w_down, d_down_hbm, 2, True)
+                end_copy(d).start()
     for d in others:
         end_copy(d).wait_recv()
         out_ref[...] += line_in[d - 1].astype(f32)
     for d in others:
-        line_copy(d).wait_send()
         end_copy(d).wait_send()
     for side in range(2):
         for k in range(count):
             for mask in subsets(cube.scatter_orders[side][k + 1 :]):
                 for d in outward:
                     back_copy(side, k, mask, d).wait_send()
-    for index, (source, hbm) in enumerate(
-        ((w_gate, d_gate_hbm), (w_up, d_up_hbm), (w_down, d_down_hbm))
-    ):
-        pltpu.make_async_copy(source, hbm, store.at[index]).wait()
-
-
-def expert_turn(payload, c, w_gate, w_up, w_down, hidden, chips, heads, number):
+    moe_copy(0).wait()
+    for chip in range(chips):
+        give_up(chip).wait()
+        keep_up(chip).wait()
+    give_down().wait()
+    keep_down().wait()
+
+
+def expert_turn(payload, c, w_up, w_down, chips, heads, number):
     rows, columns = payload.shape
-    width, total = w_gate.shape
+    experts_here, width, double = w_up.shape
+    hidden = double // 2
+    total = experts_here * hidden
     cube = Cube(chips, False)
     count = cube.number
     tokens = chips * heads * rows
     half = rows // 2
-    tile = 256 if total % 256 == 0 else hidden
     slots = [chips >> (k + 1) for k in range(count)]
+    share = jax.ShapeDtypeStruct((chips, experts_here, width // (2 * chips), double), bf16)
+    down_share = jax.ShapeDtypeStruct((experts_here, hidden // 2, width), bf16)
     return pl.pallas_call(
-        functools.partial(turn_kernel, cube, heads, tile, hidden),
+        functools.partial(turn_kernel, cube, heads, hidden),
         out_shape=(
             jax.ShapeDtypeStruct((rows, columns), f32),
             jax.ShapeDtypeStruct((tokens, width), bf16),
-            jax.ShapeDtypeStruct((width, total), bf16),
-            jax.ShapeDtypeStruct((width, total), bf16),
-            jax.ShapeDtypeStruct((total, width), bf16),
+            share,
+            share,
+            down_share,
+            down_share,
         ),
-        in_specs=[WHOLE, ANY, ANY, ANY, ANY],
-        out_specs=(WHOLE, ANY, ANY, ANY, ANY),
+        in_specs=[WHOLE, ANY, ANY, ANY],
+        out_specs=(WHOLE, ANY, ANY, ANY, ANY, ANY),
         scratch_shapes=[
             pltpu.VMEM((chips, heads, rows, columns), bf16),
             pltpu.VMEM((width, tokens), bf16),
             pltpu.VMEM((tokens, width), bf16),
-            pltpu.VMEM((width, total), bf16),
-            pltpu.VMEM((width, total), bf16),
+            pltpu.VMEM((experts_here, width, double), bf16),
             pltpu.VMEM((total, width), bf16),
             pltpu.VMEM((tokens, total), bf16),
-            pltpu.VMEM((tokens, total), bf16),
-            pltpu.VMEM((tokens, total), bf16),
+            pltpu.VMEM((experts_here, tokens, double), bf16),
             pltpu.VMEM((heads * rows, LANES), f32),
             pltpu.VMEM((heads * rows, width), bf16),
             pltpu.VMEM((heads - 1, rows, columns), bf16),
         ]
         + [pltpu.VMEM((2, s, heads, half, columns), bf16) for s in slots]
         + [
-            DMA((4,)),
-            DMA((4,)),
+            DMA((3,)),
+            DMA((chips + 2,)),
             DMA,
-            DMA((heads - 1,)),
-            DMA((heads - 1,)),
+            DMA((heads + 1,)),
+            DMA((heads,)),
             DMA((2, chips, heads)),
             DMA((2, chips, heads)),
             DMA((2, count, slots[0], heads)),
             DMA((2, count, slots[0], heads)),
             DMA((heads - 1,)),
             DMA((heads - 1,)),
+            DMA((chips + 1,)),
+            DMA((chips + 1,)),
         ],
         compiler_params=pltpu.CompilerParams(
             collective_id=number, has_side_effects=True, vmem_limit_bytes=63 << 20
         ),
         name="expert_turn",
-    )(payload, c, w_gate, w_up, w_down)
+    )(payload, c, w_up, w_down)
+
+
+def start_kernel(cube, heads, hidden, *refs):
+    x_ref, slice_ref, up_ref, down_ref, x_out, dense_out, up_out, down_out = refs[:8]
+    local, x_send, x_recv, line_send, line_recv, send, recv = refs[8:15]
+    up_send, up_recv, twin_send, twin_recv = refs[15:]
+    chips = cube.chips
+    chip, core, hz = lax.axis_index("chip"), lax.axis_index("core"), lax.axis_index("head")
+    twin = {"core": 1 - core}
+    others = near(heads)
+    slice_rows = up_ref.shape[1]
+    units = up_ref.shape[2] // 2
+    part_heads = heads // 2
+    meet(
+        [{"chip": flip(chip, mask)} for mask in range(1, chips)]
+        + [twin]
+        + [{"head": (hz + d) % heads} for d in others]
+    )
+    middle = jnp.minimum(hz, heads - 1 - hz)
+
+    def source(rank):
+        if rank == 0:
+            return hz
+        far = (rank + 1) // 2
+        near_one = hz - far if rank % 2 else hz + far
+        far_one = jnp.where(hz < heads - 1 - hz, hz + (rank - middle), hz - (rank - middle))
+        return jnp.where(rank <= 2 * middle, near_one, far_one)
+
+    def x_copy(rank, step):
+        head = source(rank)
+        return pltpu.make_async_remote_copy(
+            src_ref=x_ref if rank == 0 else x_out.at[head],
+            dst_ref=x_out.at[head],
+            send_sem=x_send.at[heads if rank == 0 and step < 0 else head],
+            recv_sem=x_recv.at[head],
+            device_id={"head": (hz + step + heads) % heads},
+            device_id_type=MESH,
+        )
+
+    def along(rank, act):
+        head = source(rank)
+        goes_up = hz + 1 < heads
+        goes_down = hz > 0
+        if rank:
+            goes_up = goes_up & (head < hz)
+            goes_down = goes_down & (head > hz)
+
+        @pl.when(goes_up)
+        def _():
+            act(x_copy(rank, 1))
+
+        @pl.when(goes_down)
+        def _():
+            act(x_copy(rank, -1))
+
+    def slice_copy(d):
+        place = (hz + d) % heads
+        return pltpu.make_async_remote_copy(
+            src_ref=slice_ref.at[place],
+            dst_ref=dense_out.at[chip, core, hz],
+            send_sem=line_send.at[d - 1],
+            recv_sem=line_recv.at[d - 1],
+            device_id={"head": place},
+            device_id_type=MESH,
+        )
+
+    def dense_copy(side, mask, k):
+        order = cube.gather_orders[side]
+        later = mask | (1 << order[k])
+        place = dense_out.at[cube.place(mask) + (pl.ds(side * part_heads, part_heads),)]
+        return pltpu.make_async_remote_copy(
+            src_ref=place,
+            dst_ref=place,
+            send_sem=send.at[side, later],
+            recv_sem=recv.at[side, later],
+            device_id=cube.peer(order[k]),
+            device_id_type=MESH,
+        )
+
+    def steps_after(side, mask):
+        order = cube.gather_orders[side]
+        last = max([k for k in range(cube.number) if (mask >> order[k]) & 1], default=-1)
+        return range(last + 1, cube.number)
+
+    def dense_turn(mask):
+        for side in range(2):
+            if mask:
+                order = cube.gather_orders[side]
+                k = max(k for k in range(cube.number) if (mask >> order[k]) & 1)
+                dense_copy(side, mask & ~(1 << order[k]), k).wait_recv()
+            for k in steps_after(side, mask):
+                dense_copy(side, mask, k).start()
+
+    def up_rows(mask):
+        return pl.ds((flip(chip, mask) * 2 + core) * slice_rows, slice_rows)
+
+    def unit_columns(part, mask):
+        return pl.ds(pl.multiple_of(part * units + flip(chip, mask) * hidden, hidden), hidden)
+
+    def up_copy(part, mask):
+        return pltpu.make_async_remote_copy(
+            src_ref=up_ref.at[:, :, unit_columns(part, mask)],
+            dst_ref=up_out.at[:, up_rows(0), pl.ds(part * hidden, hidden)],
+            send_sem=up_send.at[part, mask],
+            recv_sem=up_recv.at[part, mask],
+            device_id={"chip": flip(chip, mask)},
+            device_id_type=MESH,
+        )
+
+    def up_twin(mask):
+        place = up_out.at[:, up_rows(mask), :]
+        return pltpu.make_async_remote_copy(
+            src_ref=place,
+            dst_ref=place,
+            send_sem=twin_send.at[mask],
+            recv_sem=twin_recv.at[mask],
+            device_id=twin,
+            device_id_type=MESH,
+        )
+
+    down_twin = pltpu.make_async_remote_copy(
+        src_ref=down_ref,
+        dst_ref=down_out.at[:, core],
+        send_sem=twin_send.at[chips],
+        recv_sem=twin_recv.at[chips],
+        device_id=twin,
+        device_id_type=MESH,
+    )
+    locals_ = [
+        pltpu.make_async_copy(slice_ref.at[hz], dense_out.at[chip, core, hz], local.at[0]),
+        pltpu.make_async_copy(x_ref, x_out.at[hz], local.at[1]),
+        pltpu.make_async_copy(down_ref, down_out.at[:, core], local.at[2]),
+    ] + [
+        pltpu.make_async_copy(
+            up_ref.at[:, :, unit_columns(part, 0)],
+            up_out.at[:, up_rows(0), pl.ds(part * hidden, hidden)],
+            local.at[3 + part],
+        )
+        for part in range(2)
+    ]
+    for d in others:
+        slice_copy(d).start()
+    for copy in locals_:
+        copy.start()
+    along(0, lambda copy: copy.start())
+    down_twin.start()
+    locals_[0].wait()
+    for d in others:
+        slice_copy(d).wait_recv()
+    dense_turn(0)
+    for mask in range(1, chips):
+        for part in range(2):
+            up_copy(part, mask).start()
+    masks = sorted(range(1, 2 * chips), key=lambda m: bin(m).count("1"))
+    shares = [masks[len(masks) * i // heads : len(masks) * (i + 1) // heads] for i in range(heads)]
+    for mask in shares[0]:
+        dense_turn(mask)
+    for rank in range(1, heads):
+        x_copy(rank, 1).wait_recv()
+        along(rank, lambda copy: copy.start())
+        for mask in shares[rank]:
+            dense_turn(mask)
+    for copy in locals_[3:]:
+        copy.wait()
+    up_twin(0).start()
+    for mask in range(1, chips):
+        for part in range(2):
+            up_copy(part, mask).wait_recv()
+        up_twin(mask).start()
+    for copy in locals_[1:3]:
+        copy.wait()
+    down_twin.wait()
+    for mask in range(chips):
+        up_twin(mask).wait()
+    for rank in range(heads):
+        along(rank, lambda copy: copy.wait_send())
+    for d in others:
+        slice_copy(d).wait_send()
+    for mask in [0] + masks:
+        for side in range(2):
+            for k in steps_after(side, mask):
+                dense_copy(side, mask, k).wait_send()
+    for mask in range(1, chips):
+        for part in range(2):
+            up_copy(part, mask).wait_send()
+
+
+def start(x, slices, w_gate_up, w_down, chips, heads, hidden, number):
+    cube = Cube(chips, True)
+    experts_here, slice_rows, _ = w_gate_up.shape
+    width = slice_rows * 2 * chips
+    return pl.pallas_call(
+        functools.partial(start_kernel, cube, heads, hidden),
+        out_shape=(
+            jax.ShapeDtypeStruct((heads,) + x.shape, bf16),
+            jax.ShapeDtypeStruct((chips, 2) + slices.shape, bf16),
+            jax.ShapeDtypeStruct((experts_here, width, 2 * hidden), bf16),
+            jax.ShapeDtypeStruct((experts_here, 2) + w_down.shape[1:], bf16),
+        ),
+        in_specs=[ANY] * 4,
+        out_specs=(ANY,) * 4,
+        scratch_shapes=[
+            DMA((5,)),
+            DMA((heads + 1,)),
+            DMA((heads,)),
+            DMA((heads - 1,)),
+            DMA((heads - 1,)),
+            DMA((2, 2 * chips)),
+            DMA((2, 2 * chips)),
+            DMA((2, chips)),
+            DMA((2, chips)),
+            DMA((chips + 1,)),
+            DMA((chips + 1,)),
+        ],
+        compiler_params=pltpu.CompilerParams(collective_id=number, has_side_effects=True),
+        name="start",
+    )(x, slices, w_gate_up, w_down)
+
+
+def end_kernel(cube, heads, first_ref, in_ref, first_out, out_ref, *refs):
+    count = cube.number
+    arrived = refs[:count]
+    parts = refs[count : 2 * count]
+    local, first_send, first_recv, line_send, line_recv, send, recv = refs[2 * count :]
+    hz = lax.axis_index("head")
+    others = near(heads)[::-1]
+    half = in_ref.shape[-2] // 2
+    rows = in_ref.shape[-2] // heads
+    meet([cube.peer(digit) for digit in range(count)] + [{"head": (hz + d) % heads} for d in others])
+    own = pltpu.make_async_copy(first_ref.at[hz], first_out.at[hz], local)
+    own.start()
+    copies = {}
+
+    def slot(side, k, mask):
+        return subsets(cube.scatter_orders[side][k + 1 :]).index(mask)
+
+    def mine(side, mask):
+        return in_ref.at[cube.place(mask) + (pl.ds(side * half, half),)]
+
+    def total(side, steps, mask):
+        value = mine(side, mask)[...].astype(f32)
+        for j in range(steps):
+            copies[(side, j, mask)].wait_recv()
+            value = value + arrived[j][side, slot(side, j, mask)].astype(f32)
+        return value.astype(bf16)
+
+    def first_copy(d):
+        place = (hz + d) % heads
+        return pltpu.make_async_remote_copy(
+            src_ref=first_ref.at[place],
+            dst_ref=first_out.at[hz],
+            send_sem=first_send.at[d - 1],
+            recv_sem=first_recv.at[d - 1],
+            device_id={"head": place},
+            device_id_type=MESH,
+        )
+
+    for k in range(count):
+        for side in range(2):
+            order = cube.scatter_orders[side]
+            for mask in subsets(order[k + 1 :])[::-1]:
+                full = mask | (1 << order[k])
+                where = slot(side, k, mask)
+                if k == 0:
+                    piece = mine(side, full)
+                else:
+                    piece = parts[k - 1].at[side, where]
+                    piece[...] = total(side, k, full)
+                copies[(side, k, mask)] = pltpu.make_async_remote_copy(
+                    src_ref=piece,
+                    dst_ref=arrived[k].at[side, where],
+                    send_sem=send.at[side, k, where],
+                    recv_sem=recv.at[side, k, where],
+                    device_id=cube.peer(order[k]),
+                    device_id_type=MESH,
+                )
+                copies[(side, k, mask)].start()
+        if k == 0:
+            for d in others:
+                first_copy(d).start()
+    done = parts[count - 1]
+    for side in range(2):
+        done[0, pl.ds(side * half, half)] = total(side, count, 0)
+
+    def line_copy(d):
+        place = (hz + d) % heads
+        return pltpu.make_async_remote_copy(
+            src_ref=done.at[0, pl.ds(pl.multiple_of(place * rows, 16), rows)],
+            dst_ref=out_ref.at[hz],
+            send_sem=line_send.at[d - 1],
+            recv_sem=line_recv.at[d - 1],
+            device_id={"head": place},
+            device_id_type=MESH,
+        )
+
+    for d in others:
+        line_copy(d).start()
+    out_ref[hz] = done[0, pl.ds(pl.multiple_of(hz * rows, 16), rows)]
+    for copy in copies.values():
+        copy.wait_send()
+    own.wait()
+    for d in others:
+        line_copy(d).wait()
+    for d in others:
+        first_copy(d).wait()
+
+
+def end(first, sums, chips, heads, number):
+    rows, columns = sums.shape[-2:]
+    cube = Cube(chips, True)
+    count = cube.number
+    half = rows // 2
+    slots = [(1 << count) >> (k + 1) for k in range(count)]
+    return pl.pallas_call(
+        functools.partial(end_kernel, cube, heads),
+        out_shape=(
+            jax.ShapeDtypeStruct(first.shape, bf16),
+            jax.ShapeDtypeStruct((heads, rows // heads, columns), bf16),
+        ),
+        in_specs=[ANY, WHOLE],
+        out_specs=(ANY, WHOLE),
+        scratch_shapes=[pltpu.VMEM((2, s, half, columns), bf16) for s in slots]
+        + [pltpu.VMEM((2, s, half, columns), bf16) for s in slots[1:]]
+        + [
+            pltpu.VMEM((1, rows, columns), bf16),
+            DMA,
+            DMA((heads - 1,)),
+            DMA((heads - 1,)),
+            DMA((heads - 1,)),
+            DMA((heads - 1,)),
+            DMA((2, count, slots[0])),
+            DMA((2, count, slots[0])),
+        ],
+        compiler_params=pltpu.CompilerParams(
+            collective_id=number, has_side_effects=True, vmem_limit_bytes=40 << 20
+        ),
+        name="end",
+    )(first, sums)
+
+
+def place_kernel(chips, hidden, *refs):
+    pieces, out_ref = refs[:chips], refs[chips]
+    chip = lax.axis_index("chip")
+    units = out_ref.shape[2] // 2
+    for mask in range(chips):
+        for part in range(2):
+            begin = pl.multiple_of(part * units + flip(chip, mask) * hidden, hidden)
+            out_ref[:, :, pl.ds(begin, hidden)] = pieces[mask][
+                :, :, pl.ds(part * hidden, hidden)
+            ].astype(f32)
+
+
+def place_units(pieces, hidden):
+    chips = len(pieces)
+    experts_here, rows, double = pieces[0].shape
+    return pl.pallas_call(
+        functools.partial(place_kernel, chips, hidden),
+        grid=(experts_here,),
+        out_shape=jax.ShapeDtypeStruct((experts_here, rows, chips * double), f32),
+        in_specs=[pl.BlockSpec((1, rows, double), lambda e: (e, 0, 0))] * chips,
+        out_specs=pl.BlockSpec((1, rows, chips * double), lambda e: (e, 0, 0)),
+        name="place_units",
+    )(*pieces)
 
 
 def across(value, chips, mask):
     if mask == 0:
         return value
     return lax.ppermute(value, "chip", [(i, i ^ mask) for i in range(chips)])
+
+
+class Sums:
+    def __init__(self, blocks):
+        self.chips, self.heads = blocks.shape[:2]
+        rows, columns = blocks.shape[2:]
+        self.sides = blocks.reshape(self.chips, self.heads, 2, rows // 2, columns)
+        self.cube = Cube(self.chips, False)
+        self.arrived = {}
+        self.shape = (rows, columns)
+
+    def block(self, side, mask, steps):
+        chip = lax.axis_index("chip")
+        value = lax.dynamic_index_in_dim(self.sides[:, :, side], chip ^ mask, 0, keepdims=False)
+        value = value.astype(f32)
+        for j in range(steps):
+            order = self.cube.scatter_orders[side]
+            where = subsets(order[j + 1 :]).index(mask)
+            value = value + self.arrived[(side, j)][where].astype(f32)
+        return value
+
+    def plane(self, k):
+        for side in range(2):
+            order = self.cube.scatter_orders[side]
+            give = jnp.stack(
+                [
+                    self.block(side, mask | (1 << order[k]), k).astype(bf16)
+                    for mask in subsets(order[k + 1 :])
+                ]
+            )
+            self.arrived[(side, k)] = across(give, self.chips, 1 << order[k])
+
+    def along(self):
+        count = self.cube.number
+        whole = jnp.concatenate([self.block(side, 0, count) for side in range(2)], axis=1)
+        head = lax.axis_index("head")
+        self.own = lax.dynamic_index_in_dim(whole, head, 0, keepdims=False)
+        whole = whole.astype(bf16)
+        self.line = []
+        for d in range(1, self.heads):
+            give = lax.dynamic_index_in_dim(whole, (head + d) % self.heads, 0, keepdims=False)
+            pairs = [(i, (i + d) % self.heads) for i in range(self.heads)]
+            self.line.append(lax.ppermute(give, "head", pairs))
+
+    def result(self):
+        return self.own + sum(value.astype(f32) for value in self.line)
+
+
+def pin(sums, value):
+    keys = list(sums.arrived)
+    out = lax.optimization_barrier((value, [sums.arrived[key] for key in keys]))
+    for key, kept in zip(keys, out[1]):
+        sums.arrived[key] = kept
+    return out[0]
 
 
 def sibling(value):
@@ -886,47 +1431,59 @@
     seq_index = chip * 2 + core
     dense_rows = query_key_value_weight.shape[0]
 
-    parts = w_gate_up.reshape(loc_experts, slice_rows, 2, chips, hidden).transpose(3, 2, 1, 0, 4)
-    parts = parts.reshape(chips, 2, slice_rows, loc_experts * hidden)
-    piled = jnp.zeros((chips, 2, 2, slice_rows, loc_experts * hidden), bf16)
-    for mask in range(chips):
-        piece = lax.dynamic_index_in_dim(parts, chip ^ mask, 0, keepdims=False)
-        piece = across(piece, chips, mask)
-        other = sibling(piece)
-        piled = lax.dynamic_update_slice(piled, piece[None, None], (chip ^ mask, core, 0, 0, 0))
-        piled = lax.dynamic_update_slice(piled, other[None, None], (chip ^ mask, 1 - core, 0, 0, 0))
-    piled = piled.transpose(2, 0, 1, 3, 4).reshape(2, width, loc_experts * hidden)
-    expert_gate, expert_up = piled[0], piled[1]
-    down_other = sibling(w_down)
-    expert_down = (
-        jnp.where(
-            core == 0,
-            jnp.concatenate([w_down, down_other], axis=1),
-            jnp.concatenate([down_other, w_down], axis=1),
-        )
-    ).reshape(loc_experts * hidden, width)
-
-    grad_all = lax.all_gather(
-        cotangent.reshape(tokens_present, width), ("chip", "head"), axis=0, tiled=True
-    )
-    dense_out = lax.all_gather(output_weight, ("chip", "core", "head"), axis=0, tiled=True)
-
     extras = jnp.concatenate([router_weight, norm_attn[:, None], norm_ffn[:, None]], axis=1)
     extras = jnp.pad(extras, ((0, 0), (0, LANES - extras.shape[1])))
     slices = query_key_value_weight.reshape(dense_rows, head_number, loc_columns).transpose(1, 0, 2)
     slices = jnp.concatenate(
         [slices, jnp.broadcast_to(extras, (head_number,) + extras.shape)], axis=2
     )
-    lined = line_exchange(slices, head_number, 1)
-    dense = gather(
-        lined.reshape(head_number * dense_rows, loc_columns + LANES), chips, 1, True, 2
-    ).reshape(width, loc_columns + LANES)
+    group_tokens = chips * head_number * tokens_present
+    columns = width + LANES
+    fused = hidden % LANES == 0 and group_tokens <= 2048
+    own_tokens = layer_input.reshape(tokens_present, width)
+    cots = cotangent.reshape(tokens_present, width)
+    if fused:
+        x_line, dense, expert_up, expert_down = start(
+            own_tokens, slices, w_gate_up, w_down, chips, head_number, hidden, 1
+        )
+        expert_down = expert_down.reshape(loc_experts * hidden, width)
+        dense = dense.reshape(width, loc_columns + LANES)
+        cots, x_line = lax.optimization_barrier((cots, x_line))
+    else:
+        parts = w_gate_up.reshape(loc_experts, slice_rows, 2, chips, hidden).transpose(3, 2, 1, 0, 4)
+        parts = parts.reshape(chips, 2, slice_rows, loc_experts * hidden)
+        piled = jnp.zeros((chips, 2, 2, slice_rows, loc_experts * hidden), bf16)
+        for mask in range(chips):
+            piece = lax.dynamic_index_in_dim(parts, chip ^ mask, 0, keepdims=False)
+            piece = across(piece, chips, mask)
+            other = sibling(piece)
+            piled = lax.dynamic_update_slice(piled, piece[None, None], (chip ^ mask, core, 0, 0, 0))
+            piled = lax.dynamic_update_slice(piled, other[None, None], (chip ^ mask, 1 - core, 0, 0, 0))
+        piled = piled.transpose(2, 0, 1, 3, 4).reshape(2, width, loc_experts * hidden)
+        expert_gate, expert_up = piled[0], piled[1]
+        down_other = sibling(w_down)
+        expert_down = (
+            jnp.where(
+                core == 0,
+                jnp.concatenate([w_down, down_other], axis=1),
+                jnp.concatenate([down_other, w_down], axis=1),
+            )
+        ).reshape(loc_experts * hidden, width)
+
+        lined = line_exchange(slices, head_number, 1)
+        dense = gather(
+            lined.reshape(head_number * dense_rows, loc_columns + LANES), chips, 1, True, 2
+        ).reshape(width, loc_columns + LANES)
+        x_line = line_exchange(layer_input.reshape(tokens_present, width), head_number, 3, True)
+
+    grad_all = lax.all_gather(cots, ("chip", "head"), axis=0, tiled=True)
+    dense_out = lax.all_gather(output_weight, ("chip", "core", "head"), axis=0, tiled=True)
+
     dense_qkv = dense[:, :loc_columns]
     dense_router = dense[:, loc_columns : loc_columns + EXPERTS]
     gain_attn = dense[:, loc_columns + EXPERTS].astype(f32)
     gain_ffn = dense[:, loc_columns + EXPERTS + 1].astype(f32)
 
-    x_line = line_exchange(layer_input.reshape(tokens_present, width), head_number, 3, True)
     x_line = x_line.reshape(line_tokens, width).astype(f32)
     normed_line = x_line * lax.rsqrt(jnp.mean(x_line * x_line, axis=1, keepdims=True) + epsilon)
     first_line = (normed_line * gain_attn).astype(bf16)
@@ -1056,13 +1613,17 @@
     spread_low = (spread - spread_high.astype(f32)).astype(bf16)
     pad = jnp.zeros((tokens_present, LOW - EXPERTS), bf16)
     payload = jnp.concatenate([second_input, spread_high, pad, spread_low, pad], axis=1)
-    columns = width + LANES
-    group_tokens = chips * head_number * tokens_present
-    needs = 10 * group_tokens * width + 6 * width * expert_gate.shape[1]
-    if needs + 6 * group_tokens * expert_gate.shape[1] <= 60 << 20:
-        back, moe_part, d_gate_w, d_up_w, d_down_w = expert_turn(
-            payload, grad_all, expert_gate, expert_up, expert_down, hidden, chips, head_number, 6
-        )
+    if fused:
+        back, moe_part, keep_up, other_up, keep_down, other_down = expert_turn(
+            payload, grad_all, expert_up, expert_down, chips, head_number, 6
+        )
+        moe_sums = Sums(moe_part.reshape(chips, head_number, tokens_present, width))
+        shared = (keep_up.astype(f32) + other_up.astype(f32)).astype(bf16)
+        pieces = [
+            across(lax.dynamic_index_in_dim(shared, chip ^ mask, 0, keepdims=False), chips, mask)
+            for mask in range(chips)
+        ]
+        down_share = keep_down.astype(f32) + other_down.astype(f32)
     else:
         x_all = gather(payload, chips, head_number, False, 6).reshape(group_tokens, columns)
         moe_part, back_part, d_gate_w, d_up_w, d_down_w = experts(
@@ -1070,28 +1631,25 @@
         )
         back_part = back_part.reshape(chips, head_number, tokens_present, columns)
         back = scatter_sum(back_part, chips, head_number, False, 7)
-    moe = lax.psum_scatter(moe_part, ("chip", "head"), scatter_dimension=0, tiled=True)
-    mixed_out = (middle + moe.astype(f32)).astype(bf16)
-    mixed_out = mixed_out.reshape(sequence_batch, token_rows, width)
-
-    grads = jnp.stack([d_gate_w, d_up_w]).reshape(2, chips, 2, slice_rows, loc_experts * hidden)
-    keep = lax.dynamic_index_in_dim(grads, core, 2, keepdims=False)
-    give = lax.dynamic_index_in_dim(grads, 1 - core, 2, keepdims=False)
-    shared = (keep.astype(f32) + sibling(give).astype(f32)).astype(bf16)
-    piled = jnp.zeros((chips, 2, slice_rows, loc_experts * hidden), bf16)
-    for mask in range(chips):
-        piece = across(lax.dynamic_index_in_dim(shared, chip ^ mask, 1, keepdims=False), chips, mask)
-        piled = lax.dynamic_update_slice(piled, piece[None], (chip ^ mask, 0, 0, 0))
-    up_share = (
-        piled.reshape(chips, 2, slice_rows, loc_experts, hidden)
-        .transpose(3, 2, 1, 0, 4)
-        .astype(f32)
-        .reshape(loc_experts, slice_rows, 2 * FF)
-    )
-    d_down_w = d_down_w.reshape(loc_experts, 2, hidden // 2, width)
-    keep = lax.dynamic_index_in_dim(d_down_w, core, 1, keepdims=False)
-    give = lax.dynamic_index_in_dim(d_down_w, 1 - core, 1, keepdims=False)
-    down_share = keep.astype(f32) + sibling(give).astype(f32)
+        moe = lax.psum_scatter(moe_part, ("chip", "head"), scatter_dimension=0, tiled=True)
+        grads = jnp.stack([d_gate_w, d_up_w]).reshape(2, chips, 2, slice_rows, loc_experts * hidden)
+        keep = lax.dynamic_index_in_dim(grads, core, 2, keepdims=False)
+        give = lax.dynamic_index_in_dim(grads, 1 - core, 2, keepdims=False)
+        shared = (keep.astype(f32) + sibling(give).astype(f32)).astype(bf16)
+        piled = jnp.zeros((chips, 2, slice_rows, loc_experts * hidden), bf16)
+        for mask in range(chips):
+            piece = across(lax.dynamic_index_in_dim(shared, chip ^ mask, 1, keepdims=False), chips, mask)
+            piled = lax.dynamic_update_slice(piled, piece[None], (chip ^ mask, 0, 0, 0))
+        up_share = (
+            piled.reshape(chips, 2, slice_rows, loc_experts, hidden)
+            .transpose(3, 2, 1, 0, 4)
+            .astype(f32)
+            .reshape(loc_experts, slice_rows, 2 * FF)
+        )
+        d_down_w = d_down_w.reshape(loc_experts, 2, hidden // 2, width)
+        keep = lax.dynamic_index_in_dim(d_down_w, core, 1, keepdims=False)
+        give = lax.dynamic_index_in_dim(d_down_w, 1 - core, 1, keepdims=False)
+        down_share = keep.astype(f32) + sibling(give).astype(f32)
 
     grad_out = cotangent.reshape(tokens_present, width).astype(f32)
     d_kept = back[:, width : width + EXPERTS]
@@ -1121,6 +1679,10 @@
     grad_local = to_blocks(
         line_exchange(grad_heads, head_number, 8).reshape(line_tokens, group_columns)
     ).reshape(sequence_batch, blk, key_value_location, query_group, HEAD_WIDTH)
+    if fused:
+        moe_sums.plane(0)
+        grad_local = pin(moe_sums, grad_local)
+        moe_sums.plane(1)
     delta = jnp.sum(grad_local.transpose(0, 2, 3, 1, 4).astype(f32) * attended, axis=-1)
 
     def backward_block(state, piece, offset, token_count):
@@ -1157,6 +1719,9 @@
         jnp.zeros((sequence_batch, length, kv_columns), bf16),
     )
     grad_q, grad_store = sweep(backward_block, back_zero)
+    if fused:
+        grad_store = pin(moe_sums, grad_store)
+        moe_sums.along()
     grad_store = (
         grad_store.reshape(sequence_batch, 2 * chips, blk, kv_columns)
         .transpose(1, 0, 2, 3)
@@ -1173,21 +1738,7 @@
         .astype(bf16)
     )
     grad_first_part = jnp.dot(grad_qkv, dense_qkv.T, preferred_element_type=f32)
-    grad_first = jnp.sum(
-        line_exchange(
-            grad_first_part.astype(bf16).reshape(head_number, tokens_present, width),
-            head_number,
-            10,
-        ).astype(f32),
-        axis=0,
-    )
     grad_gain_attn = jnp.sum(grad_first_part * normed_line, axis=0)
-    inverse_one = lax.rsqrt(jnp.mean(tokens * tokens, axis=1, keepdims=True) + epsilon)
-    normed_one = tokens * inverse_one
-    scaled_one = grad_first * gain_attn
-    grad_input = grad_mid + inverse_one * (
-        scaled_one - normed_one * jnp.mean(scaled_one * normed_one, axis=1, keepdims=True)
-    )
     grad_dense_qkv = jnp.dot(first_line.T, grad_qkv, preferred_element_type=f32)
     sums = jnp.concatenate(
         [
@@ -1199,12 +1750,42 @@
         ],
         axis=1,
     ).astype(bf16)
-    sums = scatter_sum(
-        sums.reshape(chips, 2, head_number * dense_rows, loc_columns + LANES), chips, 1, True, 11
-    )
-    sums = line_exchange(
-        sums.reshape(head_number, dense_rows, loc_columns + LANES), head_number, 12
-    )
+    if fused:
+        grad_first, sums = end(
+            grad_first_part.astype(bf16).reshape(head_number, tokens_present, width),
+            sums.reshape(chips, 2, head_number * dense_rows, loc_columns + LANES),
+            chips,
+            head_number,
+            13,
+        )
+        pieces, grad_first = lax.optimization_barrier((pieces, grad_first))
+        grad_first = jnp.sum(grad_first.astype(f32), axis=0)
+        sums = sums.astype(f32)
+        up_share = place_units(pieces, hidden)
+        moe = moe_sums.result()
+    else:
+        grad_first = jnp.sum(
+            line_exchange(
+                grad_first_part.astype(bf16).reshape(head_number, tokens_present, width),
+                head_number,
+                10,
+            ).astype(f32),
+            axis=0,
+        )
+        sums = scatter_sum(
+            sums.reshape(chips, 2, head_number * dense_rows, loc_columns + LANES), chips, 1, True, 11
+        )
+        sums = line_exchange(
+            sums.reshape(head_number, dense_rows, loc_columns + LANES), head_number, 12
+        )
+    inverse_one = lax.rsqrt(jnp.mean(tokens * tokens, axis=1, keepdims=True) + epsilon)
+    normed_one = tokens * inverse_one
+    scaled_one = grad_first * gain_attn
+    grad_input = grad_mid + inverse_one * (
+        scaled_one - normed_one * jnp.mean(scaled_one * normed_one, axis=1, keepdims=True)
+    )
+    mixed_out = (middle + moe.astype(f32)).astype(bf16)
+    mixed_out = mixed_out.reshape(sequence_batch, token_rows, width)
     qkv_share = sums[:, :, :loc_columns].transpose(1, 0, 2).reshape(dense_rows, -1)
     extra = jnp.sum(sums[:, :, loc_columns:], axis=0)
     return (

time: 902 us -> 671 us (0.74)
  waiting for transfers between devices: 150 us -> 59.5 us
  local copies, waits for them, and re-layouts: 160 us -> 76.4 us
  Pallas kernels: 463 us -> 408 us
    pallas_call x1 -> x4, Pallas kernels: 193 us -> 341 us  [the longest x1 169 us: expert_turn(): pl.pallas_call(functools.partial(turn_kernel, cube, heads, hidden), out_s...]
    reduce_scatter x1 -> x0, waiting for transfers between devices: 120 us -> none  [per_device(): lax.psum_scatter(moe_part, ('chip', 'head'), scatter_dimension=0, tiled=T...]
    pallas_call x6 -> x2, Pallas kernels: 141 us -> 29.5 us  [line_exchange(): pl.pallas_call(functools.partial(line_kernel, heads, same), out_shape=jax...]
    pallas_call x2 -> x1, Pallas kernels: 67 us -> 20.5 us  [gather(): pl.pallas_call(functools.partial(gather_kernel, cube, heads), out_shape=j...]
    pallas_call x2 -> x1, Pallas kernels: 61.6 us -> 17.5 us  [scatter_sum(): pl.pallas_call(functools.partial(scatter_kernel, cube, heads), out_shape=...]
    reshape x4 -> x0, local copies, waits for them, and re-layouts: 38.3 us -> none  [the longest x2 21.6 us: per_device(): up_share = piled.reshape(chips, 2, slice_rows, loc_experts, hidden).trans...]
    dynamic_slice x6 -> x0, local copies, waits for them, and re-layouts: 14.1 us -> none  [the longest x5 11.7 us: per_device(): piece = lax.dynamic_index_in_dim(parts, chip ^ mask, 0, keepdims=False)]
    dynamic_update_slice x12 -> x0, local copies, waits for them, and re-layouts: 13 us -> none  [the longest x4 7.32 us: per_device(): piled = lax.dynamic_update_slice(piled, piece[None], (chip ^ mask, 0, 0, 0))]
  transfers between devices with their start and end apart: 17 -> 13, of which waited for: 3 -> 4; matrix products, arithmetic and copies ran while one was open for 28% -> 23% of each run, Pallas kernels for 30% -> 36%
where the time goes in v3:
time: 671 us; the launch traced here: 661 us
  Pallas kernels  408 us (61%)
  local copies, waits for them, and re-layouts  76.4 us (11%)
  waiting for transfers between devices  59.5 us (9%)
  other arithmetic  46 us (7%)
  matrix products  39.1 us (6%)
  starting transfers between devices  15.7 us (2%)
  between operations  15 us (2%)
    pallas_call x1, Pallas kernels, expert_turn(): pl.pallas_call(functools.partial(turn_kernel, cube, heads, hidden), out_s...  169 us
    pallas_call x1, Pallas kernels, start(): pl.pallas_call(functools.partial(start_kernel, cube, heads, hidden), out_...  117 us
    pallas_call x1, Pallas kernels, end(): pl.pallas_call(functools.partial(end_kernel, cube, heads), out_shape=(jax...  46.5 us
    ppermute x7, waiting for transfers between devices, across(): return lax.ppermute(value, 'chip', [(i, i ^ mask) for i in range(chips)])  41 us
    pallas_call x2, Pallas kernels, line_exchange(): pl.pallas_call(functools.partial(line_kernel, heads, same), out_shape=jax...  29.5 us
    pallas_call x1, Pallas kernels, gather(): pl.pallas_call(functools.partial(gather_kernel, cube, heads), out_shape=j...  20.5 us
    pallas_call x1, Pallas kernels, scatter_sum(): pl.pallas_call(functools.partial(scatter_kernel, cube, heads), out_shape=...  17.5 us
  transfers between devices with their start and end apart: 13, of which 4 were waited for; matrix products, arithmetic and copies ran while one was open for 23% of the time, Pallas kernels for 36%

profile of v3, /device:TPU:0, one launch (start us, length us, event | category | flops | bytes accessed | tf_op | source)
XLA Modules:
  0.0 660.7 jit_solution(17362815370326251367)
XLA Ops:
  10.5 117.1 %start.1 = (bf16[4,128,1536]{2,1,0:T(8,128)(2,1)}, bf16[4,2,4,48,768]{4,3,2,1,0:T(8,128)(2,1)}, bf16[10,1536,256]{2,1,0:T(8,128)(2,1)}, bf16[10,2,64,1536]{3,2,1,0:T(8,128)(2,1)}) custom-call(bf16[128,1536]{1,0:T(8,128)(2,1)} %bitcast.304, bf16[4,48,768]{2,1,0:T(8,128)(2,1)} %pad_maximum_fusion.6.refs_1_, bf16[10,192,1024]{2,1,0:T(8,128)(2,1)} %refs_2_.1, ...), custom_call_target="tpu_custom_call" | custom-call | tf_op jit(solution)/shard_map/start/pallas_call | solution.py:1161
  132.1 4.6 fusion.54
  136.8 3.3 copy.209
  140.1 2.5 reshape_reshape.15
  147.3 20.5 %gather.1 = bf16[4,2,512,256]{3,2,1,0:T(8,128)(2,1)} custom-call(bf16[512,256]{1,0:T(8,128)(2,1)} %reshape.587.in_ref), custom_call_target="tpu_custom_call" | custom-call | tf_op jit(solution)/shard_map/gather/pallas_call | solution.py:173
  167.8 4.5 copy.212
  172.3 2.9 reshape.555
  176.0 6.0 while.38
  176.0 5.8 conditional.6
  183.0 2.8 convert_element_type.302
  187.9 18.2 %line_exchange.2 = bf16[4,128,384]{2,1,0:T(8,128)(2,1)} custom-call(bf16[4,128,384]{2,1,0:T(8,128)(2,1)} %bitcast.326), custom_call_target="tpu_custom_call" | custom-call | tf_op jit(solution)/shard_map/line_exchange/pallas_call | solution.py:332
  209.6 3.1 multiply_convert_fusion
  212.7 3.1 copy.234
  217.2 3.2 multiply_reduce_fusion.3
  224.3 4.8 all-gather.5.cloned.1.call-done.refs_1_
  229.2 168.7 %expert_turn.1 = (f32[128,1664]{1,0:T(8,128)}, bf16[2048,1536]{1,0:T(8,128)(2,1)}, bf16[4,10,192,256]{3,2,1,0:T(8,128)(2,1)}, bf16[4,10,192,256]{3,2,1,0:T(8,128...) custom-call(bf16[128,1664]{1,0:T(8,128)(2,1)} %concatenate.38.refs_0_, ...), custom_call_target="tpu_custom_call" | custom-call | tf_op jit(solution)/shard_map/expert_turn/pallas_call | solution.py:925
  398.9 3.3 fusion.85
  407.1 4.0 collective-permute-start
  411.1 2.4 multiply_reduce_fusion.1
  418.0 5.0 convolution_convert_fusion.1
  426.8 11.3 %line_exchange.3 = bf16[4,128,384]{2,1,0:T(8,128)(2,1)} custom-call(bf16[4,128,384]{2,1,0:T(8,128)(2,1)} %bitcast.325), custom_call_target="tpu_custom_call" | custom-call | tf_op jit(solution)/shard_map/line_exchange/pallas_call | solution.py:332
  438.1 2.1 copy.227
  440.2 2.7 reshape_reshape.19
  442.9 2.2 concatenate.47
  445.1 4.8 add_convert_fusion
  455.4 3.5 convolution_convert_fusion
  458.9 2.4 fusion.50
  462.4 2.5 fusion.51
  465.7 2.5 convert_add_fusion
  469.0 8.8 %while.39 = (s32[]{:T(128)}, f32[2,256,2,3,64]{1,4,3,2,0:T(8,128)S(1)}, bf16[2,2048,256]{1,2,0:T(8,128)(2,1)S(1)}, s32[]{:T(128)}, bf16[2,2048,256]{1,2,0:T(8,12...) while((s32[]{:T(128)}, ...), condition=%wide.region_21.22_spmd.clone, body=%wide.region_18.21_spmd.clone.sunk | while | flops 1024066304 | bytes 39651704 | solution.py:1554
  469.0 8.7 %conditional.7 = ((f32[2,256,2,3,64]{1,4,3,2,0:T(8,128)S(1)}, bf16[2,2048,256]{1,2,0:T(8,128)(2,1)S(1)})) conditional(s32[]{:T(128)} %convert_element_type.468, (f32[2,256,2,3,64]{1,4,3,2,0:T(8,128)S(1)}, bf16[2,2048,256]{1,2,0:T(8,128)(2,1)S(1)}) %tuple.135, (s32[]{:T(128)}, bf16[2,2048,256]{1,2,0:T(8,128)(2,1)}, s32[2,256]{1,0:T(2,128)S(1)}, ...), branch_computations={%region_19.19_spmd, %region_20.20_spmd} | conditional | flops 1024066304 | bytes 39650412 | solution.py:1547
  478.6 38.9 %collective-permute-done.3 = bf16[1,4,64,1536]{3,2,1,0:T(8,128)(2,1)} collective-permute-done((bf16[1,4,64,1536]{3,2,1,0:T(8,128)(2,1)}, bf16[1,4,64,1536]{3,2,1,0:T(8,128)(2,1)}, u32[]{:S(2)}, u32[]{:S(2)}) %collective-permute-start.3) | collective-permute-done | bytes 786464 | tf_op jit(solution)/shard_map/ppermute | solution.py:1338
  517.5 2.1 collective-permute-done.2
  521.6 4.6 copy.229
  526.2 17.5 %scatter_sum.1 = f32[512,256]{1,0:T(8,128)} custom-call(bf16[4,2,512,256]{3,2,1,0:T(8,128)(2,1)} %bitcast.306), custom_call_target="tpu_custom_call" | custom-call | tf_op jit(solution)/shard_map/scatter_sum/pallas_call | solution.py:281
  546.6 2.3 convert_element_type.348
  548.9 2.4 copy.233
  551.3 4.5 fusion.44
  557.2 3.8 convolution_convert_fusion.2
  561.1 3.7 concatenate.45.in_ref
  566.2 46.5 %end.1 = (bf16[4,128,1536]{2,1,0:T(8,128)(2,1)S(1)}, bf16[4,48,768]{2,1,0:T(8,128)(2,1)S(1)}) custom-call(bf16[4,128,1536]{2,1,0:T(8,128)(2,1)S(1)} %bitcast.297, bf16[4,2,192,768]{3,2,1,0:T(8,128)(2,1)S(1)} %concatenate.45.in_ref), custom_call_target="tpu_custom_call" | custom-call | tf_op jit(solution)/shard_map/end/pallas_call | solution.py:1283
  615.6 2.9 convert_add_fusion.1
  619.8 2.1 collective-permute-start.4
  621.9 2.6 collective-permute-start.6
  624.5 8.6 %place_units.1 = f32[10,192,1024]{2,1,0:T(8,128)} custom-call(bf16[10,192,256]{2,1,0:T(8,128)(2,1)} %get-tuple-element.672.refs_0_, bf16[10,192,256]{2,1,0:T(8,128)(2,1)} %collective-permute-done.7.refs_1_, bf16[10,192,256]{2,1,0:T(8,128)(2,1)} %collective-permute-done.8.refs_2_, bf16[10,192,256]{2,1,0:T(8,128)(2,1)} %collective-permute-done.9.refs_3_), custom_call_target="tpu_custom_call" | custom-call | tf_op jit(solution)/shard_map/place_units/pallas_call | solution.py:1325
  634.6 2.5 fusion.60
  637.1 12.9 %collective-permute-done.5 = bf16[128,1536]{1,0:T(8,128)(2,1)} collective-permute-done((bf16[128,1536]{1,0:T(8,128)(2,1)}, bf16[128,1536]{1,0:T(8,128)(2,1)}, u32[]{:S(2)}, u32[]{:S(2)}) %collective-permute-start.5) | collective-permute-done | bytes 393248 | tf_op jit(solution)/shard_map/ppermute | solution.py:1381
  650.0 2.2 fusion.68
  (254 shorter events, 77.1 us)
Async XLA Ops:
  7.2 210.0 %all-gather.3.cloned.1.call-start = ((), (), s32[]{:S(2)}) async-start(), calls=%async_computation.1 | async-start | bytes 4866048 | tf_op jit(solution)/shard_map/all_gather | solution.py:1480
  7.9 221.3 %all-gather.5.cloned.1.call-start = ((), (), s32[]{:S(2)}) async-start(), calls=%async_computation.2 | async-start | bytes 6684672 | tf_op jit(solution)/shard_map/all_gather | solution.py:1479
  10.5 117.2 %copy-start.37 = (s32[2,64,8]{1,2,0:T(8,128)S(1)}, s32[2,64,8]{1,2,0:T(8,128)}, u32[]{:S(2)}) copy-start(s32[2,64,8]{1,2,0:T(8,128)} %param.22) | copy-start | bytes 12292
  127.7 524.6 %reduce-scatter.2.cloned.1.call-start = ((), (), s32[]{:S(2)}) async-start(), calls=%async_computation.3 | async-start | bytes 4866048 | tf_op jit(solution)/shard_map/reduce_scatter | solution.py:1670
  132.1 77.4 %copy-start.34 = (f32[1536]{0:T(1024)}, f32[1536]{0:T(1024)S(1)}, u32[]{:S(2)}) copy-start(f32[1536]{0:T(1024)S(1)} %get-tuple-element.776) | copy-start | bytes 18436
  132.1 90.1 %copy-start.32 = (f32[1536]{0:T(1024)}, f32[1536]{0:T(1024)S(1)}, u32[]{:S(2)}) copy-start(f32[1536]{0:T(1024)S(1)} %get-tuple-element.775) | copy-start | bytes 18436
  182.0 27.5 %copy-start.11 = (f32[2,2,3,256,64]{3,4,2,1,0:T(8,128)}, f32[2,2,3,256,64]{3,4,2,1,0:T(8,128)S(1)}, u32[]{:S(2)}) copy-start(f32[2,2,3,256,64]{3,4,2,1,0:T(8,128)S(1)} %get-tuple-element.649) | copy-start | bytes 2359300
  182.0 30.7 %copy-start.4 = (bf16[2,2048,256]{1,2,0:T(8,128)(2,1)}, bf16[2,2048,256]{1,2,0:T(8,128)(2,1)S(1)}, u32[]{:S(2)}) copy-start(bf16[2,2048,256]{1,2,0:T(8,128)(2,1)S(1)} %get-tuple-element.1100) | copy-start | bytes 6291460
  182.0 30.7 %copy-start.30 = (s32[2,256]{1,0:T(2,128)}, s32[2,256]{1,0:T(2,128)S(1)}, u32[]{:S(2)}) copy-start(s32[2,256]{1,0:T(2,128)S(1)} %get-tuple-element.1109) | copy-start | bytes 6148
  182.0 26.1 %copy-start.41 = (s32[2,64,8]{1,2,0:T(8,128)S(1)}, s32[2,64,8]{1,2,0:T(8,128)}, u32[]{:S(2)}) copy-start(s32[2,64,8]{1,2,0:T(8,128)} %param.23) | copy-start | bytes 12292
  209.6 6.2 copy-start.8
  209.6 7.6 %copy-start.15 = (bf16[128,4,384]{0,2,1:T(8,128)(2,1)S(1)}, bf16[128,4,384]{0,2,1:T(8,128)(2,1)}, u32[]{:S(2)}) copy-start(bf16[128,4,384]{0,2,1:T(8,128)(2,1)} %copy.214) | copy-start | bytes 1179652
  215.9 4.5 copy-start.42
  402.3 56.6 %copy-start.5 = (bf16[4,4,1,64,1536]{4,3,2,1,0:T(8,128)(2,1)}, bf16[4,4,1,64,1536]{4,3,2,1,0:T(8,128)(2,1)S(1)}, u32[]{:S(2)}) copy-start(bf16[4,4,1,64,1536]{4,3,2,1,0:T(8,128)(2,1)S(1)} %get-tuple-element.829) | copy-start | bytes 9437188
  404.0 54.9 %collective-permute-start.1 = (bf16[2,4,64,1536]{3,2,1,0:T(8,128)(2,1)}, bf16[2,4,64,1536]{3,2,1,0:T(8,128)(2,1)}, u32[]{:S(2)}, u32[]{:S(2)}) collective-permute-start(bf16[2,4,64,1536]{3,2,1,0:T(8,128)(2,1)} %pad_maximum_fusion.3), channel_id=1, source_target_pairs={{0,16},{8,24},{16,0},{24,8},{1,17},{9,25},{17,1},{25,9},{2,18},{10... | collective-permute-start | bytes 4718600 | tf_op jit(solution)/shard_map/ppermute | solution.py:1338
  405.6 5.5 copy-start.2
  405.6 5.5 copy-start.26
  405.6 5.5 copy-start.33
  405.6 5.5 copy-start.40
  405.7 7.7 %copy-start.20 = (bf16[2,64,1536]{2,1,0:T(8,128)(2,1)S(1)}, bf16[2,64,1536]{2,1,0:T(8,128)(2,1)}, u32[]{:S(2)}) copy-start(bf16[2,64,1536]{2,1,0:T(8,128)(2,1)} %param.31) | copy-start | bytes 1179652
  407.1 7.5 %copy-start.22 = (bf16[1536,128]{1,0:T(8,128)(2,1)S(1)}, bf16[1536,128]{1,0:T(8,128)(2,1)}, u32[]{:S(2)}) copy-start(bf16[1536,128]{1,0:T(8,128)(2,1)} %copy.235) | copy-start | bytes 1179652
  407.1 51.8 %collective-permute-start = (bf16[2,4,64,1536]{3,2,1,0:T(8,128)(2,1)}, bf16[2,4,64,1536]{3,2,1,0:T(8,128)(2,1)}, u32[]{:S(2)}, u32[]{:S(2)}) collective-permute-start(bf16[2,4,64,1536]{3,2,1,0:T(8,128)(2,1)} %pad_maximum_fusion.2), channel_id=1, source_target_pairs={{0,8},{8,0},{16,24},{24,16},{1,9},{9,1},{17,25},{25,17},{2,10},{10... | collective-permute-start | bytes 4718600 | tf_op jit(solution)/shard_map/ppermute | solution.py:1338
  449.9 5.5 copy-start.7
  449.9 5.5 copy-start.16
  451.9 160.9 %collective-permute-start.7 = (bf16[10,192,256]{2,1,0:T(8,128)(2,1)}, bf16[10,192,256]{2,1,0:T(8,128)(2,1)}, u32[]{:S(2)}, u32[]{:S(2)}) collective-permute-start(bf16[10,192,256]{2,1,0:T(8,128)(2,1)} %get-tuple-element.833), channel_id=1, source_target_pairs={{0,8},{8,0},{16,24},{24,16},{1,9},{9,1},{17,25},{25,17},{2,10},{10... | collective-permute-start | bytes 2949128 | tf_op jit(solution)/shard_map/ppermute | solution.py:1338
  452.9 159.9 %collective-permute-start.8 = (bf16[10,192,256]{2,1,0:T(8,128)(2,1)}, bf16[10,192,256]{2,1,0:T(8,128)(2,1)}, u32[]{:S(2)}, u32[]{:S(2)}) collective-permute-start(bf16[10,192,256]{2,1,0:T(8,128)(2,1)} %get-tuple-element.832), channel_id=1, source_target_pairs={{0,16},{8,24},{16,0},{24,8},{1,17},{9,25},{17,1},{25,9},{2,18},{10... | collective-permute-start | bytes 2949128 | tf_op jit(solution)/shard_map/ppermute | solution.py:1338
  453.8 159.0 %collective-permute-start.9 = (bf16[10,192,256]{2,1,0:T(8,128)(2,1)}, bf16[10,192,256]{2,1,0:T(8,128)(2,1)}, u32[]{:S(2)}, u32[]{:S(2)}) collective-permute-start(bf16[10,192,256]{2,1,0:T(8,128)(2,1)} %get-tuple-element.831), channel_id=1, source_target_pairs={{0,24},{8,16},{16,8},{24,0},{1,25},{9,17},{17,9},{25,1},{2,26},{10... | collective-permute-start | bytes 2949128 | tf_op jit(solution)/shard_map/ppermute | solution.py:1338
  458.9 6.8 %copy-start.17 = (bf16[10,64,1536]{2,1,0:T(8,128)(2,1)S(1)}, bf16[10,64,1536]{2,1,0:T(8,128)(2,1)}, u32[]{:S(2)}) copy-start(bf16[10,64,1536]{2,1,0:T(8,128)(2,1)} %get-tuple-element.676) | copy-start | bytes 5898244
  458.9 6.8 %copy-start.18 = (bf16[10,64,1536]{2,1,0:T(8,128)(2,1)S(1)}, bf16[10,64,1536]{2,1,0:T(8,128)(2,1)}, u32[]{:S(2)}) copy-start(bf16[10,64,1536]{2,1,0:T(8,128)(2,1)} %get-tuple-element.677) | copy-start | bytes 5898244
  461.3 56.2 %collective-permute-start.3 = (bf16[1,4,64,1536]{3,2,1,0:T(8,128)(2,1)}, bf16[1,4,64,1536]{3,2,1,0:T(8,128)(2,1)}, u32[]{:S(2)}, u32[]{:S(2)}) collective-permute-start(bf16[1,4,64,1536]{3,2,1,0:T(8,128)(2,1)} %fusion.50), channel_id=1, source_target_pairs={{0,8},{8,0},{16,24},{24,16},{1,9},{9,1},{17,25},{25,17},{2,10},{10... | collective-permute-start | bytes 2359304 | tf_op jit(solution)/shard_map/ppermute | solution.py:1338
  464.9 54.7 %collective-permute-start.2 = (bf16[1,4,64,1536]{3,2,1,0:T(8,128)(2,1)}, bf16[1,4,64,1536]{3,2,1,0:T(8,128)(2,1)}, u32[]{:S(2)}, u32[]{:S(2)}) collective-permute-start(bf16[1,4,64,1536]{3,2,1,0:T(8,128)(2,1)} %fusion.51), channel_id=1, source_target_pairs={{0,16},{8,24},{16,0},{24,8},{1,17},{9,25},{17,1},{25,9},{2,18},{10... | collective-permute-start | bytes 2359304 | tf_op jit(solution)/shard_map/ppermute | solution.py:1338
  526.2 19.3 %copy-start.23 = (bf16[2,256,2,3,64]{1,4,3,2,0:T(8,128)(2,1)S(1)}, bf16[2,256,2,3,64]{1,4,3,2,0:T(8,128)(2,1)}, u32[]{:S(2)}) copy-start(bf16[2,256,2,3,64]{1,4,3,2,0:T(8,128)(2,1)} %convert_element_type.344) | copy-start | bytes 1179652
  526.2 19.3 %copy-start.29 = (f32[256,32]{0,1:T(8,128)S(1)}, f32[256,32]{0,1:T(8,128)}, u32[]{:S(2)}) copy-start(f32[256,32]{0,1:T(8,128)} %copy-done.28) | copy-start | bytes 98308
  526.2 19.3 %copy-start.36 = (f32[256,32]{0,1:T(8,128)S(1)}, f32[256,32]{0,1:T(8,128)}, u32[]{:S(2)}) copy-start(f32[256,32]{0,1:T(8,128)} %get-tuple-element.850) | copy-start | bytes 98308
  545.5 5.8 copy-start.14
  545.5 5.8 copy-start.44
  551.3 5.9 copy-start.19
  555.7 5.3 copy-start.21
  566.2 46.8 %copy-start.9 = (bf16[2,64,1536]{2,1,0:T(8,128)(2,1)S(1)}, bf16[2,64,1536]{2,1,0:T(8,128)(2,1)}, u32[]{:S(2)}) copy-start(bf16[2,64,1536]{2,1,0:T(8,128)(2,1)} %param.20) | copy-start | bytes 1179652
  566.2 46.8 %copy-start.35 = (f32[1536]{0:T(1024)S(1)}, f32[1536]{0:T(1024)}, u32[]{:S(2)}) copy-start(f32[1536]{0:T(1024)} %copy-done.34) | copy-start | bytes 18436
  566.2 46.8 %copy-start.43 = (f32[2,64]{1,0:T(2,128)S(1)}, f32[2,64]{1,0:T(2,128)}, u32[]{:S(2)}) copy-start(f32[2,64]{1,0:T(2,128)} %copy-done.42) | copy-start | bytes 1540
  614.9 3.6 copy-start.27
  619.8 17.3 %collective-permute-start.4 = (bf16[128,1536]{1,0:T(8,128)(2,1)}, bf16[128,1536]{1,0:T(8,128)(2,1)}, u32[]{:S(2)}, u32[]{:S(2)}) collective-permute-start(bf16[128,1536]{1,0:T(8,128)(2,1)} %get-tuple-element.841), channel_id=1, source_target_pairs={{0,1},{1,2},{2,3},{3,0},{4,5},{5,6},{6,7},{7,4},{8,9},{9,10},{10,1... | collective-permute-start | bytes 1179656 | tf_op jit(solution)/shard_map/ppermute | solution.py:1381
  621.9 28.1 %collective-permute-start.5 = (bf16[128,1536]{1,0:T(8,128)(2,1)}, bf16[128,1536]{1,0:T(8,128)(2,1)}, u32[]{:S(2)}, u32[]{:S(2)}) collective-permute-start(bf16[128,1536]{1,0:T(8,128)(2,1)} %get-tuple-element.843), channel_id=1, source_target_pairs={{0,2},{1,3},{2,0},{3,1},{4,6},{5,7},{6,4},{7,5},{8,10},{9,11},{10,... | collective-permute-start | bytes 1179656 | tf_op jit(solution)/shard_map/ppermute | solution.py:1381
  621.9 12.7 %copy-start.10 = (bf16[2,64,1536]{2,1,0:T(8,128)(2,1)S(1)}, bf16[2,64,1536]{2,1,0:T(8,128)(2,1)}, u32[]{:S(2)}) copy-start(bf16[2,64,1536]{2,1,0:T(8,128)(2,1)} %param.20) | copy-start | bytes 1179652
  621.9 12.7 %copy-start.45 = (f32[128]{0:T(128)S(1)}, f32[128]{0:T(128)}, u32[]{:S(2)}) copy-start(f32[128]{0:T(128)} %rsqrt.40) | copy-start | bytes 1540
  621.9 28.1 %collective-permute-start.6 = (bf16[128,1536]{1,0:T(8,128)(2,1)}, bf16[128,1536]{1,0:T(8,128)(2,1)}, u32[]{:S(2)}, u32[]{:S(2)}) collective-permute-start(bf16[128,1536]{1,0:T(8,128)(2,1)} %get-tuple-element.842), channel_id=1, source_target_pairs={{0,3},{1,0},{2,1},{3,2},{4,7},{5,4},{6,5},{7,6},{8,11},{9,8},{10,9... | collective-permute-start | bytes 1179656 | tf_op jit(solution)/shard_map/ppermute | solution.py:1381
  633.0 17.0 %copy-start.3 = (f32[128,1536]{1,0:T(8,128)S(1)}, f32[128,1536]{1,0:T(8,128)}, u32[]{:S(2)}) copy-start(f32[128,1536]{1,0:T(8,128)} %copy-done.1) | copy-start | bytes 2359300
  (11 other events, 20.3 us)
Sparse Core Ops, SparseCore 0:
  10.8 81.7 all-gather.2
  127.8 101.3 all-gather.4
  459.0 112.6 reduce-scatter.1

commit v4 on v3

--- a/solution.py
+++ b/solution.py
@@ -70,6 +70,15 @@
 
 def near(count):
     return sorted(range(1, count), key=lambda step: min(step, count - step))
+
+
+def cut_rows(rows):
+    return (rows // 2 + 15) // 16 * 16
+
+
+def part_of(rows, side):
+    cut = cut_rows(rows)
+    return pl.ds(side * cut, rows - cut if side else cut)
 
 
 def meet(peers):
@@ -506,14 +515,15 @@
 
 def turn_kernel(cube, heads, hidden, *refs):
     chips, count = cube.chips, cube.number
-    own_ref, c_hbm, up_hbm, down_hbm = refs[:4]
+    own_ref, c_hbm, down_hbm = refs[:3]
+    pieces, refs = refs[3 : 3 + chips], (None,) * 4 + refs[3 + chips :]
     out_ref, moe_hbm, keep_up_hbm, other_up_hbm, keep_down_hbm, other_down_hbm = refs[4:10]
     tokens, turned, cots, w_up, w_down, acts, backs, d_gates, moe_stage, line_in = refs[10:20]
     arrived = refs[20 : 20 + count]
     load, store, own_sem, line_send, line_recv, send, recv, back_send, back_recv = refs[
         20 + count : 29 + count
     ]
-    end_send, end_recv, twin_send, twin_recv = refs[29 + count :]
+    end_send, end_recv, twin_send, twin_recv, load_send, load_recv = refs[29 + count :]
     hz = lax.axis_index("head")
     rows, columns = own_ref.shape
     experts_here, width, _ = w_up.shape
@@ -523,16 +533,38 @@
     others = near(heads)
     masks = sorted(range(chips), key=lambda m: bin(m).count("1"))
 
+    core = lax.axis_index("core")
+    twin = {"core": 1 - core}
+    slices = 2 * chips
+    slice_rows = width // slices
+
+    def up_rows(ref, chip, which):
+        return ref.at[:, pl.ds((chip * 2 + which) * slice_rows, slice_rows), :]
+
+    def w_down_parts(which):
+        return w_down.reshape(experts_here, 2, hidden // 2, width).at[:, which]
+
+    homes = [
+        (pieces[mask], up_rows(w_up, flip(lax.axis_index("chip"), mask), core))
+        for mask in range(chips)
+    ] + [(down_hbm, w_down_parts(core))]
     loads = [
         pltpu.make_async_copy(source, target, load.at[index])
-        for index, (source, target) in enumerate(
-            ((up_hbm, w_up), (down_hbm, w_down), (c_hbm, cots))
-        )
+        for index, (source, target) in enumerate([(c_hbm, cots)] + homes)
+    ]
+    shared = [
+        pltpu.make_async_remote_copy(
+            src_ref=source,
+            dst_ref=target,
+            send_sem=load_send.at[index],
+            recv_sem=load_recv.at[index],
+            device_id=twin,
+            device_id_type=MESH,
+        )
+        for index, (source, target) in enumerate(homes)
     ]
     for copy in loads:
         copy.start()
-    core = lax.axis_index("core")
-    twin = {"core": 1 - core}
     meet(
         [cube.peer(digit) for digit in range(count)]
         + [{"head": (hz + d) % heads} for d in others]
@@ -606,17 +638,29 @@
         k = max(k for k in range(count) if (mask >> order[k]) & 1)
         return plane_copy(side, mask & ~(1 << order[k]), k, rank)
 
-    def receive(mask):
-        for rank in range(heads):
-            if mask == 0:
-                if rank:
-                    line_copy(rank, 1).wait_recv()
-                along(rank, lambda copy: copy.start())
-            for side in range(2):
-                if mask:
-                    arrival(side, mask, rank).wait_recv()
-                for k in steps_after(side, mask):
-                    plane_copy(side, mask, k, rank).start()
+    def receive(mask, rank):
+        if mask == 0:
+            if rank:
+                line_copy(rank, 1).wait_recv()
+            along(rank, lambda copy: copy.start())
+        for side in range(2):
+            if mask:
+                arrival(side, mask, rank).wait_recv()
+            for k in steps_after(side, mask):
+                plane_copy(side, mask, k, rank).start()
+
+    levels = [
+        [m for m in masks if bin(m).count("1") == level] for level in range(cube.number + 1)
+    ]
+    waits = {0: [], 1: []}
+    early = max(heads - 2, 0)
+    for rank in range(heads):
+        waits[0].append((0, rank))
+        if 0 < rank <= early and count > 0:
+            waits[0] += [(m, rank - 1) for m in levels[1]]
+    waits[1] = [(m, rank) for rank in range(early, heads) for m in levels[1]]
+    for level in range(2, count + 1):
+        waits[level] = [(m, rank) for m in levels[level] for rank in range(heads)]
 
     def sent(mask):
         for rank in range(heads):
@@ -664,6 +708,8 @@
 
     own = pltpu.make_async_copy(own_ref, tokens.at[cube.place(0) + (hz,)], own_sem)
     own.start()
+    for copy in shared:
+        copy.start()
 
     first_expert = hz * experts_here
     span = min(512, width)
@@ -757,9 +803,8 @@
 
                 @pl.when(step == index)
                 def _():
-                    for other in masks:
-                        if bin(other).count("1") == level:
-                            receive(other)
+                    for event in waits[level]:
+                        receive(*event)
 
         place = cube.place(0)[0] * 0
         for index, mask in enumerate(masks):
@@ -768,7 +813,7 @@
         @pl.when(step == 0)
         def _():
             own.wait()
-            for copy in loads:
+            for copy in loads + shared:
                 copy.wait()
 
         compute(place)
@@ -786,12 +831,6 @@
                 def _():
                     for d in outward:
                         give(mask, d)
-
-        for index, mask in enumerate(masks[:-1]):
-
-            @pl.when(step == index)
-            def _():
-                mixed(place, step)
 
     def sums(side, steps, mask, d):
         value = back_place(side, mask, d)[...].astype(f32)
@@ -799,12 +838,6 @@
             back_copy(side, j, mask, d).wait_recv()
             value = value + arrived[j][side, slot(side, j, mask), d].astype(f32)
         return value
-
-    slices = 2 * chips
-    slice_rows = width // slices
-
-    def up_rows(ref, chip, which):
-        return ref.at[:, pl.ds((chip * 2 + which) * slice_rows, slice_rows), :]
 
     def keep_up(chip):
         return pltpu.make_async_copy(up_rows(w_up, chip, core), keep_up_hbm.at[chip], store.at[chip])
@@ -832,9 +865,6 @@
             device_id_type=MESH,
         )
 
-    def w_down_parts(which):
-        return w_down.reshape(experts_here, 2, hidden // 2, width).at[:, which]
-
     def up_grad(begin, end):
         @pl.loop(begin, end)
         def _(e):
@@ -855,12 +885,15 @@
         give_down().start()
         keep_down().start()
 
-    def last_mix():
-        mixed(cube.place(chips - 1)[0], 1)
+    def mix(begin, end):
+        @pl.loop(begin, end)
+        def _(index):
+            mixed(index, index)
 
     cuts = [experts_here * i // 4 for i in range(5)]
     work = [
-        last_mix,
+        lambda: mix(0, chips // 2),
+        lambda: mix(chips // 2, chips),
         lambda: up_grad(cuts[0], cuts[1]),
         lambda: up_grad(cuts[1], cuts[2]),
         lambda: up_grad(cuts[2], cuts[3]),
@@ -910,9 +943,10 @@
     keep_down().wait()
 
 
-def expert_turn(payload, c, w_up, w_down, chips, heads, number):
+def expert_turn(payload, c, pieces, w_down, heads, number):
     rows, columns = payload.shape
-    experts_here, width, double = w_up.shape
+    chips, width = len(pieces), c.shape[1]
+    experts_here, _, double = pieces[0].shape
     hidden = double // 2
     total = experts_here * hidden
     cube = Cube(chips, False)
@@ -932,7 +966,7 @@
             down_share,
             down_share,
         ),
-        in_specs=[WHOLE, ANY, ANY, ANY],
+        in_specs=[WHOLE] + [ANY] * (2 + chips),
         out_specs=(WHOLE, ANY, ANY, ANY, ANY, ANY),
         scratch_shapes=[
             pltpu.VMEM((chips, heads, rows, columns), bf16),
@@ -948,7 +982,7 @@
         ]
         + [pltpu.VMEM((2, s, heads, half, columns), bf16) for s in slots]
         + [
-            DMA((3,)),
+            DMA((chips + 2,)),
             DMA((chips + 2,)),
             DMA,
             DMA((heads + 1,)),
@@ -961,29 +995,36 @@
             DMA((heads - 1,)),
             DMA((chips + 1,)),
             DMA((chips + 1,)),
+            DMA((chips + 1,)),
+            DMA((chips + 1,)),
         ],
         compiler_params=pltpu.CompilerParams(
             collective_id=number, has_side_effects=True, vmem_limit_bytes=63 << 20
         ),
         name="expert_turn",
-    )(payload, c, w_up, w_down)
-
-
-def start_kernel(cube, heads, hidden, *refs):
-    x_ref, slice_ref, up_ref, down_ref, x_out, dense_out, up_out, down_out = refs[:8]
-    local, x_send, x_recv, line_send, line_recv, send, recv = refs[8:15]
-    up_send, up_recv, twin_send, twin_recv = refs[15:]
+    )(payload, c, w_down, *pieces)
+
+
+def start_kernel(cube, heads, *refs):
+    x_ref, slice_ref, unit_ref, column_ref, row_ref, x_out, dense_out, unit_out, slot_out = refs[:9]
+    local, x_send, x_recv, line_send, line_recv, send, recv, unit_send, unit_recv = refs[9:]
     chips = cube.chips
     chip, core, hz = lax.axis_index("chip"), lax.axis_index("core"), lax.axis_index("head")
-    twin = {"core": 1 - core}
     others = near(heads)
-    slice_rows = up_ref.shape[1]
-    units = up_ref.shape[2] // 2
     part_heads = heads // 2
+    across_all = {"chip": flip(chip, chips - 1)}
     meet(
-        [{"chip": flip(chip, mask)} for mask in range(1, chips)]
-        + [twin]
+        [cube.peer(digit) for digit in range(cube.number)]
         + [{"head": (hz + d) % heads} for d in others]
+        + [across_all]
+    )
+    unit_copy = pltpu.make_async_remote_copy(
+        src_ref=unit_ref,
+        dst_ref=unit_out,
+        send_sem=unit_send,
+        recv_sem=unit_recv,
+        device_id=across_all,
+        device_id_type=MESH,
     )
     middle = jnp.minimum(hz, heads - 1 - hz)
 
@@ -1060,66 +1101,30 @@
             for k in steps_after(side, mask):
                 dense_copy(side, mask, k).start()
 
-    def up_rows(mask):
-        return pl.ds((flip(chip, mask) * 2 + core) * slice_rows, slice_rows)
-
-    def unit_columns(part, mask):
-        return pl.ds(pl.multiple_of(part * units + flip(chip, mask) * hidden, hidden), hidden)
-
-    def up_copy(part, mask):
-        return pltpu.make_async_remote_copy(
-            src_ref=up_ref.at[:, :, unit_columns(part, mask)],
-            dst_ref=up_out.at[:, up_rows(0), pl.ds(part * hidden, hidden)],
-            send_sem=up_send.at[part, mask],
-            recv_sem=up_recv.at[part, mask],
-            device_id={"chip": flip(chip, mask)},
-            device_id_type=MESH,
-        )
-
-    def up_twin(mask):
-        place = up_out.at[:, up_rows(mask), :]
-        return pltpu.make_async_remote_copy(
-            src_ref=place,
-            dst_ref=place,
-            send_sem=twin_send.at[mask],
-            recv_sem=twin_recv.at[mask],
-            device_id=twin,
-            device_id_type=MESH,
-        )
-
-    down_twin = pltpu.make_async_remote_copy(
-        src_ref=down_ref,
-        dst_ref=down_out.at[:, core],
-        send_sem=twin_send.at[chips],
-        recv_sem=twin_recv.at[chips],
-        device_id=twin,
-        device_id_type=MESH,
-    )
     locals_ = [
         pltpu.make_async_copy(slice_ref.at[hz], dense_out.at[chip, core, hz], local.at[0]),
         pltpu.make_async_copy(x_ref, x_out.at[hz], local.at[1]),
-        pltpu.make_async_copy(down_ref, down_out.at[:, core], local.at[2]),
-    ] + [
-        pltpu.make_async_copy(
-            up_ref.at[:, :, unit_columns(part, 0)],
-            up_out.at[:, up_rows(0), pl.ds(part * hidden, hidden)],
-            local.at[3 + part],
-        )
-        for part in range(2)
     ]
+    def count_slots():
+        row = row_ref[...]
+        first = row // column_ref.shape[0] * column_ref.shape[0]
+        total = jnp.zeros(row.shape, jnp.int32)
+        step = LANES
+        for begin in range(0, column_ref.shape[0], step):
+            column = column_ref[pl.ds(begin, step), :]
+            earlier = ((column < row) & (column >= first)).astype(jnp.int32)
+            total = total + jnp.sum(earlier, axis=0, keepdims=True)
+        slot_out[...] = total
+
     for d in others:
         slice_copy(d).start()
     for copy in locals_:
         copy.start()
     along(0, lambda copy: copy.start())
-    down_twin.start()
     locals_[0].wait()
     for d in others:
         slice_copy(d).wait_recv()
     dense_turn(0)
-    for mask in range(1, chips):
-        for part in range(2):
-            up_copy(part, mask).start()
     masks = sorted(range(1, 2 * chips), key=lambda m: bin(m).count("1"))
     shares = [masks[len(masks) * i // heads : len(masks) * (i + 1) // heads] for i in range(heads)]
     for mask in shares[0]:
@@ -1129,18 +1134,11 @@
         along(rank, lambda copy: copy.start())
         for mask in shares[rank]:
             dense_turn(mask)
-    for copy in locals_[3:]:
-        copy.wait()
-    up_twin(0).start()
-    for mask in range(1, chips):
-        for part in range(2):
-            up_copy(part, mask).wait_recv()
-        up_twin(mask).start()
-    for copy in locals_[1:3]:
-        copy.wait()
-    down_twin.wait()
-    for mask in range(chips):
-        up_twin(mask).wait()
+        if rank == 1:
+            unit_copy.start()
+            count_slots()
+    unit_copy.wait()
+    locals_[1].wait()
     for rank in range(heads):
         along(rank, lambda copy: copy.wait_send())
     for d in others:
@@ -1149,41 +1147,34 @@
         for side in range(2):
             for k in steps_after(side, mask):
                 dense_copy(side, mask, k).wait_send()
-    for mask in range(1, chips):
-        for part in range(2):
-            up_copy(part, mask).wait_send()
-
-
-def start(x, slices, w_gate_up, w_down, chips, heads, hidden, number):
+
+
+def start(x, slices, unit, keys, chips, heads, number):
     cube = Cube(chips, True)
-    experts_here, slice_rows, _ = w_gate_up.shape
-    width = slice_rows * 2 * chips
     return pl.pallas_call(
-        functools.partial(start_kernel, cube, heads, hidden),
+        functools.partial(start_kernel, cube, heads),
         out_shape=(
             jax.ShapeDtypeStruct((heads,) + x.shape, bf16),
             jax.ShapeDtypeStruct((chips, 2) + slices.shape, bf16),
-            jax.ShapeDtypeStruct((experts_here, width, 2 * hidden), bf16),
-            jax.ShapeDtypeStruct((experts_here, 2) + w_down.shape[1:], bf16),
+            jax.ShapeDtypeStruct(unit.shape, bf16),
+            jax.ShapeDtypeStruct((1, keys.size), jnp.int32),
         ),
-        in_specs=[ANY] * 4,
-        out_specs=(ANY,) * 4,
+        in_specs=[ANY] * 3 + [WHOLE] * 2,
+        out_specs=(ANY,) * 3 + (WHOLE,),
         scratch_shapes=[
-            DMA((5,)),
+            DMA((2,)),
             DMA((heads + 1,)),
             DMA((heads,)),
             DMA((heads - 1,)),
             DMA((heads - 1,)),
             DMA((2, 2 * chips)),
             DMA((2, 2 * chips)),
-            DMA((2, chips)),
-            DMA((2, chips)),
-            DMA((chips + 1,)),
-            DMA((chips + 1,)),
+            DMA,
+            DMA,
         ],
         compiler_params=pltpu.CompilerParams(collective_id=number, has_side_effects=True),
         name="start",
-    )(x, slices, w_gate_up, w_down)
+    )(x, slices, unit, keys[:, None], keys[None, :])
 
 
 def end_kernel(cube, heads, first_ref, in_ref, first_out, out_ref, *refs):
@@ -1338,58 +1329,628 @@
     return lax.ppermute(value, "chip", [(i, i ^ mask) for i in range(chips)])
 
 
-class Sums:
-    def __init__(self, blocks):
-        self.chips, self.heads = blocks.shape[:2]
-        rows, columns = blocks.shape[2:]
-        self.sides = blocks.reshape(self.chips, self.heads, 2, rows // 2, columns)
-        self.cube = Cube(self.chips, False)
-        self.arrived = {}
-        self.shape = (rows, columns)
-
-    def block(self, side, mask, steps):
-        chip = lax.axis_index("chip")
-        value = lax.dynamic_index_in_dim(self.sides[:, :, side], chip ^ mask, 0, keepdims=False)
-        value = value.astype(f32)
+class LineGather:
+    def __init__(self, cube, heads, own, out, sems):
+        self.cube, self.heads, self.own, self.out = cube, heads, own, out
+        self.local, self.line_send, self.line_recv, self.send, self.recv = sems
+        self.hz = lax.axis_index("head")
+        self.middle = jnp.minimum(self.hz, heads - 1 - self.hz)
+        self.rows = own.shape[0]
+
+    @staticmethod
+    def scratch(cube, heads):
+        return [
+            DMA,
+            DMA((heads + 1,)),
+            DMA((heads,)),
+            DMA((2, 1 << cube.number, heads)),
+            DMA((2, 1 << cube.number, heads)),
+        ]
+
+    def source(self, rank):
+        hz, heads, middle = self.hz, self.heads, self.middle
+        if rank == 0:
+            return hz
+        far = (rank + 1) // 2
+        near_one = hz - far if rank % 2 else hz + far
+        far_one = jnp.where(hz < heads - 1 - hz, hz + (rank - middle), hz - (rank - middle))
+        return jnp.where(rank <= 2 * middle, near_one, far_one)
+
+    def line_copy(self, rank, step):
+        head = self.source(rank)
+        place = self.out.at[self.cube.place(0) + (head,)]
+        return pltpu.make_async_remote_copy(
+            src_ref=self.own if rank == 0 else place,
+            dst_ref=place,
+            send_sem=self.line_send.at[self.heads if rank == 0 and step < 0 else head],
+            recv_sem=self.line_recv.at[head],
+            device_id={"head": (self.hz + step + self.heads) % self.heads},
+            device_id_type=MESH,
+        )
+
+    def along(self, rank, act):
+        head = self.source(rank)
+        goes_up = self.hz + 1 < self.heads
+        goes_down = self.hz > 0
+        if rank:
+            goes_up = goes_up & (head < self.hz)
+            goes_down = goes_down & (head > self.hz)
+
+        @pl.when(goes_up)
+        def _():
+            act(self.line_copy(rank, 1))
+
+        @pl.when(goes_down)
+        def _():
+            act(self.line_copy(rank, -1))
+
+    def plane_copy(self, side, mask, k, rank):
+        digit = self.cube.gather_orders[side][k]
+        later = mask | (1 << digit)
+        head = self.source(rank)
+        part = part_of(self.rows, side)
+        place = self.out.at[self.cube.place(mask) + (head, part)]
+        return pltpu.make_async_remote_copy(
+            src_ref=self.own.at[part] if mask == 0 and rank == 0 else place,
+            dst_ref=place,
+            send_sem=self.send.at[side, later, head],
+            recv_sem=self.recv.at[side, later, head],
+            device_id=self.cube.peer(digit),
+            device_id_type=MESH,
+        )
+
+    def steps_after(self, side, mask):
+        order = self.cube.gather_orders[side]
+        last = max([k for k in range(self.cube.number) if (mask >> order[k]) & 1], default=-1)
+        return range(last + 1, self.cube.number)
+
+    def begin(self):
+        self.own_copy = pltpu.make_async_copy(
+            self.own, self.out.at[self.cube.place(0) + (self.hz,)], self.local
+        )
+        self.own_copy.start()
+
+    def receive(self, mask, rank):
+        if mask == 0:
+            if rank:
+                self.line_copy(rank, 1).wait_recv()
+            self.along(rank, lambda copy: copy.start())
+        for side in range(2):
+            if mask:
+                order = self.cube.gather_orders[side]
+                k = max(k for k in range(self.cube.number) if (mask >> order[k]) & 1)
+                self.plane_copy(side, mask & ~(1 << order[k]), k, rank).wait_recv()
+            for k in self.steps_after(side, mask):
+                self.plane_copy(side, mask, k, rank).start()
+
+    def events(self):
+        masks = sorted(range(1 << self.cube.number), key=lambda m: bin(m).count("1"))
+        return [(mask, rank) for mask in masks for rank in range(self.heads)]
+
+    def finish(self):
+        self.own_copy.wait()
+        for mask, rank in self.events():
+            if mask == 0:
+                self.along(rank, lambda copy: copy.wait_send())
+            for side in range(2):
+                for k in self.steps_after(side, mask):
+                    self.plane_copy(side, mask, k, rank).wait_send()
+
+
+class LineSums:
+    def __init__(self, cube, heads, blocks, out, refs):
+        self.cube, self.heads, self.blocks, self.out = cube, heads, blocks, out
+        count = cube.number
+        self.arrived, self.parts = refs[:count], refs[count : 2 * count - 1]
+        self.line_out, self.line_in, self.send, self.recv, self.end_send, self.end_recv = refs[
+            2 * count - 1 :
+        ]
+        self.hz = lax.axis_index("head")
+        self.rows = blocks.shape[-2]
+        self.outward = near(heads)[::-1] + [0]
+        self.turns = heads + count
+
+    @staticmethod
+    def scratch(cube, heads, rows, columns):
+        count = cube.number
+        slots = [(1 << count) >> (k + 1) for k in range(count)]
+        half = cut_rows(rows)
+        return (
+            [pltpu.VMEM((2, s, heads, half, columns), bf16) for s in slots]
+            + [pltpu.VMEM((2, s, heads, half, columns), bf16) for s in slots[1:]]
+            + [
+                pltpu.VMEM((heads - 1, rows, columns), bf16),
+                pltpu.VMEM((heads - 1, rows, columns), bf16),
+                DMA((2, count, slots[0], heads)),
+                DMA((2, count, slots[0], heads)),
+                DMA((heads - 1,)),
+                DMA((heads - 1,)),
+            ]
+        )
+
+    def slot(self, side, k, mask):
+        return subsets(self.cube.scatter_orders[side][k + 1 :]).index(mask)
+
+    def mine(self, side, mask, d):
+        place = self.cube.place(mask) + ((self.hz + d) % self.heads,)
+        return self.blocks.at[place + (part_of(self.rows, side),)]
+
+    def there(self, ref, side, where, d):
+        return ref.at[side, where, d, pl.ds(0, part_of(self.rows, side).size)]
+
+    def copy_of(self, side, k, mask, d):
+        order = self.cube.scatter_orders[side]
+        where = self.slot(side, k, mask)
+        if k == 0:
+            piece = self.mine(side, mask | (1 << order[0]), d)
+        else:
+            piece = self.there(self.parts[k - 1], side, where, d)
+        return pltpu.make_async_remote_copy(
+            src_ref=piece,
+            dst_ref=self.there(self.arrived[k], side, where, d),
+            send_sem=self.send.at[side, k, where, d],
+            recv_sem=self.recv.at[side, k, where, d],
+            device_id=self.cube.peer(order[k]),
+            device_id_type=MESH,
+        )
+
+    def end_copy(self, d):
+        return pltpu.make_async_remote_copy(
+            src_ref=self.line_out.at[d - 1],
+            dst_ref=self.line_in.at[d - 1],
+            send_sem=self.end_send.at[d - 1],
+            recv_sem=self.end_recv.at[d - 1],
+            device_id={"head": (self.hz + d) % self.heads},
+            device_id_type=MESH,
+        )
+
+    def sums(self, side, steps, mask, d):
+        value = self.mine(side, mask, d)[...].astype(f32)
         for j in range(steps):
-            order = self.cube.scatter_orders[side]
-            where = subsets(order[j + 1 :]).index(mask)
-            value = value + self.arrived[(side, j)][where].astype(f32)
+            self.copy_of(side, j, mask, d).wait_recv()
+            value = value + self.there(self.arrived[j], side, self.slot(side, j, mask), d)[
+                ...
+            ].astype(f32)
         return value
 
-    def plane(self, k):
+    def turn(self, turn):
+        count = self.cube.number
+        if turn < self.heads:
+            for side in range(2):
+                for mask in subsets(self.cube.scatter_orders[side][1:])[::-1]:
+                    self.copy_of(side, 0, mask, self.outward[turn]).start()
+        for k in range(1, count):
+            if 0 <= turn - k < self.heads:
+                d = self.outward[turn - k]
+                for side in range(2):
+                    order = self.cube.scatter_orders[side]
+                    for mask in subsets(order[k + 1 :])[::-1]:
+                        value = self.sums(side, k, mask | (1 << order[k]), d)
+                        place = self.there(self.parts[k - 1], side, self.slot(side, k, mask), d)
+                        place[...] = value.astype(bf16)
+                        self.copy_of(side, k, mask, d).start()
+        if 0 <= turn - count < self.heads:
+            d = self.outward[turn - count]
+            for side in range(2):
+                value = self.sums(side, count, 0, d)
+                part = part_of(self.rows, side)
+                if d:
+                    self.line_out[d - 1, part] = value.astype(bf16)
+                else:
+                    self.out[part] = value
+            if d:
+                self.end_copy(d).start()
+
+    def finish(self):
+        others = near(self.heads)
+        for d in others:
+            self.end_copy(d).wait_recv()
+            self.out[...] += self.line_in[d - 1].astype(f32)
+        for d in others:
+            self.end_copy(d).wait_send()
         for side in range(2):
-            order = self.cube.scatter_orders[side]
-            give = jnp.stack(
-                [
-                    self.block(side, mask | (1 << order[k]), k).astype(bf16)
-                    for mask in subsets(order[k + 1 :])
-                ]
+            for k in range(self.cube.number):
+                for mask in subsets(self.cube.scatter_orders[side][k + 1 :]):
+                    for d in self.outward:
+                        self.copy_of(side, k, mask, d).wait_send()
+
+
+TN = (((0,), (0,)), ((), ()))
+
+
+def allowed(key_segments, query_segments, block, rows, seq):
+    columns = query_segments.shape[1]
+    key_place = block * rows + lax.broadcasted_iota(jnp.int32, (rows, columns), 0)
+    query_place = seq * rows + lax.broadcasted_iota(jnp.int32, (rows, columns), 1) % rows
+    return (key_segments == query_segments) & (key_place <= query_place)
+
+
+def attend_kernel(cube, heads, group, beside, *refs):
+    q_ref, kv_ref, key_seg, query_seg = refs[:4]
+    near_refs, refs = refs[4 : 4 + len(beside)], refs[4 + len(beside) :]
+    lines_ref, kv_out, out_turned, lse_ref = refs[:4]
+    far_refs, refs = refs[4 : 4 + len(beside)], refs[4 + len(beside) :]
+    stage, top, total, acc, send, recv, line_send, line_recv = refs[:8]
+    chip, core, hz = lax.axis_index("chip"), lax.axis_index("core"), lax.axis_index("head")
+    seq = chip * 2 + core
+    others = near(heads)[::-1]
+    batch, rows, columns = kv_ref.shape
+    kv_heads = columns // (2 * HEAD_WIDTH)
+    part = rows // 2
+    meet([cube.peer(digit) for digit in range(cube.number)] + [{"head": (hz + d) % heads} for d in others])
+    kv_out[chip, core] = kv_ref[...]
+    gathers = [
+        LineGather(Cube(cube.chips, with_core), heads, *pair, refs[8 + 5 * i : 13 + 5 * i])
+        for i, (with_core, pair) in enumerate(zip(beside, zip(near_refs, far_refs)))
+    ]
+    events = sorted(
+        (
+            ((index + 0.5) / len(one.events()), one, event)
+            for one in gathers
+            for index, event in enumerate(one.events())
+        ),
+        key=lambda item: item[0],
+    )
+
+    def copy_of(side, mask, k):
+        order = cube.gather_orders[side]
+        later = mask | (1 << order[k])
+        place = cube.place(mask) + (slice(None), pl.ds(side * part, part))
+        return pltpu.make_async_remote_copy(
+            src_ref=kv_ref.at[:, pl.ds(side * part, part)] if mask == 0 else kv_out.at[place],
+            dst_ref=kv_out.at[place],
+            send_sem=send.at[side, later],
+            recv_sem=recv.at[side, later],
+            device_id=cube.peer(order[k]),
+            device_id_type=MESH,
+        )
+
+    copies = []
+
+    def forward(mask):
+        for side in range(2):
+            order = cube.gather_orders[side]
+            last = max([k for k in range(cube.number) if (mask >> order[k]) & 1], default=-1)
+            if mask:
+                copy_of(side, mask & ~(1 << order[last]), last).wait_recv()
+            for k in range(last + 1, cube.number):
+                copy_of(side, mask, k).start()
+                copies.append((side, mask, k))
+
+    forward(0)
+    top[...] = jnp.full_like(top, negative)
+    total[...] = jnp.zeros_like(total)
+    acc[...] = jnp.zeros_like(acc)
+
+    def block_step(block):
+        place = (block // 2, block % 2)
+        for b in range(batch):
+            mask = allowed(
+                key_seg[b, pl.ds(pl.multiple_of(block * rows, rows), rows), :],
+                query_seg[b],
+                block,
+                rows,
+                seq,
             )
-            self.arrived[(side, k)] = across(give, self.chips, 1 << order[k])
-
-    def along(self):
-        count = self.cube.number
-        whole = jnp.concatenate([self.block(side, 0, count) for side in range(2)], axis=1)
-        head = lax.axis_index("head")
-        self.own = lax.dynamic_index_in_dim(whole, head, 0, keepdims=False)
-        whole = whole.astype(bf16)
-        self.line = []
-        for d in range(1, self.heads):
-            give = lax.dynamic_index_in_dim(whole, (head + d) % self.heads, 0, keepdims=False)
-            pairs = [(i, (i + d) % self.heads) for i in range(self.heads)]
-            self.line.append(lax.ppermute(give, "head", pairs))
-
-    def result(self):
-        return self.own + sum(value.astype(f32) for value in self.line)
-
-
-def pin(sums, value):
-    keys = list(sums.arrived)
-    out = lax.optimization_barrier((value, [sums.arrived[key] for key in keys]))
-    for key, kept in zip(keys, out[1]):
-        sums.arrived[key] = kept
-    return out[0]
+            for j in range(kv_heads):
+                pair = b * kv_heads + j
+                begin = j * 2 * HEAD_WIDTH
+                keys = kv_out[place + (b, slice(None), pl.ds(begin, HEAD_WIDTH))]
+                values = kv_out[place + (b, slice(None), pl.ds(begin + HEAD_WIDTH, HEAD_WIDTH))]
+                scores = lax.dot_general(keys, q_ref[pair], NT, preferred_element_type=f32)
+                scores = jnp.where(mask, scores, negative)
+                new = jnp.maximum(top[pair], jnp.max(scores, axis=0, keepdims=True))
+                weights = jnp.exp(scores - new)
+                shrink = jnp.exp(top[pair] - new)
+                top[pair] = new
+                total[pair] = total[pair] * shrink + jnp.sum(weights, axis=0, keepdims=True)
+                acc[pair] = acc[pair] * shrink + lax.dot_general(
+                    values, weights.astype(bf16), TN, preferred_element_type=f32
+                )
+
+    block_step(seq)
+    for one in gathers:
+        one.begin()
+    for _, one, event in events[: len(gathers)]:
+        one.receive(*event)
+    for mask in sorted(range(1, 1 << cube.number), key=lambda m: bin(m).count("1")):
+        forward(mask)
+    turns = 2 * cube.chips
+    skip = len(gathers)
+    rest = len(events) - skip
+    if beside:
+        for turn in range(turns):
+            for _, one, event in events[
+                skip + rest * turn // turns : skip + rest * (turn + 1) // turns
+            ]:
+                one.receive(*event)
+
+            @pl.when(turn < seq)
+            def _():
+                block_step(turn)
+
+    else:
+
+        @pl.loop(0, seq)
+        def _(block):
+            block_step(block)
+
+    spot = rows // heads
+    for b in range(batch):
+        for j in range(kv_heads):
+            pair = b * kv_heads + j
+            value = acc[pair] / total[pair]
+            out_turned[pair] = value
+            lse_ref[pair] = top[pair] + jnp.log(total[pair])
+            value = value.T.astype(bf16)
+            for g in range(group):
+                for head in range(heads):
+                    begin = (j * group + g) * HEAD_WIDTH
+                    stage[head, pl.ds(b * spot, spot), pl.ds(begin, HEAD_WIDTH)] = value[
+                        g * rows + head * spot : g * rows + (head + 1) * spot
+                    ]
+
+    def line_copy(d):
+        return pltpu.make_async_remote_copy(
+            src_ref=stage.at[(hz + d) % heads],
+            dst_ref=lines_ref.at[hz],
+            send_sem=line_send.at[d - 1],
+            recv_sem=line_recv.at[d - 1],
+            device_id={"head": (hz + d) % heads},
+            device_id_type=MESH,
+        )
+
+    for d in others:
+        line_copy(d).start()
+    lines_ref[hz] = stage[hz]
+    for side, mask, k in copies:
+        copy_of(side, mask, k).wait_send()
+    for d in others:
+        line_copy(d).wait()
+    for one in gathers:
+        one.finish()
+
+
+def attend(queries, keys_values, key_seg, query_seg, beside, chips, heads, group, number):
+    batch, rows, columns = keys_values.shape
+    pairs, wide, depth = queries.shape
+    cube = Cube(chips, True)
+    group_columns = group * columns // 2
+    tokens = batch * rows // heads
+    return pl.pallas_call(
+        functools.partial(attend_kernel, cube, heads, group, [core for _, core in beside]),
+        out_shape=(
+            jax.ShapeDtypeStruct((heads, tokens, group_columns), bf16),
+            jax.ShapeDtypeStruct((chips, 2, batch, rows, columns), bf16),
+            jax.ShapeDtypeStruct((pairs, depth, wide), f32),
+            jax.ShapeDtypeStruct((pairs, 1, wide), f32),
+        )
+        + tuple(
+            jax.ShapeDtypeStruct((chips,) + (2,) * with_core + (heads,) + value.shape, bf16)
+            for value, with_core in beside
+        ),
+        in_specs=[WHOLE] * 4 + [ANY] * len(beside),
+        out_specs=(WHOLE,) * 4 + (ANY,) * len(beside),
+        scratch_shapes=[
+            pltpu.VMEM((heads, tokens, group_columns), bf16),
+            pltpu.VMEM((pairs, 1, wide), f32),
+            pltpu.VMEM((pairs, 1, wide), f32),
+            pltpu.VMEM((pairs, depth, wide), f32),
+            DMA((2, 2 * chips)),
+            DMA((2, 2 * chips)),
+            DMA((heads - 1,)),
+            DMA((heads - 1,)),
+        ]
+        + [item for _, core in beside for item in LineGather.scratch(Cube(chips, core), heads)],
+        compiler_params=pltpu.CompilerParams(
+            collective_id=number, has_side_effects=True, vmem_limit_bytes=50 << 20
+        ),
+        name="attend",
+    )(queries, keys_values, key_seg, query_seg, *[value for value, _ in beside])
+
+
+def attend_back_kernel(cube, heads, group, beside, *refs):
+    q_ref, kv_ref, key_seg, query_seg, out_turned, lse_ref, dh_ref = refs[:7]
+    near_refs, refs = refs[7 : 7 + len(beside)], refs[7 + len(beside) :]
+    dq_ref, dkv_ref = refs[:2]
+    far_refs, refs = refs[2 : 2 + len(beside)], (None,) * 9 + refs[2 + len(beside) :]
+    count = cube.number
+    landed, d_out, delta, dq_turned, grads = refs[9:14]
+    arrived, parts = refs[14 : 14 + count], refs[14 + count : 13 + 2 * count]
+    send, recv, line_send, line_recv = refs[13 + 2 * count : 17 + 2 * count]
+    turns = 2 * cube.chips
+    rest = refs[17 + 2 * count :]
+    sums_beside = []
+    for with_core, source, target in zip(beside, near_refs, far_refs):
+        own_cube = Cube(cube.chips, with_core)
+        size = 2 * own_cube.number + 5
+        sums_beside.append(LineSums(own_cube, heads, source, target, rest[:size]))
+        rest = rest[size:]
+    chip, core, hz = lax.axis_index("chip"), lax.axis_index("core"), lax.axis_index("head")
+    seq = chip * 2 + core
+    others = near(heads)[::-1]
+    batch, rows, columns = kv_ref.shape[2:]
+    kv_heads = columns // (2 * HEAD_WIDTH)
+    spot = rows // heads
+    half = grads.shape[2] // 2
+    meet([cube.peer(digit) for digit in range(count)] + [{"head": (hz + d) % heads} for d in others])
+
+    def line_copy(d):
+        return pltpu.make_async_remote_copy(
+            src_ref=dh_ref.at[(hz + d) % heads],
+            dst_ref=landed.at[hz],
+            send_sem=line_send.at[d - 1],
+            recv_sem=line_recv.at[d - 1],
+            device_id={"head": (hz + d) % heads},
+            device_id_type=MESH,
+        )
+
+    for d in others:
+        line_copy(d).start()
+    for one in sums_beside:
+        one.turn(0)
+    landed[hz] = dh_ref[hz]
+    grads[...] = jnp.zeros_like(grads)
+    dq_turned[...] = jnp.zeros_like(dq_turned)
+    for d in others:
+        line_copy(d).wait()
+    for b in range(batch):
+        for j in range(kv_heads):
+            pair = b * kv_heads + j
+            for g in range(group):
+                for head in range(heads):
+                    begin = (j * group + g) * HEAD_WIDTH
+                    d_out[pair, pl.ds(g * rows + head * spot, spot), :] = landed[
+                        head, pl.ds(b * spot, spot), pl.ds(begin, HEAD_WIDTH)
+                    ]
+            delta[pair] = jnp.sum(
+                d_out[pair].astype(f32).T * out_turned[pair], axis=0, keepdims=True
+            )
+
+    def block_step(block):
+        place = (block // 2, block % 2)
+        for b in range(batch):
+            mask = allowed(
+                key_seg[b, pl.ds(pl.multiple_of(block * rows, rows), rows), :],
+                query_seg[b],
+                block,
+                rows,
+                seq,
+            )
+            for j in range(kv_heads):
+                pair = b * kv_heads + j
+                begin = j * 2 * HEAD_WIDTH
+                keys = kv_ref[place + (b, slice(None), pl.ds(begin, HEAD_WIDTH))]
+                values = kv_ref[place + (b, slice(None), pl.ds(begin + HEAD_WIDTH, HEAD_WIDTH))]
+                scores = lax.dot_general(keys, q_ref[pair], NT, preferred_element_type=f32)
+                probs = jnp.exp(jnp.where(mask, scores, negative) - lse_ref[pair])
+                d_probs = lax.dot_general(values, d_out[pair], NT, preferred_element_type=f32)
+                d_scores = (probs * (d_probs - delta[pair])).astype(bf16)
+                dq_turned[pair] += lax.dot_general(
+                    keys, d_scores, TN, preferred_element_type=f32
+                )
+                d_keys = jnp.dot(d_scores, q_ref[pair], preferred_element_type=f32)
+                d_values = jnp.dot(probs.astype(bf16), d_out[pair], preferred_element_type=f32)
+                grads[place + (pl.ds(b * rows, rows), pl.ds(begin, 2 * HEAD_WIDTH))] = (
+                    jnp.concatenate([d_keys, d_values], axis=1).astype(bf16)
+                )
+
+    done = 1
+    if beside:
+        for turn in range(turns):
+
+            @pl.when(turn <= seq)
+            def _():
+                block_step(turn)
+
+            if turn % 3 == 2:
+                for one in sums_beside:
+                    one.turn(done)
+                done += 1
+
+    else:
+
+        @pl.loop(0, seq + 1)
+        def _(block):
+            block_step(block)
+
+    def slot(side, k, mask):
+        return subsets(cube.scatter_orders[side][k + 1 :]).index(mask)
+
+    def mine(side, mask):
+        return grads.at[cube.place(mask) + (pl.ds(side * half, half),)]
+
+    copies = {}
+
+    def sums(side, steps, mask):
+        value = mine(side, mask)[...].astype(f32)
+        for j in range(steps):
+            copies[(side, j, mask)].wait_recv()
+            value = value + arrived[j][side, slot(side, j, mask)].astype(f32)
+        return value
+
+    for k in range(count):
+        for side in range(2):
+            order = cube.scatter_orders[side]
+            for mask in subsets(order[k + 1 :])[::-1]:
+                full = mask | (1 << order[k])
+                where = slot(side, k, mask)
+                if k == 0:
+                    piece = mine(side, full)
+                else:
+                    piece = parts[k - 1].at[side, where]
+                    piece[...] = sums(side, k, full).astype(bf16)
+                copies[(side, k, mask)] = pltpu.make_async_remote_copy(
+                    src_ref=piece,
+                    dst_ref=arrived[k].at[side, where],
+                    send_sem=send.at[side, k, where],
+                    recv_sem=recv.at[side, k, where],
+                    device_id=cube.peer(order[k]),
+                    device_id_type=MESH,
+                )
+                copies[(side, k, mask)].start()
+        for one in sums_beside:
+            if done < one.turns:
+                one.turn(done)
+        done += 1
+    scale = HEAD_WIDTH ** (-0.5)
+    for pair in range(batch * kv_heads):
+        dq_ref[pair] = (dq_turned[pair] * scale).T.astype(bf16)
+    for side in range(2):
+        dkv_ref[pl.ds(side * half, half)] = sums(side, count, 0)
+    for turn in range(done, max([one.turns for one in sums_beside], default=0)):
+        for one in sums_beside:
+            if turn < one.turns:
+                one.turn(turn)
+    for copy in copies.values():
+        copy.wait_send()
+    for one in sums_beside:
+        one.finish()
+
+
+def attend_back(
+    queries, kv_all, key_seg, query_seg, out_turned, lse, d_heads, beside, heads, group, number
+):
+    chips, _, batch, rows, columns = kv_all.shape
+    pairs, wide, depth = queries.shape
+    cube = Cube(chips, True)
+    count = cube.number
+    half = batch * rows // 2
+    slots = [(1 << count) >> (k + 1) for k in range(count)]
+    return pl.pallas_call(
+        functools.partial(attend_back_kernel, cube, heads, group, [core for _, core in beside]),
+        out_shape=(
+            jax.ShapeDtypeStruct((pairs, wide, depth), bf16),
+            jax.ShapeDtypeStruct((batch * rows, columns), f32),
+        )
+        + tuple(jax.ShapeDtypeStruct(value.shape[-2:], f32) for value, _ in beside),
+        in_specs=[WHOLE] * (7 + len(beside)),
+        out_specs=(WHOLE,) * (2 + len(beside)),
+        scratch_shapes=[
+            pltpu.VMEM(d_heads.shape, bf16),
+            pltpu.VMEM((pairs, wide, depth), bf16),
+            pltpu.VMEM((pairs, 1, wide), f32),
+            pltpu.VMEM((pairs, depth, wide), f32),
+            pltpu.VMEM((chips, 2, batch * rows, columns), bf16),
+        ]
+        + [pltpu.VMEM((2, s, half, columns), bf16) for s in slots]
+        + [pltpu.VMEM((2, s, half, columns), bf16) for s in slots[1:]]
+        + [
+            DMA((2, count, slots[0])),
+            DMA((2, count, slots[0])),
+            DMA((heads - 1,)),
+            DMA((heads - 1,)),
+        ]
+        + [
+            item
+            for value, core in beside
+            for item in LineSums.scratch(Cube(chips, core), *value.shape[-3:])
+        ],
+        compiler_params=pltpu.CompilerParams(
+            collective_id=number, has_side_effects=True, vmem_limit_bytes=56 << 20
+        ),
+        name="attend_back",
+    )(queries, kv_all, key_seg, query_seg, out_turned, lse, d_heads, *[v for v, _ in beside])
 
 
 def sibling(value):
@@ -1443,12 +2004,20 @@
     own_tokens = layer_input.reshape(tokens_present, width)
     cots = cotangent.reshape(tokens_present, width)
     if fused:
-        x_line, dense, expert_up, expert_down = start(
-            own_tokens, slices, w_gate_up, w_down, chips, head_number, hidden, 1
-        )
-        expert_down = expert_down.reshape(loc_experts * hidden, width)
+
+        def unit_of(weights, mask):
+            begins = [part * FF + (chip ^ mask) * hidden for part in range(2)]
+            cut = [lax.dynamic_slice_in_dim(weights, begin, hidden, 2) for begin in begins]
+            return jnp.concatenate(cut, axis=2)
+
+        keys = (routes * pairs + pair_rank).reshape(pairs)
+        x_line, dense, last_unit, slot = start(
+            own_tokens, slices, unit_of(w_gate_up, chips - 1), keys, chips, head_number, 1
+        )
+        x_line, w_gate_up = lax.optimization_barrier((x_line, w_gate_up))
+        units = [across(unit_of(w_gate_up, mask), chips, mask) for mask in range(chips - 1)]
+        units.append(last_unit)
         dense = dense.reshape(width, loc_columns + LANES)
-        cots, x_line = lax.optimization_barrier((cots, x_line))
     else:
         parts = w_gate_up.reshape(loc_experts, slice_rows, 2, chips, hidden).transpose(3, 2, 1, 0, 4)
         parts = parts.reshape(chips, 2, slice_rows, loc_experts * hidden)
@@ -1476,8 +2045,9 @@
         ).reshape(width, loc_columns + LANES)
         x_line = line_exchange(layer_input.reshape(tokens_present, width), head_number, 3, True)
 
-    grad_all = lax.all_gather(cots, ("chip", "head"), axis=0, tiled=True)
-    dense_out = lax.all_gather(output_weight, ("chip", "core", "head"), axis=0, tiled=True)
+    if not fused:
+        grad_all = lax.all_gather(cots, ("chip", "head"), axis=0, tiled=True)
+        dense_out = lax.all_gather(output_weight, ("chip", "core", "head"), axis=0, tiled=True)
 
     dense_qkv = dense[:, :loc_columns]
     dense_router = dense[:, loc_columns : loc_columns + EXPERTS]
@@ -1518,77 +2088,32 @@
         .reshape(sequence_batch * blk, key_value_location * 2 * HEAD_WIDTH)
     )
     kv_columns = key_value_location * 2 * HEAD_WIDTH
-    kv_all = (
-        gather(keys_values, chips, 1, True, 4)
-        .reshape(2 * chips, sequence_batch, blk, kv_columns)
-        .transpose(1, 0, 2, 3)
-        .reshape(sequence_batch, length, kv_columns)
+    pairs_here = sequence_batch * key_value_location
+    group_columns = key_value_location * query_group * HEAD_WIDTH
+    queries = (
+        (query_rows.astype(f32) * scale)
+        .astype(bf16)
+        .transpose(0, 2, 3, 1, 4)
+        .reshape(pairs_here, query_group * blk, HEAD_WIDTH)
     )
+    key_seg = segments[:, :, None]
     q_seg = lax.dynamic_slice_in_dim(segments, q_start, blk, 1)
-
-    def key_view(piece, offset, token_count):
-        portion = lax.dynamic_slice_in_dim(piece, offset, token_count, 1).reshape(
-            sequence_batch, token_count, key_value_location, 2, HEAD_WIDTH
-        )
-        return (portion[:, :, :, 0], portion[:, :, :, 1])
-
-    def key_mask(begin, token_count):
-        k_pos = begin + jnp.arange(token_count, dtype=jnp.int32)
-        k_seg = lax.dynamic_slice_in_dim(segments, begin, token_count, 1)
-        same = q_seg[:, :, None] == k_seg[:, None, :]
-        causal = k_pos[None, None, :] <= q_pos[None, :, None]
-        return (same & causal)[:, None, None]
-
-    def sweep(function, state):
-        sub = 512
-
-        def turn(index, inner):
-            offset = index * sub
-            return lax.cond(
-                offset <= q_start + blk - 1,
-                lambda now: function(now, kv_all, offset, sub),
-                lambda now: now,
-                inner,
-            )
-
-        return lax.fori_loop(0, length // sub, turn, state)
-
-    def forward_block(state, piece, offset, token_count):
-        top_now, total, accum = state
-        keys, values = key_view(piece, offset, token_count)
-        scores = (
-            jnp.einsum("sqhgd,skhd->shgqk", query_rows, keys, preferred_element_type=f32) * scale
-        )
-        mask = key_mask(offset, token_count)
-        scores = jnp.where(mask, scores, negative)
-        top_new = jnp.maximum(top_now, jnp.max(scores, axis=-1))
-        weights = jnp.where(mask, jnp.exp(scores - top_new[..., None]), 0.0)
-        shrink = jnp.exp(top_now - top_new)
-        total = total * shrink + jnp.sum(weights, axis=-1)
-        accum = accum * shrink[..., None] + jnp.einsum(
-            "shgqk,skhd->shgqd", weights.astype(bf16), values, preferred_element_type=f32
-        )
-        return (top_new, total, accum)
-
-    state_zero = (
-        jnp.full((sequence_batch, key_value_location, query_group, blk), negative, f32),
-        jnp.zeros((sequence_batch, key_value_location, query_group, blk), f32),
-        jnp.zeros((sequence_batch, key_value_location, query_group, blk, HEAD_WIDTH), f32),
+    query_seg = jnp.tile(q_seg[:, None, :], (1, 1, query_group))
+    lines, kv_all, out_turned, lse, *beside = attend(
+        queries,
+        keys_values.reshape(sequence_batch, blk, kv_columns),
+        key_seg,
+        query_seg,
+        [(output_weight, True), (cots, False)] if fused else [],
+        chips,
+        head_number,
+        query_group,
+        4,
     )
-    top_now, total, accum = sweep(forward_block, state_zero)
-    lse = top_now + jnp.log(total)
-    attended = accum / total[..., None]
-    group_columns = key_value_location * query_group * HEAD_WIDTH
-    heads_local = to_lines(
-        attended.transpose(0, 3, 1, 2, 4).reshape(sequence_batch, blk, group_columns).astype(bf16)
-    )
-    mixed_heads = (
-        line_exchange(
-            heads_local.reshape(head_number, tokens_present, group_columns), head_number, 5
-        )
-        .transpose(1, 0, 2)
-        .reshape(tokens_present, QUERY_HEADS * HEAD_WIDTH)
-    )
+    if fused:
+        dense_out = beside[0].reshape(QUERY_HEADS * HEAD_WIDTH, width)
+        grad_all = beside[1].reshape(group_tokens, width)
+    mixed_heads = lines.transpose(1, 0, 2).reshape(tokens_present, QUERY_HEADS * HEAD_WIDTH)
     tokens = layer_input.reshape(tokens_present, width).astype(f32)
     middle = tokens + jnp.dot(mixed_heads, dense_out, preferred_element_type=f32)
     inverse_two = lax.rsqrt(jnp.mean(middle * middle, axis=1, keepdims=True) + epsilon)
@@ -1599,13 +2124,14 @@
     hot = route_flat[:, :, None] == jnp.arange(EXPERTS, dtype=jnp.int32)[None, None, :]
     chosen = jnp.sum(jnp.where(hot, router_logits[:, None, :], 0.0), axis=2)
     gates = jax.nn.softmax(chosen, axis=-1)
-    expert_of = route_flat.reshape(pairs)
-    rank = pair_rank.reshape(pairs)
-    slot = jnp.sum(
-        (expert_of[None, :] == expert_of[:, None]) & (rank[None, :] < rank[:, None]),
-        axis=1,
-        dtype=jnp.int32,
-    )
+    if not fused:
+        expert_of = route_flat.reshape(pairs)
+        rank = pair_rank.reshape(pairs)
+        slot = jnp.sum(
+            (expert_of[None, :] == expert_of[:, None]) & (rank[None, :] < rank[:, None]),
+            axis=1,
+            dtype=jnp.int32,
+        )
     kept = (slot < CAP).reshape(tokens_present, top).astype(f32)
     weights_pair = gates * kept
     spread = jnp.sum(jnp.where(hot, weights_pair[:, :, None], 0.0), axis=1)
@@ -1615,14 +2141,8 @@
     payload = jnp.concatenate([second_input, spread_high, pad, spread_low, pad], axis=1)
     if fused:
         back, moe_part, keep_up, other_up, keep_down, other_down = expert_turn(
-            payload, grad_all, expert_up, expert_down, chips, head_number, 6
-        )
-        moe_sums = Sums(moe_part.reshape(chips, head_number, tokens_present, width))
-        shared = (keep_up.astype(f32) + other_up.astype(f32)).astype(bf16)
-        pieces = [
-            across(lax.dynamic_index_in_dim(shared, chip ^ mask, 0, keepdims=False), chips, mask)
-            for mask in range(chips)
-        ]
+            payload, grad_all, units, w_down, head_number, 6
+        )
         down_share = keep_down.astype(f32) + other_down.astype(f32)
     else:
         x_all = gather(payload, chips, head_number, False, 6).reshape(group_tokens, columns)
@@ -1667,69 +2187,47 @@
     )
     grad_attn = grad_mid.astype(bf16)
     grad_dense_out = jnp.dot(mixed_heads.T, grad_attn, preferred_element_type=f32)
-    out_share = lax.psum_scatter(
-        grad_dense_out.astype(bf16), ("chip", "core", "head"), scatter_dimension=0, tiled=True
-    ).astype(f32)
+    grad_dense_out = grad_dense_out.astype(bf16)
+    if not fused:
+        out_share = lax.psum_scatter(
+            grad_dense_out, ("chip", "core", "head"), scatter_dimension=0, tiled=True
+        ).astype(f32)
     grad_heads = (
         jnp.dot(grad_attn, dense_out.T, preferred_element_type=f32)
         .astype(bf16)
         .reshape(tokens_present, head_number, group_columns)
         .transpose(1, 0, 2)
     )
-    grad_local = to_blocks(
-        line_exchange(grad_heads, head_number, 8).reshape(line_tokens, group_columns)
-    ).reshape(sequence_batch, blk, key_value_location, query_group, HEAD_WIDTH)
+    grad_q, grad_kv, *beside = attend_back(
+        queries,
+        kv_all,
+        key_seg,
+        query_seg,
+        out_turned,
+        lse,
+        grad_heads,
+        [
+            (moe_part.reshape(chips, head_number, tokens_present, width), False),
+            (grad_dense_out.reshape(chips, 2, head_number, dense_rows, width), True),
+        ]
+        if fused
+        else [],
+        head_number,
+        query_group,
+        8,
+    )
     if fused:
-        moe_sums.plane(0)
-        grad_local = pin(moe_sums, grad_local)
-        moe_sums.plane(1)
-    delta = jnp.sum(grad_local.transpose(0, 2, 3, 1, 4).astype(f32) * attended, axis=-1)
-
-    def backward_block(state, piece, offset, token_count):
-        grad_q, grad_store = state
-        keys, values = key_view(piece, offset, token_count)
-        scores = (
-            jnp.einsum("sqhgd,skhd->shgqk", query_rows, keys, preferred_element_type=f32) * scale
-        )
-        mask = key_mask(offset, token_count)
-        probs = jnp.where(mask, jnp.exp(scores - lse[..., None]), 0.0)
-        grad_probs = jnp.einsum("sqhgd,skhd->shgqk", grad_local, values, preferred_element_type=f32)
-        grad_scores = (probs * (grad_probs - delta[..., None])).astype(bf16)
-        grad_q = (
-            grad_q
-            + jnp.einsum("shgqk,skhd->sqhgd", grad_scores, keys, preferred_element_type=f32) * scale
-        )
-        grad_k = (
-            jnp.einsum("shgqk,sqhgd->skhd", grad_scores, query_rows, preferred_element_type=f32)
-            * scale
-        )
-        grad_v = jnp.einsum(
-            "shgqk,sqhgd->skhd", probs.astype(bf16), grad_local, preferred_element_type=f32
-        )
-        block_width = jnp.stack([grad_k, grad_v], axis=3).reshape(
-            sequence_batch, token_count, kv_columns
-        )
-        grad_store = lax.dynamic_update_slice_in_dim(
-            grad_store, block_width.astype(bf16), offset, 1
-        )
-        return (grad_q, grad_store)
-
-    back_zero = (
-        jnp.zeros((sequence_batch, blk, key_value_location, query_group, HEAD_WIDTH), f32),
-        jnp.zeros((sequence_batch, length, kv_columns), bf16),
-    )
-    grad_q, grad_store = sweep(backward_block, back_zero)
-    if fused:
-        grad_store = pin(moe_sums, grad_store)
-        moe_sums.along()
-    grad_store = (
-        grad_store.reshape(sequence_batch, 2 * chips, blk, kv_columns)
-        .transpose(1, 0, 2, 3)
-        .reshape(chips, 2, sequence_batch * blk, kv_columns)
-    )
-    grad_kv = scatter_sum(grad_store, chips, 1, True, 9).reshape(
-        sequence_batch, blk, key_value_location, 2, HEAD_WIDTH
-    )
+        moe, out_share = beside
+        keep_up, grad_kv = lax.optimization_barrier((keep_up, grad_kv))
+        shared = (keep_up.astype(f32) + other_up.astype(f32)).astype(bf16)
+        pieces = [
+            across(lax.dynamic_index_in_dim(shared, chip ^ mask, 0, keepdims=False), chips, mask)
+            for mask in range(chips)
+        ]
+    grad_q = grad_q.reshape(
+        sequence_batch, key_value_location, query_group, blk, HEAD_WIDTH
+    ).transpose(0, 3, 1, 2, 4)
+    grad_kv = grad_kv.reshape(sequence_batch, blk, key_value_location, 2, HEAD_WIDTH)
     grad_proj = jnp.concatenate([grad_q.astype(bf16), grad_kv.astype(bf16)], axis=3).astype(f32)
     unturned = rotate(grad_proj[:, :, :, : query_group + 1], cosine, -sine)
     grad_qkv = to_lines(
@@ -1762,7 +2260,6 @@
         grad_first = jnp.sum(grad_first.astype(f32), axis=0)
         sums = sums.astype(f32)
         up_share = place_units(pieces, hidden)
-        moe = moe_sums.result()
     else:
         grad_first = jnp.sum(
             line_exchange(

time: 671 us -> 580 us (0.86)
  waiting for transfers between devices: 59.5 us -> 0.01 us
  Pallas kernels: 408 us -> 467 us
  local copies, waits for them, and re-layouts: 76.4 us -> 44.4 us
  other arithmetic: 46 us -> 25.2 us
  between operations: 15 us -> 1.67 us
  starting transfers between devices: 15.7 us -> 4.65 us
  matrix products: 39.1 us -> 28.6 us
    pallas_call x5 -> x3, Pallas kernels: 185 us -> 261 us  [the longest x1 107 us: attend_back(): pl.pallas_call(functools.partial(attend_back_kernel, cube, heads, group,...]
    ppermute x7 -> x5, waiting for transfers between devices: 41 us -> 0.01 us  [across(): return lax.ppermute(value, 'chip', [(i, i ^ mask) for i in range(chips)])]
    pallas_call x1, Pallas kernels: 169 us -> 155 us  [expert_turn(): pl.pallas_call(functools.partial(turn_kernel, cube, heads, hidden), out_s...]
    ppermute x3 -> x0, waiting for transfers between devices: 12.9 us -> none  [along(): self.line.append(lax.ppermute(give, 'head', pairs))]
    dot_general x7 -> x0, matrix products: 9.26 us -> none  [the longest x1 2.07 us: backward_block(): jnp.einsum('sqhgd,skhd->shgqk', grad_local, values, preferred_element_typ...]
    convert_element_type x6 -> x0, other arithmetic: 8.46 us -> none  [the longest x2 4.9 us: plane(): self.block(side, mask | 1 << order[k], k).astype(bf16)]
    reshape x2 -> x3, local copies, waits for them, and re-layouts: 7.44 us -> 0.42 us  [the longest x1 0.26 us: per_device(): grad_q.reshape(sequence_batch, key_value_location, query_group, blk, HEAD...]
  transfers between devices with their start and end apart: 13 -> 5, of which waited for: 4 -> 0; matrix products, arithmetic and copies ran while one was open for 23% -> 11% of each run, Pallas kernels for 36% -> 26%
where the time goes in v4:
time: 580 us; the launch traced here: 571 us
  Pallas kernels  467 us (81%)
  local copies, waits for them, and re-layouts  44.4 us (8%)
  matrix products  28.6 us (5%)
  other arithmetic  25.2 us (4%)
    pallas_call x1, Pallas kernels, expert_turn(): pl.pallas_call(functools.partial(turn_kernel, cube, heads, hidden), out_s...  155 us
    pallas_call x1, Pallas kernels, attend_back(): pl.pallas_call(functools.partial(attend_back_kernel, cube, heads, group,...  107 us
    pallas_call x1, Pallas kernels, attend(): pl.pallas_call(functools.partial(attend_kernel, cube, heads, group, [core...  105 us
    pallas_call x1, Pallas kernels, start(): pl.pallas_call(functools.partial(start_kernel, cube, heads), out_shape=(j...  49.1 us
    pallas_call x1, Pallas kernels, end(): pl.pallas_call(functools.partial(end_kernel, cube, heads), out_shape=(jax...  42.8 us
  transfers between devices with their start and end apart: 5, of which 0 were waited for; matrix products, arithmetic and copies ran while one was open for 11% of the time, Pallas kernels for 26%

profile of v4, /device:TPU:0, one launch (start us, length us, event | category | flops | bytes accessed | tf_op | source)
XLA Modules:
  0.0 571.4 jit_solution(13307547702770198894)
XLA Ops:
  1.5 1.0 broadcast_in_dim_reshape.9.refs_3_
  4.0 1.0 copy.196
  5.7 1.3 constant_dynamic-slice_fusion.8
  7.0 1.1 pad_maximum_fusion.refs_2_
  8.1 49.1 %start.1 = (bf16[4,128,1536]{2,1,0:T(8,128)(2,1)}, bf16[4,2,4,48,768]{4,3,2,1,0:T(8,128)(2,1)}, bf16[10,192,256]{2,1,0:T(8,128)(2,1)}, s32[1,1024]{1,0:T(1,128)}) custom-call(bf16[128,1536]{1,0:T(8,128)(2,1)} %bitcast.109, bf16[4,48,768]{2,1,0:T(8,128)(2,1)} %pad_maximum_fusion.5.refs_1_, bf16[10,192,256]{2,1,0:T(8,128)(2,1)} %pad_maximum_fusion.refs_2_, ...), custom_call_target="tpu_custom_call" | custom-call | tf_op jit(solution)/shard_map/start/pallas_call | solution.py:1154
  57.2 3.1 constant_dynamic-slice_fusion.1
  60.2 1.2 pad_maximum_fusion.2
  61.4 1.1 collective-permute-start
  62.5 1.1 pad_maximum_fusion.3
  63.6 1.7 convert_reduce_fusion.1
  66.5 4.0 fusion.9
  70.5 3.0 copy.158
  73.5 2.5 reshape_reshape.4
  76.0 1.0 slice.128
  77.2 1.4 multiply_subtract_fusion
  79.4 2.0 copy.161.refs_2_
  81.4 105.1 %attend.1 = (bf16[4,128,384]{2,1,0:T(8,128)(2,1)S(1)}, bf16[4,2,2,256,256]{4,3,2,1,0:T(8,128)(2,1)}, f32[4,64,768]{2,1,0:T(8,128)S(1)}, f32[4,1,768]{2,1,0:T(1,1...) custom-call(bf16[4,768,64]{2,1,0:T(8,128)(2,1)S(1)} %bitcast.101, ...), custom_call_target="tpu_custom_call" | custom-call | tf_op jit(solution)/shard_map/attend/pallas_call | solution.py:1720
  187.6 3.4 multiply_reduce_fusion.3
  191.4 1.4 fusion.26
  193.1 1.6 multiply_convert_fusion
  194.8 2.8 copy.180
  197.7 0.9 copy.181
  200.4 1.1 pad_maximum_fusion.1.refs_3_
  201.4 154.7 %expert_turn.1 = (f32[128,1664]{1,0:T(8,128)}, bf16[2048,1536]{1,0:T(8,128)(2,1)}, bf16[4,10,192,256]{3,2,1,0:T(8,128)(2,1)}, bf16[4,10,192,256]{3,2,1,0:T(8,128...) custom-call(bf16[128,1664]{1,0:T(8,128)(2,1)} %concatenate.48.refs_0_, ...), custom_call_target="tpu_custom_call" | custom-call | tf_op jit(solution)/shard_map/expert_turn/pallas_call | solution.py:959
  356.2 0.9 slice.78
  357.3 2.0 multiply_reduce_fusion.1
  359.6 4.3 convolution_convert_fusion.1
  363.9 3.6 convolution_convert_fusion
  367.7 0.9 copy.172
  368.6 106.7 %attend_back.1 = (bf16[4,768,64]{2,1,0:T(8,128)(2,1)}, f32[512,256]{1,0:T(8,128)}, f32[128,1536]{1,0:T(8,128)}, f32[48,1536]{1,0:T(8,128)}) custom-call(bf16[4,768,64]{2,1,0:T(8,128)(2,1)} %bitcast.102, bf16[4,2,2,256,256]{4,3,2,1,0:T(8,128)(2,1)} %get-tuple-element.45.refs_1_, s32[2,2048,1]{2,1,0:T(8,128)} %copy.161.refs_2_, s32[2,1,768]{2,1,0:T(1,128)} %copy-done.8, ...), custom_call_target="tpu_custom_call" | custom-call | tf_op jit(solution)/shard_map/attend_back/pallas_call | solution.py:1920
  475.4 2.0 add_convert_fusion.1
  477.3 3.6 add_convert_fusion
  480.9 2.0 dynamic-slice_bitcast_fusion
  482.9 2.0 collective-permute-start.3
  484.9 1.5 collective-permute-start.4
  488.3 2.4 copy.179
  490.7 1.8 convolution_convert_fusion.3
  492.7 4.4 fusion.1
  497.1 1.5 concatenate.58
  498.6 1.5 concatenate.59
  500.0 3.7 convolution_convert_fusion.2
  503.8 3.7 concatenate.57.in_ref
  507.6 1.4 copy-done.3
  509.0 42.8 %end.1 = (bf16[4,128,1536]{2,1,0:T(8,128)(2,1)S(1)}, bf16[4,48,768]{2,1,0:T(8,128)(2,1)S(1)}) custom-call(bf16[4,128,1536]{2,1,0:T(8,128)(2,1)S(1)} %bitcast.103, bf16[4,2,192,768]{3,2,1,0:T(8,128)(2,1)S(1)} %concatenate.57.in_ref), custom_call_target="tpu_custom_call" | custom-call | tf_op jit(solution)/shard_map/end/pallas_call | solution.py:1274
  551.8 1.1 copy-done.1
  555.2 4.1 convert_add_fusion
  560.7 1.2 fusion.15
  561.9 8.6 %place_units.1 = f32[10,192,1024]{2,1,0:T(8,128)} custom-call(bf16[10,192,256]{2,1,0:T(8,128)(2,1)} %get-tuple-element.65.refs_0_, bf16[10,192,256]{2,1,0:T(8,128)(2,1)} %collective-permute-done.2.refs_1_, bf16[10,192,256]{2,1,0:T(8,128)(2,1)} %collective-permute-done.3.refs_2_, bf16[10,192,256]{2,1,0:T(8,128)(2,1)} %collective-permute-done.4.refs_3_), custom_call_target="tpu_custom_call" | custom-call | tf_op jit(solution)/shard_map/place_units/pallas_call | solution.py:1316
  (148 shorter events, 16.0 us)
Async XLA Ops:
  60.2 5.2 copy-start.14
  61.4 140.1 %collective-permute-start = (bf16[10,192,256]{2,1,0:T(8,128)(2,1)}, bf16[10,192,256]{2,1,0:T(8,128)(2,1)}, u32[]{:S(2)}, u32[]{:S(2)}) collective-permute-start(bf16[10,192,256]{2,1,0:T(8,128)(2,1)} %pad_maximum_fusion.2), channel_id=1, source_target_pairs={{0,8},{8,0},{16,24},{24,16},{1,9},{9,1},{17,25},{25,17},{2,10},{10... | collective-permute-start | bytes 2949128 | tf_op jit(solution)/shard_map/ppermute | solution.py:1329
  63.6 137.8 %collective-permute-start.1 = (bf16[10,192,256]{2,1,0:T(8,128)(2,1)}, bf16[10,192,256]{2,1,0:T(8,128)(2,1)}, u32[]{:S(2)}, u32[]{:S(2)}) collective-permute-start(bf16[10,192,256]{2,1,0:T(8,128)(2,1)} %pad_maximum_fusion.3), channel_id=1, source_target_pairs={{0,16},{8,24},{16,0},{24,8},{1,17},{9,25},{17,1},{25,9},{2,18},{10... | collective-permute-start | bytes 2949128 | tf_op jit(solution)/shard_map/ppermute | solution.py:1329
  76.0 2.6 copy-start.28
  78.6 0.8 copy-start.29
  78.7 2.6 copy-start.4
  78.8 2.6 copy-start.7
  79.2 107.3 %copy-start = (bf16[2,2,3,256,64]{4,3,2,1,0:T(8,128)(2,1)}, bf16[2,2,3,256,64]{4,3,2,1,0:T(8,128)(2,1)S(1)}, u32[]{:S(2)}) copy-start(bf16[2,2,3,256,64]{4,3,2,1,0:T(8,128)(2,1)S(1)} %copy.159) | copy-start | bytes 1179652
  81.3 106.3 %copy-start.12 = (bf16[2,64,1536]{2,1,0:T(8,128)(2,1)S(1)}, bf16[2,64,1536]{2,1,0:T(8,128)(2,1)}, u32[]{:S(2)}) copy-start(bf16[2,64,1536]{2,1,0:T(8,128)(2,1)} %param.12) | copy-start | bytes 1179652
  81.3 109.7 %copy-start.8 = (s32[2,1,768]{2,1,0:T(1,128)}, s32[2,1,768]{2,1,0:T(1,128)S(1)}, u32[]{:S(2)}) copy-start(s32[2,1,768]{2,1,0:T(1,128)S(1)} %tile.10.refs_3_) | copy-start | bytes 18436
  186.5 0.9 copy-start.6
  187.3 3.7 copy-start.9
  187.6 3.4 copy-start.17
  187.6 3.4 copy-start.32
  191.0 2.1 copy-start.15
  197.6 2.8 copy-start.20
  197.6 2.8 copy-start.21
  198.8 157.4 %copy-start.30 = (f32[2,64]{1,0:T(2,128)}, f32[2,64]{1,0:T(2,128)S(1)}, u32[]{:S(2)}) copy-start(f32[2,64]{1,0:T(2,128)S(1)} %add_rsqrt_fusion.1) | copy-start | bytes 1540
  356.2 3.1 copy-start.5
  357.3 2.3 copy-start.27
  359.6 4.3 copy-start.10
  359.6 4.3 copy-start.18
  368.6 108.7 %copy-start.19 = (bf16[4,10,192,256]{3,2,1,0:T(8,128)(2,1)S(1)}, bf16[4,10,192,256]{3,2,1,0:T(8,128)(2,1)}, u32[]{:S(2)}) copy-start(bf16[4,10,192,256]{3,2,1,0:T(8,128)(2,1)} %get-tuple-element.57) | copy-start | bytes 11796484
  480.9 5.5 copy-start.25
  482.9 4.4 copy-start.24
  482.9 76.5 %collective-permute-start.2 = (bf16[10,192,256]{2,1,0:T(8,128)(2,1)}, bf16[10,192,256]{2,1,0:T(8,128)(2,1)}, u32[]{:S(2)}, u32[]{:S(2)}) collective-permute-start(bf16[10,192,256]{2,1,0:T(8,128)(2,1)} %get-tuple-element.115), channel_id=1, source_target_pairs={{0,8},{8,0},{16,24},{24,16},{1,9},{9,1},{17,25},{25,17},{2,10},{10... | collective-permute-start | bytes 2949128 | tf_op jit(solution)/shard_map/ppermute | solution.py:1329
  482.9 76.5 %collective-permute-start.3 = (bf16[10,192,256]{2,1,0:T(8,128)(2,1)}, bf16[10,192,256]{2,1,0:T(8,128)(2,1)}, u32[]{:S(2)}, u32[]{:S(2)}) collective-permute-start(bf16[10,192,256]{2,1,0:T(8,128)(2,1)} %get-tuple-element.114), channel_id=1, source_target_pairs={{0,16},{8,24},{16,0},{24,8},{1,17},{9,25},{17,1},{25,9},{2,18},{10... | collective-permute-start | bytes 2949128 | tf_op jit(solution)/shard_map/ppermute | solution.py:1329
  484.9 74.5 %collective-permute-start.4 = (bf16[10,192,256]{2,1,0:T(8,128)(2,1)}, bf16[10,192,256]{2,1,0:T(8,128)(2,1)}, u32[]{:S(2)}, u32[]{:S(2)}) collective-permute-start(bf16[10,192,256]{2,1,0:T(8,128)(2,1)} %get-tuple-element.113), channel_id=1, source_target_pairs={{0,24},{8,16},{16,8},{24,0},{1,25},{9,17},{17,9},{25,1},{2,26},{10... | collective-permute-start | bytes 2949128 | tf_op jit(solution)/shard_map/ppermute | solution.py:1329
  487.8 4.9 copy-start.16
  492.7 7.3 %copy-start.23 = (bf16[1536,512]{1,0:T(8,128)(2,1)S(1)}, bf16[1536,512]{1,0:T(8,128)(2,1)}, u32[]{:S(2)}) copy-start(bf16[1536,512]{1,0:T(8,128)(2,1)} %copy.180) | copy-start | bytes 4718596
  507.6 1.4 copy-start.3
  551.8 1.1 copy-start.1
  552.9 2.3 copy-start.22
  555.2 4.2 copy-start.2
  559.4 1.0 copy-start.13
  559.4 1.0 copy-start.31
  559.4 1.3 copy-start.11
  559.4 1.3 copy-start.33
  561.9 8.6 %copy-start.26 = (f32[48,1536]{1,0:T(8,128)S(1)}, f32[48,1536]{1,0:T(8,128)}, u32[]{:S(2)}) copy-start(f32[48,1536]{1,0:T(8,128)} %get-tuple-element.152) | copy-start | bytes 884740

commit v5 on v4

--- a/solution.py
+++ b/solution.py
@@ -1039,8 +1039,8 @@
     def x_copy(rank, step):
         head = source(rank)
         return pltpu.make_async_remote_copy(
-            src_ref=x_ref if rank == 0 else x_out.at[head],
-            dst_ref=x_out.at[head],
+            src_ref=x_ref if rank == 0 else x_out.at[:, head],
+            dst_ref=x_out.at[:, head],
             send_sem=x_send.at[heads if rank == 0 and step < 0 else head],
             recv_sem=x_recv.at[head],
             device_id={"head": (hz + step + heads) % heads},
@@ -1103,7 +1103,7 @@
 
     locals_ = [
         pltpu.make_async_copy(slice_ref.at[hz], dense_out.at[chip, core, hz], local.at[0]),
-        pltpu.make_async_copy(x_ref, x_out.at[hz], local.at[1]),
+        pltpu.make_async_copy(x_ref, x_out.at[:, hz], local.at[1]),
     ]
     def count_slots():
         row = row_ref[...]
@@ -1154,7 +1154,7 @@
     return pl.pallas_call(
         functools.partial(start_kernel, cube, heads),
         out_shape=(
-            jax.ShapeDtypeStruct((heads,) + x.shape, bf16),
+            jax.ShapeDtypeStruct((x.shape[0], heads) + x.shape[1:], bf16),
             jax.ShapeDtypeStruct((chips, 2) + slices.shape, bf16),
             jax.ShapeDtypeStruct(unit.shape, bf16),
             jax.ShapeDtypeStruct((1, keys.size), jnp.int32),
@@ -1187,7 +1187,7 @@
     half = in_ref.shape[-2] // 2
     rows = in_ref.shape[-2] // heads
     meet([cube.peer(digit) for digit in range(count)] + [{"head": (hz + d) % heads} for d in others])
-    own = pltpu.make_async_copy(first_ref.at[hz], first_out.at[hz], local)
+    own = pltpu.make_async_copy(first_ref.at[:, hz], first_out.at[hz], local)
     own.start()
     copies = {}
 
@@ -1207,7 +1207,7 @@
     def first_copy(d):
         place = (hz + d) % heads
         return pltpu.make_async_remote_copy(
-            src_ref=first_ref.at[place],
+            src_ref=first_ref.at[:, place],
             dst_ref=first_out.at[hz],
             send_sem=first_send.at[d - 1],
             recv_sem=first_recv.at[d - 1],
@@ -1274,7 +1274,7 @@
     return pl.pallas_call(
         functools.partial(end_kernel, cube, heads),
         out_shape=(
-            jax.ShapeDtypeStruct(first.shape, bf16),
+            jax.ShapeDtypeStruct((heads, first.shape[0]) + first.shape[2:], bf16),
             jax.ShapeDtypeStruct((heads, rows // heads, columns), bf16),
         ),
         in_specs=[ANY, WHOLE],
@@ -1313,12 +1313,13 @@
 def place_units(pieces, hidden):
     chips = len(pieces)
     experts_here, rows, double = pieces[0].shape
+    group = 2 if experts_here % 2 == 0 else 1
     return pl.pallas_call(
         functools.partial(place_kernel, chips, hidden),
-        grid=(experts_here,),
+        grid=(experts_here // group,),
         out_shape=jax.ShapeDtypeStruct((experts_here, rows, chips * double), f32),
-        in_specs=[pl.BlockSpec((1, rows, double), lambda e: (e, 0, 0))] * chips,
-        out_specs=pl.BlockSpec((1, rows, chips * double), lambda e: (e, 0, 0)),
+        in_specs=[pl.BlockSpec((group, rows, double), lambda e: (e, 0, 0))] * chips,
+        out_specs=pl.BlockSpec((group, rows, chips * double), lambda e: (e, 0, 0)),
         name="place_units",
     )(*pieces)
 
@@ -1437,6 +1438,84 @@
                     self.plane_copy(side, mask, k, rank).wait_send()
 
 
+class DenseGather:
+    def __init__(self, cube, heads, own, out, sems):
+        self.cube, self.heads, self.own, self.out = cube, heads, own, out
+        self.local, self.line_send, self.line_recv, self.send, self.recv = sems
+        self.hz = lax.axis_index("head")
+
+    @staticmethod
+    def scratch(cube, heads):
+        return [
+            DMA,
+            DMA((heads - 1,)),
+            DMA((heads - 1,)),
+            DMA((2, 1 << cube.number)),
+            DMA((2, 1 << cube.number)),
+        ]
+
+    def line_copy(self, d):
+        return pltpu.make_async_remote_copy(
+            src_ref=self.own,
+            dst_ref=self.out.at[self.cube.place(0) + (self.hz,)],
+            send_sem=self.line_send.at[d - 1],
+            recv_sem=self.line_recv.at[d - 1],
+            device_id={"head": (self.hz + d) % self.heads},
+            device_id_type=MESH,
+        )
+
+    def flat_copy(self, side, mask, k):
+        digit = self.cube.gather_orders[side][k]
+        later = mask | (1 << digit)
+        part = self.heads // 2
+        place = self.out.at[self.cube.place(mask) + (pl.ds(side * part, part),)]
+        return pltpu.make_async_remote_copy(
+            src_ref=place,
+            dst_ref=place,
+            send_sem=self.send.at[side, later],
+            recv_sem=self.recv.at[side, later],
+            device_id=self.cube.peer(digit),
+            device_id_type=MESH,
+        )
+
+    def steps_after(self, side, mask):
+        order = self.cube.gather_orders[side]
+        last = max([k for k in range(self.cube.number) if (mask >> order[k]) & 1], default=-1)
+        return range(last + 1, self.cube.number)
+
+    def begin(self):
+        self.own_copy = pltpu.make_async_copy(
+            self.own, self.out.at[self.cube.place(0) + (self.hz,)], self.local
+        )
+        self.own_copy.start()
+        for d in near(self.heads)[::-1]:
+            self.line_copy(d).start()
+
+    def events(self):
+        return [(mask, 2) for mask in range(1 << self.cube.number)]
+
+    def receive(self, mask, _):
+        if mask == 0:
+            self.own_copy.wait()
+            for d in near(self.heads):
+                self.line_copy(d).wait_recv()
+        for side in range(2):
+            if mask:
+                order = self.cube.gather_orders[side]
+                k = max(k for k in range(self.cube.number) if (mask >> order[k]) & 1)
+                self.flat_copy(side, mask & ~(1 << order[k]), k).wait_recv()
+            for k in self.steps_after(side, mask):
+                self.flat_copy(side, mask, k).start()
+
+    def finish(self):
+        for d in near(self.heads):
+            self.line_copy(d).wait_send()
+        for mask in range(1 << self.cube.number):
+            for side in range(2):
+                for k in self.steps_after(side, mask):
+                    self.flat_copy(side, mask, k).wait_send()
+
+
 class LineSums:
     def __init__(self, cube, heads, blocks, out, refs):
         self.cube, self.heads, self.blocks, self.out = cube, heads, blocks, out
@@ -1448,7 +1527,7 @@
         self.hz = lax.axis_index("head")
         self.rows = blocks.shape[-2]
         self.outward = near(heads)[::-1] + [0]
-        self.turns = heads + count
+        self.turns = heads + count + 1
 
     @staticmethod
     def scratch(cube, heads, rows, columns):
@@ -1520,8 +1599,8 @@
                 for mask in subsets(self.cube.scatter_orders[side][1:])[::-1]:
                     self.copy_of(side, 0, mask, self.outward[turn]).start()
         for k in range(1, count):
-            if 0 <= turn - k < self.heads:
-                d = self.outward[turn - k]
+            if 0 <= turn - k - 1 < self.heads:
+                d = self.outward[turn - k - 1]
                 for side in range(2):
                     order = self.cube.scatter_orders[side]
                     for mask in subsets(order[k + 1 :])[::-1]:
@@ -1529,8 +1608,8 @@
                         place = self.there(self.parts[k - 1], side, self.slot(side, k, mask), d)
                         place[...] = value.astype(bf16)
                         self.copy_of(side, k, mask, d).start()
-        if 0 <= turn - count < self.heads:
-            d = self.outward[turn - count]
+        if 0 <= turn - count - 1 < self.heads:
+            d = self.outward[turn - count - 1]
             for side in range(2):
                 value = self.sums(side, count, 0, d)
                 part = part_of(self.rows, side)
@@ -1579,18 +1658,23 @@
     part = rows // 2
     meet([cube.peer(digit) for digit in range(cube.number)] + [{"head": (hz + d) % heads} for d in others])
     kv_out[chip, core] = kv_ref[...]
-    gathers = [
-        LineGather(Cube(cube.chips, with_core), heads, *pair, refs[8 + 5 * i : 13 + 5 * i])
-        for i, (with_core, pair) in enumerate(zip(beside, zip(near_refs, far_refs)))
-    ]
-    events = sorted(
-        (
-            ((index + 0.5) / len(one.events()), one, event)
-            for one in gathers
-            for index, event in enumerate(one.events())
-        ),
-        key=lambda item: item[0],
-    )
+    gathers = []
+    rest_refs = refs[8:]
+    for with_core, own_block, all_blocks in zip(beside, near_refs, far_refs):
+        kind = DenseGather if with_core else LineGather
+        own_cube = Cube(cube.chips, with_core)
+        gathers.append(kind(own_cube, heads, own_block, all_blocks, rest_refs[:5]))
+        rest_refs = rest_refs[5:]
+    fronts = {}
+    for one in gathers:
+        for mask, rank in one.events():
+            fronts.setdefault(rank + bin(mask).count("1"), []).append((one, (mask, rank)))
+    last_front = max(fronts, default=0)
+    now = cube.number + 1
+
+    def pass_front(index):
+        for one, event in fronts.get(index, []):
+            one.receive(*event)
 
     def copy_of(side, mask, k):
         order = cube.gather_orders[side]
@@ -1618,6 +1702,9 @@
                 copies.append((side, mask, k))
 
     forward(0)
+    for one in gathers:
+        one.begin()
+    pass_front(0)
     top[...] = jnp.full_like(top, negative)
     total[...] = jnp.zeros_like(total)
     acc[...] = jnp.zeros_like(acc)
@@ -1649,21 +1736,18 @@
                 )
 
     block_step(seq)
-    for one in gathers:
-        one.begin()
-    for _, one, event in events[: len(gathers)]:
-        one.receive(*event)
-    for mask in sorted(range(1, 1 << cube.number), key=lambda m: bin(m).count("1")):
-        forward(mask)
+    for level in range(1, cube.number + 1):
+        for mask in range(1, 1 << cube.number):
+            if bin(mask).count("1") == level:
+                forward(mask)
+    pass_front(1)
+    now = 2
     turns = 2 * cube.chips
-    skip = len(gathers)
-    rest = len(events) - skip
     if beside:
         for turn in range(turns):
-            for _, one, event in events[
-                skip + rest * turn // turns : skip + rest * (turn + 1) // turns
-            ]:
-                one.receive(*event)
+            if turn == turns // 2:
+                pass_front(now)
+                now += 1
 
             @pl.when(turn < seq)
             def _():
@@ -1703,6 +1787,8 @@
     for d in others:
         line_copy(d).start()
     lines_ref[hz] = stage[hz]
+    for index in range(now, last_front + 1):
+        pass_front(index)
     for side, mask, k in copies:
         copy_of(side, mask, k).wait_send()
     for d in others:
@@ -1741,7 +1827,11 @@
             DMA((heads - 1,)),
             DMA((heads - 1,)),
         ]
-        + [item for _, core in beside for item in LineGather.scratch(Cube(chips, core), heads)],
+        + [
+            item
+            for _, core in beside
+            for item in (DenseGather if core else LineGather).scratch(Cube(chips, core), heads)
+        ],
         compiler_params=pltpu.CompilerParams(
             collective_id=number, has_side_effects=True, vmem_limit_bytes=50 << 20
         ),
@@ -1749,11 +1839,14 @@
     )(queries, keys_values, key_seg, query_seg, *[value for value, _ in beside])
 
 
-def attend_back_kernel(cube, heads, group, beside, *refs):
+def attend_back_kernel(cube, heads, group, beside, shares, *refs):
     q_ref, kv_ref, key_seg, query_seg, out_turned, lse_ref, dh_ref = refs[:7]
     near_refs, refs = refs[7 : 7 + len(beside)], refs[7 + len(beside) :]
+    pair_refs, refs = refs[:shares], refs[shares:]
     dq_ref, dkv_ref = refs[:2]
-    far_refs, refs = refs[2 : 2 + len(beside)], (None,) * 9 + refs[2 + len(beside) :]
+    far_refs, refs = refs[2 : 2 + len(beside)], refs[2 + len(beside) :]
+    added = refs[: cube.chips] if shares else ()
+    refs = (None,) * 9 + refs[len(added) :]
     count = cube.number
     landed, d_out, delta, dq_turned, grads = refs[9:14]
     arrived, parts = refs[14 : 14 + count], refs[14 + count : 13 + 2 * count]
@@ -1766,6 +1859,29 @@
         size = 2 * own_cube.number + 5
         sums_beside.append(LineSums(own_cube, heads, source, target, rest[:size]))
         rest = rest[size:]
+
+    def load_pair(mask):
+        place = flip(lax.axis_index("chip"), mask)
+        return [
+            pltpu.make_async_copy(pair_refs[i].at[place], rest[i], rest[3].at[i]) for i in range(2)
+        ]
+
+    def store_sum(mask):
+        return pltpu.make_async_copy(rest[2], added[mask], rest[3].at[2])
+
+    def add_pair(turn):
+        mask = turn // 2
+        if turn % 2 == 0:
+            for copy in load_pair(mask):
+                copy.start()
+            return
+        for copy in load_pair(mask):
+            copy.wait()
+        if mask:
+            store_sum(mask - 1).wait()
+        rest[2][...] = (rest[0][...].astype(f32) + rest[1][...].astype(f32)).astype(bf16)
+        store_sum(mask).start()
+
     chip, core, hz = lax.axis_index("chip"), lax.axis_index("core"), lax.axis_index("head")
     seq = chip * 2 + core
     others = near(heads)[::-1]
@@ -1787,8 +1903,9 @@
 
     for d in others:
         line_copy(d).start()
-    for one in sums_beside:
-        one.turn(0)
+    for turn in range(2):
+        for one in sums_beside:
+            one.turn(turn)
     landed[hz] = dh_ref[hz]
     grads[...] = jnp.zeros_like(grads)
     dq_turned[...] = jnp.zeros_like(dq_turned)
@@ -1835,7 +1952,7 @@
                     jnp.concatenate([d_keys, d_values], axis=1).astype(bf16)
                 )
 
-    done = 1
+    done = 2
     if beside:
         for turn in range(turns):
 
@@ -1843,6 +1960,8 @@
             def _():
                 block_step(turn)
 
+            if shares:
+                add_pair(turn)
             if turn % 3 == 2:
                 for one in sums_beside:
                     one.turn(done)
@@ -1906,10 +2025,12 @@
         copy.wait_send()
     for one in sums_beside:
         one.finish()
+    if shares:
+        store_sum(cube.chips - 1).wait()
 
 
 def attend_back(
-    queries, kv_all, key_seg, query_seg, out_turned, lse, d_heads, beside, heads, group, number
+    queries, kv_all, key_seg, query_seg, out_turned, lse, d_heads, beside, shares, heads, group, number
 ):
     chips, _, batch, rows, columns = kv_all.shape
     pairs, wide, depth = queries.shape
@@ -1918,14 +2039,17 @@
     half = batch * rows // 2
     slots = [(1 << count) >> (k + 1) for k in range(count)]
     return pl.pallas_call(
-        functools.partial(attend_back_kernel, cube, heads, group, [core for _, core in beside]),
+        functools.partial(
+            attend_back_kernel, cube, heads, group, [core for _, core in beside], len(shares)
+        ),
         out_shape=(
             jax.ShapeDtypeStruct((pairs, wide, depth), bf16),
             jax.ShapeDtypeStruct((batch * rows, columns), f32),
         )
-        + tuple(jax.ShapeDtypeStruct(value.shape[-2:], f32) for value, _ in beside),
-        in_specs=[WHOLE] * (7 + len(beside)),
-        out_specs=(WHOLE,) * (2 + len(beside)),
+        + tuple(jax.ShapeDtypeStruct(value.shape[-2:], f32) for value, _ in beside)
+        + tuple(jax.ShapeDtypeStruct(shares[0].shape[1:], bf16) for _ in range(chips) if shares),
+        in_specs=[WHOLE] * (7 + len(beside)) + [ANY] * len(shares),
+        out_specs=(WHOLE,) * (2 + len(beside)) + (ANY,) * (chips * bool(shares)),
         scratch_shapes=[
             pltpu.VMEM(d_heads.shape, bf16),
             pltpu.VMEM((pairs, wide, depth), bf16),
@@ -1945,12 +2069,16 @@
             item
             for value, core in beside
             for item in LineSums.scratch(Cube(chips, core), *value.shape[-3:])
-        ],
+        ]
+        + [pltpu.VMEM(shares[0].shape[1:], bf16) for _ in range(3) if shares]
+        + [DMA((3,)) for _ in range(1) if shares],
         compiler_params=pltpu.CompilerParams(
             collective_id=number, has_side_effects=True, vmem_limit_bytes=56 << 20
         ),
         name="attend_back",
-    )(queries, kv_all, key_seg, query_seg, out_turned, lse, d_heads, *[v for v, _ in beside])
+    )(
+        queries, kv_all, key_seg, query_seg, out_turned, lse, d_heads, *[v for v, _ in beside], *shares
+    )
 
 
 def sibling(value):
@@ -2012,7 +2140,7 @@
 
         keys = (routes * pairs + pair_rank).reshape(pairs)
         x_line, dense, last_unit, slot = start(
-            own_tokens, slices, unit_of(w_gate_up, chips - 1), keys, chips, head_number, 1
+            layer_input, slices, unit_of(w_gate_up, chips - 1), keys, chips, head_number, 1
         )
         x_line, w_gate_up = lax.optimization_barrier((x_line, w_gate_up))
         units = [across(unit_of(w_gate_up, mask), chips, mask) for mask in range(chips - 1)]
@@ -2060,6 +2188,8 @@
 
     def to_blocks(value):
         columns = value.shape[1:]
+        if fused:
+            return value.reshape((sequence_batch, blk) + columns)
         return (
             value.reshape((head_number, sequence_batch, token_rows) + columns)
             .swapaxes(0, 1)
@@ -2068,6 +2198,8 @@
 
     def to_lines(value):
         columns = value.shape[2:]
+        if fused:
+            return value.reshape((line_tokens,) + columns)
         return (
             value.reshape((sequence_batch, head_number, token_rows) + columns)
             .swapaxes(0, 1)
@@ -2104,15 +2236,15 @@
         keys_values.reshape(sequence_batch, blk, kv_columns),
         key_seg,
         query_seg,
-        [(output_weight, True), (cots, False)] if fused else [],
+        [(cots, False), (output_weight, True)] if fused else [],
         chips,
         head_number,
         query_group,
         4,
     )
     if fused:
-        dense_out = beside[0].reshape(QUERY_HEADS * HEAD_WIDTH, width)
-        grad_all = beside[1].reshape(group_tokens, width)
+        grad_all = beside[0].reshape(group_tokens, width)
+        dense_out = beside[1].reshape(QUERY_HEADS * HEAD_WIDTH, width)
     mixed_heads = lines.transpose(1, 0, 2).reshape(tokens_present, QUERY_HEADS * HEAD_WIDTH)
     tokens = layer_input.reshape(tokens_present, width).astype(f32)
     middle = tokens + jnp.dot(mixed_heads, dense_out, preferred_element_type=f32)
@@ -2212,18 +2344,14 @@
         ]
         if fused
         else [],
+        [keep_up, other_up] if fused else [],
         head_number,
         query_group,
         8,
     )
     if fused:
-        moe, out_share = beside
-        keep_up, grad_kv = lax.optimization_barrier((keep_up, grad_kv))
-        shared = (keep_up.astype(f32) + other_up.astype(f32)).astype(bf16)
-        pieces = [
-            across(lax.dynamic_index_in_dim(shared, chip ^ mask, 0, keepdims=False), chips, mask)
-            for mask in range(chips)
-        ]
+        moe, out_share, *shared = beside
+        pieces = [across(shared[mask], chips, mask) for mask in range(chips)]
     grad_q = grad_q.reshape(
         sequence_batch, key_value_location, query_group, blk, HEAD_WIDTH
     ).transpose(0, 3, 1, 2, 4)
@@ -2250,14 +2378,14 @@
     ).astype(bf16)
     if fused:
         grad_first, sums = end(
-            grad_first_part.astype(bf16).reshape(head_number, tokens_present, width),
+            grad_first_part.astype(bf16).reshape(sequence_batch, head_number, token_rows, width),
             sums.reshape(chips, 2, head_number * dense_rows, loc_columns + LANES),
             chips,
             head_number,
             13,
         )
         pieces, grad_first = lax.optimization_barrier((pieces, grad_first))
-        grad_first = jnp.sum(grad_first.astype(f32), axis=0)
+        grad_first = jnp.sum(grad_first.astype(f32), axis=0).reshape(tokens_present, width)
         sums = sums.astype(f32)
         up_share = place_units(pieces, hidden)
     else:

time: 580 us -> 549 us (0.947)
  Pallas kernels: 467 us -> 452 us
  other arithmetic: 25.2 us -> 17.6 us
  matrix products: 28.6 us -> 21.9 us
    pallas_call x1, Pallas kernels: 107 us -> 96.7 us  [attend_back(): pl.pallas_call(functools.partial(attend_back_kernel, cube, heads, group,...]
    unnamed x73 -> x80, local copies, waits for them, and re-layouts: 5.8 us -> 12.8 us
    pallas_call x1, Pallas kernels: 105 us -> 99 us  [attend(): pl.pallas_call(functools.partial(attend_kernel, cube, heads, group, [core...]
  transfers between devices with their start and end apart: 5 -> 5, of which waited for: 0 -> 0; matrix products, arithmetic and copies ran while one was open for 11% -> 8% of each run, Pallas kernels for 26% -> 26%
where the time goes in v5:
time: 549 us; the launch traced here: 541 us
  Pallas kernels  452 us (82%)
  local copies, waits for them, and re-layouts  42.2 us (8%)
  matrix products  21.9 us (4%)
  other arithmetic  17.6 us (3%)
    pallas_call x1, Pallas kernels, expert_turn(): pl.pallas_call(functools.partial(turn_kernel, cube, heads, hidden), out_s...  158 us
    pallas_call x1, Pallas kernels, attend(): pl.pallas_call(functools.partial(attend_kernel, cube, heads, group, [core...  99 us
    pallas_call x1, Pallas kernels, attend_back(): pl.pallas_call(functools.partial(attend_back_kernel, cube, heads, group,...  96.7 us
    pallas_call x1, Pallas kernels, start(): pl.pallas_call(functools.partial(start_kernel, cube, heads), out_shape=(j...  49.1 us
    pallas_call x1, Pallas kernels, end(): pl.pallas_call(functools.partial(end_kernel, cube, heads), out_shape=(jax...  42.9 us
    unnamed x80, local copies, waits for them, and re-layouts  12.8 us
  transfers between devices with their start and end apart: 5, of which 0 were waited for; matrix products, arithmetic and copies ran while one was open for 8% of the time, Pallas kernels for 26%

profile of v5, /device:TPU:0, one launch (start us, length us, event | category | flops | bytes accessed | tf_op | source)
XLA Modules:
  0.0 540.6 jit_solution(3727746351467423770)
XLA Ops:
  1.5 1.0 broadcast_in_dim_reshape.9.refs_3_
  4.0 1.0 copy.212
  5.7 1.3 constant_dynamic-slice_fusion.8
  7.0 1.1 pad_maximum_fusion.refs_2_
  8.1 49.1 %start.1 = (bf16[2,4,64,1536]{3,2,1,0:T(8,128)(2,1)}, bf16[4,2,4,48,768]{4,3,2,1,0:T(8,128)(2,1)}, bf16[10,192,256]{2,1,0:T(8,128)(2,1)}, s32[1,1024]{1,0:T(1,128)}) custom-call(bf16[2,64,1536]{2,1,0:T(8,128)(2,1)} %refs_0_.1, bf16[4,48,768]{2,1,0:T(8,128)(2,1)} %pad_maximum_fusion.4.refs_1_, bf16[10,192,256]{2,1,0:T(8,128)(2,1)} %pad_maximum_fusion.refs_2_, ...), custom_call_target="tpu_custom_call" | custom-call | tf_op jit(solution)/shard_map/start/pallas_call | solution.py:1154
  57.2 3.0 constant_dynamic-slice_fusion.1
  60.2 1.2 pad_maximum_fusion.2
  61.3 1.1 collective-permute-start
  62.5 1.1 pad_maximum_fusion.3
  63.6 1.2 fusion.22
  65.4 1.2 copy.205
  67.0 2.3 copy.169
  69.8 1.4 copy-done.22
  71.2 1.2 fusion.23
  73.8 2.0 copy.172.refs_2_
  75.9 99.0 %attend.1 = (bf16[4,128,384]{2,1,0:T(8,128)(2,1)S(1)}, bf16[4,2,2,256,256]{4,3,2,1,0:T(8,128)(2,1)}, f32[4,64,768]{2,1,0:T(8,128)S(1)}, f32[4,1,768]{2,1,0:T(1,1...) custom-call(bf16[4,768,64]{2,1,0:T(8,128)(2,1)S(1)} %bitcast.99, ...), custom_call_target="tpu_custom_call" | custom-call | tf_op jit(solution)/shard_map/attend/pallas_call | solution.py:1806
  174.9 0.9 copy-done.6
  176.0 0.7 copy-done.20
  176.8 3.2 multiply_reduce_fusion.5
  180.0 1.3 copy.206
  181.7 1.3 fusion.12
  183.5 1.6 copy.191
  185.2 0.9 copy.193
  187.0 0.9 concatenate.46.refs_0_
  187.9 1.1 pad_maximum_fusion.1.refs_3_
  189.0 158.0 %expert_turn.1 = (f32[128,1664]{1,0:T(8,128)}, bf16[2048,1536]{1,0:T(8,128)(2,1)}, bf16[4,10,192,256]{3,2,1,0:T(8,128)(2,1)}, bf16[4,10,192,256]{3,2,1,0:T(8,128...) custom-call(bf16[128,1664]{1,0:T(8,128)(2,1)} %concatenate.46.refs_0_, ...), custom_call_target="tpu_custom_call" | custom-call | tf_op jit(solution)/shard_map/expert_turn/pallas_call | solution.py:959
  346.9 0.9 slice.76
  348.0 2.0 multiply_reduce_fusion.2
  350.3 4.3 convolution_convert_fusion.1
  354.6 3.6 convolution_convert_fusion
  358.4 0.9 copy.184
  359.4 96.7 %attend_back.1 = (bf16[4,768,64]{2,1,0:T(8,128)(2,1)}, f32[512,256]{1,0:T(8,128)}, f32[128,1536]{1,0:T(8,128)}, f32[48,1536]{1,0:T(8,128)}, bf16[10,192,256]{2,1...) custom-call(bf16[4,768,64]{2,1,0:T(8,128)(2,1)} %bitcast.100, ...), custom_call_target="tpu_custom_call" | custom-call | tf_op jit(solution)/shard_map/attend_back/pallas_call | solution.py:2041
  456.1 1.1 convert_element_type.174
  459.3 0.8 add_convert_fusion
  460.5 1.7 collective-permute-start.3
  462.1 1.5 collective-permute-start.4
  465.9 2.7 fusion.1
  468.7 2.7 convolution_convert_fusion.2
  471.4 0.8 convolution_convert_fusion.3
  473.9 0.8 broadcast_in_dim.85
  474.7 3.6 concatenate.55.in_ref
  478.3 1.4 copy-done.3
  479.7 42.9 %end.1 = (bf16[4,2,64,1536]{3,2,1,0:T(8,128)(2,1)S(1)}, bf16[4,48,768]{2,1,0:T(8,128)(2,1)S(1)}) custom-call(bf16[2,4,64,1536]{3,2,1,0:T(8,128)(2,1)S(1)} %bitcast.101, bf16[4,2,192,768]{3,2,1,0:T(8,128)(2,1)S(1)} %concatenate.55.in_ref), custom_call_target="tpu_custom_call" | custom-call | tf_op jit(solution)/shard_map/end/pallas_call | solution.py:1274
  522.6 1.1 copy-done.1
  523.8 0.8 copy.209
  526.0 4.1 convert_add_fusion
  531.5 1.2 fusion.6
  532.7 6.7 %place_units.1 = f32[10,192,1024]{2,1,0:T(8,128)} custom-call(bf16[10,192,256]{2,1,0:T(8,128)(2,1)} %get-tuple-element.69.refs_0_, bf16[10,192,256]{2,1,0:T(8,128)(2,1)} %collective-permute-done.2.refs_1_, bf16[10,192,256]{2,1,0:T(8,128)(2,1)} %collective-permute-done.3.refs_2_, bf16[10,192,256]{2,1,0:T(8,128)(2,1)} %collective-permute-done.4.refs_3_), custom_call_target="tpu_custom_call" | custom-call | tf_op jit(solution)/shard_map/place_units/pallas_call | solution.py:1317
  (155 shorter events, 18.5 us)
Async XLA Ops:
  60.2 3.4 copy-start.18
  61.3 127.6 %collective-permute-start = (bf16[10,192,256]{2,1,0:T(8,128)(2,1)}, bf16[10,192,256]{2,1,0:T(8,128)(2,1)}, u32[]{:S(2)}, u32[]{:S(2)}) collective-permute-start(bf16[10,192,256]{2,1,0:T(8,128)(2,1)} %pad_maximum_fusion.2), channel_id=1, source_target_pairs={{0,8},{8,0},{16,24},{24,16},{1,9},{9,1},{17,25},{25,17},{2,10},{10... | collective-permute-start | bytes 2949128 | tf_op jit(solution)/shard_map/ppermute | solution.py:1330
  63.5 125.4 %collective-permute-start.1 = (bf16[10,192,256]{2,1,0:T(8,128)(2,1)}, bf16[10,192,256]{2,1,0:T(8,128)(2,1)}, u32[]{:S(2)}, u32[]{:S(2)}) collective-permute-start(bf16[10,192,256]{2,1,0:T(8,128)(2,1)} %pad_maximum_fusion.3), channel_id=1, source_target_pairs={{0,16},{8,24},{16,0},{24,8},{1,17},{9,25},{17,1},{25,9},{2,18},{10... | collective-permute-start | bytes 2949128 | tf_op jit(solution)/shard_map/ppermute | solution.py:1330
  64.7 1.9 copy-start.14
  69.3 1.9 copy-start.22
  69.8 2.7 copy-start.16
  71.2 1.3 copy-start.35
  72.4 0.7 copy-start.31
  72.9 0.9 copy-start.32
  73.2 2.6 copy-start.4
  73.2 2.6 copy-start.7
  73.6 101.2 %copy-start = (bf16[2,2,3,256,64]{4,3,2,1,0:T(8,128)(2,1)}, bf16[2,2,3,256,64]{4,3,2,1,0:T(8,128)(2,1)S(1)}, u32[]{:S(2)}) copy-start(bf16[2,2,3,256,64]{4,3,2,1,0:T(8,128)(2,1)S(1)} %copy.170) | copy-start | bytes 1179652
  75.8 100.2 %copy-start.8 = (s32[2,1,768]{2,1,0:T(1,128)}, s32[2,1,768]{2,1,0:T(1,128)S(1)}, u32[]{:S(2)}) copy-start(s32[2,1,768]{2,1,0:T(1,128)S(1)} %tile.10.refs_3_) | copy-start | bytes 18436
  75.9 100.9 %copy-start.12 = (bf16[2,64,1536]{2,1,0:T(8,128)(2,1)S(1)}, bf16[2,64,1536]{2,1,0:T(8,128)(2,1)}, u32[]{:S(2)}) copy-start(bf16[2,64,1536]{2,1,0:T(8,128)(2,1)} %refs_0_.1) | copy-start | bytes 1179652
  174.9 0.9 copy-start.6
  175.7 4.3 copy-start.9
  176.0 0.8 copy-start.20
  176.8 4.6 copy-start.33
  180.0 3.5 copy-start.17
  185.1 2.8 copy-start.23
  185.1 2.8 copy-start.24
  346.9 3.1 copy-start.5
  350.3 4.3 copy-start.10
  350.3 4.3 copy-start.21
  456.1 2.0 copy-start.28
  458.2 1.1 copy-start.29
  460.1 70.1 %collective-permute-start.2 = (bf16[10,192,256]{2,1,0:T(8,128)(2,1)}, bf16[10,192,256]{2,1,0:T(8,128)(2,1)}, u32[]{:S(2)}, u32[]{:S(2)}) collective-permute-start(bf16[10,192,256]{2,1,0:T(8,128)(2,1)} %get-tuple-element.60), channel_id=1, source_target_pairs={{0,8},{8,0},{16,24},{24,16},{1,9},{9,1},{17,25},{25,17},{2,10},{10... | collective-permute-start | bytes 2949128 | tf_op jit(solution)/shard_map/ppermute | solution.py:1330
  460.5 69.7 %collective-permute-start.3 = (bf16[10,192,256]{2,1,0:T(8,128)(2,1)}, bf16[10,192,256]{2,1,0:T(8,128)(2,1)}, u32[]{:S(2)}, u32[]{:S(2)}) collective-permute-start(bf16[10,192,256]{2,1,0:T(8,128)(2,1)} %get-tuple-element.61), channel_id=1, source_target_pairs={{0,16},{8,24},{16,0},{24,8},{1,17},{9,25},{17,1},{25,9},{2,18},{10... | collective-permute-start | bytes 2949128 | tf_op jit(solution)/shard_map/ppermute | solution.py:1330
  462.1 68.1 %collective-permute-start.4 = (bf16[10,192,256]{2,1,0:T(8,128)(2,1)}, bf16[10,192,256]{2,1,0:T(8,128)(2,1)}, u32[]{:S(2)}, u32[]{:S(2)}) collective-permute-start(bf16[10,192,256]{2,1,0:T(8,128)(2,1)} %get-tuple-element.62), channel_id=1, source_target_pairs={{0,24},{8,16},{16,8},{24,0},{1,25},{9,17},{17,9},{25,1},{2,26},{10... | collective-permute-start | bytes 2949128 | tf_op jit(solution)/shard_map/ppermute | solution.py:1330
  463.8 1.4 copy-start.15
  463.8 2.1 copy-start.19
  465.9 2.8 copy-start.26
  468.7 2.7 copy-start.27
  478.3 1.4 copy-start.3
  522.6 1.1 copy-start.1
  523.7 2.3 copy-start.25
  526.0 4.2 copy-start.2
  530.2 1.0 copy-start.13
  530.2 1.3 copy-start.11
  530.2 1.3 copy-start.34
  532.7 6.7 %copy-start.30 = (f32[48,1536]{1,0:T(8,128)S(1)}, f32[48,1536]{1,0:T(8,128)}, u32[]{:S(2)}) copy-start(f32[48,1536]{1,0:T(8,128)} %get-tuple-element.150) | copy-start | bytes 884740

commit v6 on v5

--- a/solution.py
+++ b/solution.py
@@ -1177,8 +1177,9 @@
     )(x, slices, unit, keys[:, None], keys[None, :])
 
 
-def end_kernel(cube, heads, first_ref, in_ref, first_out, out_ref, *refs):
+def end_kernel(cube, heads, first_ref, left_ref, right_ref, extra_ref, first_out, out_ref, *refs):
     count = cube.number
+    in_ref, refs = refs[0], refs[1:]
     arrived = refs[:count]
     parts = refs[count : 2 * count]
     local, first_send, first_recv, line_send, line_recv, send, recv = refs[2 * count :]
@@ -1215,6 +1216,19 @@
             device_id_type=MESH,
         )
 
+    for d in others:
+        first_copy(d).start()
+    strip = extra_ref.shape[0] // cube.chips
+    product = right_ref.shape[1]
+    for chip in range(cube.chips):
+        rows_here = pl.ds(chip * strip, strip)
+        value = lax.dot_general(
+            left_ref[:, rows_here], right_ref[...], TN, preferred_element_type=f32
+        )
+        in_ref[chip, :, :, pl.ds(0, product)] = value.astype(bf16).reshape(2, strip // 2, product)
+        in_ref[chip, :, :, pl.ds(product, LANES)] = extra_ref[rows_here, :].reshape(
+            2, strip // 2, LANES
+        )
     for k in range(count):
         for side in range(2):
             order = cube.scatter_orders[side]
@@ -1235,9 +1249,6 @@
                     device_id_type=MESH,
                 )
                 copies[(side, k, mask)].start()
-        if k == 0:
-            for d in others:
-                first_copy(d).start()
     done = parts[count - 1]
     for side in range(2):
         done[0, pl.ds(side * half, half)] = total(side, count, 0)
@@ -1265,8 +1276,8 @@
         first_copy(d).wait()
 
 
-def end(first, sums, chips, heads, number):
-    rows, columns = sums.shape[-2:]
+def end(first, left, right, extra, chips, heads, number):
+    rows, columns = extra.shape[0] // (2 * chips), right.shape[1] + LANES
     cube = Cube(chips, True)
     count = cube.number
     half = rows // 2
@@ -1277,9 +1288,10 @@
             jax.ShapeDtypeStruct((heads, first.shape[0]) + first.shape[2:], bf16),
             jax.ShapeDtypeStruct((heads, rows // heads, columns), bf16),
         ),
-        in_specs=[ANY, WHOLE],
+        in_specs=[ANY] + [WHOLE] * 3,
         out_specs=(ANY, WHOLE),
-        scratch_shapes=[pltpu.VMEM((2, s, half, columns), bf16) for s in slots]
+        scratch_shapes=[pltpu.VMEM((chips, 2, rows, columns), bf16)]
+        + [pltpu.VMEM((2, s, half, columns), bf16) for s in slots]
         + [pltpu.VMEM((2, s, half, columns), bf16) for s in slots[1:]]
         + [
             pltpu.VMEM((1, rows, columns), bf16),
@@ -1294,8 +1306,11 @@
         compiler_params=pltpu.CompilerParams(
             collective_id=number, has_side_effects=True, vmem_limit_bytes=40 << 20
         ),
+        cost_estimate=pl.CostEstimate(
+            flops=50_000_000_000, bytes_accessed=150_000_000, transcendentals=0
+        ),
         name="end",
-    )(first, sums)
+    )(first, left, right, extra)
 
 
 def place_kernel(chips, hidden, *refs):
@@ -2365,10 +2380,8 @@
     )
     grad_first_part = jnp.dot(grad_qkv, dense_qkv.T, preferred_element_type=f32)
     grad_gain_attn = jnp.sum(grad_first_part * normed_line, axis=0)
-    grad_dense_qkv = jnp.dot(first_line.T, grad_qkv, preferred_element_type=f32)
-    sums = jnp.concatenate(
+    extras = jnp.concatenate(
         [
-            grad_dense_qkv,
             grad_router,
             grad_gain_attn[:, None],
             grad_gain_ffn[:, None],
@@ -2379,15 +2392,20 @@
     if fused:
         grad_first, sums = end(
             grad_first_part.astype(bf16).reshape(sequence_batch, head_number, token_rows, width),
-            sums.reshape(chips, 2, head_number * dense_rows, loc_columns + LANES),
+            first_line,
+            grad_qkv,
+            extras,
             chips,
             head_number,
             13,
         )
-        pieces, grad_first = lax.optimization_barrier((pieces, grad_first))
+        pieces, grad_first, sums = lax.optimization_barrier((pieces, grad_first, sums))
+        up_share = place_units(pieces, hidden)
+        up_share, grad_first, sums, moe, down_share = lax.optimization_barrier(
+            (up_share, grad_first, sums, moe, down_share)
+        )
         grad_first = jnp.sum(grad_first.astype(f32), axis=0).reshape(tokens_present, width)
         sums = sums.astype(f32)
-        up_share = place_units(pieces, hidden)
     else:
         grad_first = jnp.sum(
             line_exchange(
@@ -2397,6 +2415,8 @@
             ).astype(f32),
             axis=0,
         )
+        grad_dense_qkv = jnp.dot(first_line.T, grad_qkv, preferred_element_type=f32)
+        sums = jnp.concatenate([grad_dense_qkv.astype(bf16), extras], axis=1)
         sums = scatter_sum(
             sums.reshape(chips, 2, head_number * dense_rows, loc_columns + LANES), chips, 1, True, 11
         )

time: 549 us -> 556 us (1.013)
  Pallas kernels: 452 us -> 464 us
  local copies, waits for them, and re-layouts: 42.2 us -> 35 us
    pallas_call x1, Pallas kernels: 42.9 us -> 56.1 us  [end(): pl.pallas_call(functools.partial(end_kernel, cube, heads), out_shape=(jax...]
    unnamed x80 -> x82, local copies, waits for them, and re-layouts: 12.8 us -> 7.47 us
  transfers between devices with their start and end apart: 5 -> 5, of which waited for: 0 -> 0; matrix products, arithmetic and copies ran while one was open for 8% -> 6% of each run, Pallas kernels for 26% -> 28%
where the time goes in v6:
time: 556 us; the launch traced here: 547 us
  Pallas kernels  464 us (83%)
  local copies, waits for them, and re-layouts  35 us (6%)
  matrix products  22.4 us (4%)
  other arithmetic  18.6 us (3%)
    pallas_call x1, Pallas kernels, expert_turn(): pl.pallas_call(functools.partial(turn_kernel, cube, heads, hidden), out_s...  159 us
    pallas_call x1, Pallas kernels, attend_back(): pl.pallas_call(functools.partial(attend_back_kernel, cube, heads, group,...  96.6 us
    pallas_call x1, Pallas kernels, attend(): pl.pallas_call(functools.partial(attend_kernel, cube, heads, group, [core...  96.2 us
    pallas_call x1, Pallas kernels, end(): pl.pallas_call(functools.partial(end_kernel, cube, heads), out_shape=(jax...  56.1 us
    pallas_call x1, Pallas kernels, start(): pl.pallas_call(functools.partial(start_kernel, cube, heads), out_shape=(j...  49.1 us
  transfers between devices with their start and end apart: 5, of which 0 were waited for; matrix products, arithmetic and copies ran while one was open for 6% of the time, Pallas kernels for 28%

profile of v6, /device:TPU:0, one launch (start us, length us, event | category | flops | bytes accessed | tf_op | source)
XLA Modules:
  0.0 546.9 jit_solution(13192661854239403051)
XLA Ops:
  0.7 0.7 multiply_add_fusion.2
  2.2 1.0 broadcast_in_dim_reshape.9.refs_3_
  3.2 0.7 pad_maximum_fusion.9
  4.0 1.0 copy.204
  5.0 0.7 pad_maximum_fusion.5.refs_1_
  5.8 1.3 constant_dynamic-slice_fusion.8
  7.0 1.1 pad_maximum_fusion.refs_2_
  8.1 49.1 %start.1 = (bf16[2,4,64,1536]{3,2,1,0:T(8,128)(2,1)}, bf16[4,2,4,48,768]{4,3,2,1,0:T(8,128)(2,1)}, bf16[10,192,256]{2,1,0:T(8,128)(2,1)}, s32[1,1024]{1,0:T(1,128)}) custom-call(bf16[2,64,1536]{2,1,0:T(8,128)(2,1)} %refs_0_.1, bf16[4,48,768]{2,1,0:T(8,128)(2,1)} %pad_maximum_fusion.5.refs_1_, bf16[10,192,256]{2,1,0:T(8,128)(2,1)} %pad_maximum_fusion.refs_2_, ...), custom_call_target="tpu_custom_call" | custom-call | tf_op jit(solution)/shard_map/start/pallas_call | solution.py:1154
  57.2 3.1 constant_dynamic-slice_fusion.1
  60.2 1.2 pad_maximum_fusion.2
  61.4 1.1 collective-permute-start
  62.5 1.1 pad_maximum_fusion.3
  65.4 2.3 fusion.22
  67.7 1.8 slice_bitcast_fusion
  70.2 1.8 copy.197
  72.6 1.6 multiply_convert_fusion.1
  74.2 2.3 copy.165
  76.5 2.8 fusion.23
  80.1 2.0 copy.168.refs_2_
  83.3 96.2 %attend.1 = (bf16[4,128,384]{2,1,0:T(8,128)(2,1)S(1)}, bf16[4,2,2,256,256]{4,3,2,1,0:T(8,128)(2,1)}, f32[4,64,768]{2,1,0:T(8,128)S(1)}, f32[4,1,768]{2,1,0:T(1,1...) custom-call(bf16[4,768,64]{2,1,0:T(8,128)(2,1)S(1)} %bitcast.84, ...), custom_call_target="tpu_custom_call" | custom-call | tf_op jit(solution)/shard_map/attend/pallas_call | solution.py:1821
  179.5 0.9 copy-done.3
  180.6 3.4 multiply_reduce_fusion.6
  184.2 1.5 fusion.13
  187.0 0.9 concatenate.43.refs_0_
  187.9 1.1 pad_maximum_fusion.1.refs_3_
  189.0 159.1 %expert_turn.1 = (f32[128,1664]{1,0:T(8,128)}, bf16[2048,1536]{1,0:T(8,128)(2,1)}, bf16[4,10,192,256]{3,2,1,0:T(8,128)(2,1)}, bf16[4,10,192,256]{3,2,1,0:T(8,128...) custom-call(bf16[128,1664]{1,0:T(8,128)(2,1)} %concatenate.43.refs_0_, bf16[2048,1536]{1,0:T(8,128)(2,1)} %bitcast.93, ...), custom_call_target="tpu_custom_call" | custom-call | tf_op jit(solution)/shard_map/expert_turn/pallas_call | solution.py:959
  348.1 0.9 slice.78
  349.2 1.3 convolution_convert_fusion.2
  350.5 2.0 multiply_reduce_fusion.4
  352.8 4.3 convolution_convert_fusion.1
  357.1 3.6 convolution_convert_fusion
  360.9 0.9 copy.180
  361.8 0.9 copy.188
  362.8 1.0 broadcast_in_dim.95
  363.8 96.6 %attend_back.1 = (bf16[4,768,64]{2,1,0:T(8,128)(2,1)}, f32[512,256]{1,0:T(8,128)}, f32[128,1536]{1,0:T(8,128)}, f32[48,1536]{1,0:T(8,128)}, bf16[10,192,256]{2,1...) custom-call(bf16[4,768,64]{2,1,0:T(8,128)(2,1)} %bitcast.85, ...), custom_call_target="tpu_custom_call" | custom-call | tf_op jit(solution)/shard_map/attend_back/pallas_call | solution.py:2056
  460.4 1.1 convert_element_type.154
  463.6 0.9 copy.202
  464.6 1.4 copy.191.right_ref
  466.0 3.6 multiply_reduce_fusion
  470.6 2.1 collective-permute-start.3
  472.6 1.4 collective-permute-start.4
  474.5 56.1 %end.1 = (bf16[4,2,64,1536]{3,2,1,0:T(8,128)(2,1)S(1)}, bf16[4,48,768]{2,1,0:T(8,128)(2,1)S(1)}) custom-call(bf16[2,4,64,1536]{3,2,1,0:T(8,128)(2,1)S(1)} %bitcast.88, bf16[512,1536]{1,0:T(8,128)(2,1)S(1)} %get-tuple-element.139.left_ref, bf16[512,640]{1,0:T(8,128)(2,1)S(1)} %copy.191.right_ref, bf16[1536,128]{1,0:T(8,128)(2,1)S(1)} %maximum_maximum_fusion.extra_ref), custom_call_target="tpu_custom_call" | custom-call | flops 49999998976 | bytes 150000000 | tf_op jit(solution)/shard_map/end/pallas_call | solution.py:1285
  530.6 2.5 convert_add_fusion
  533.1 6.7 %place_units.1 = f32[10,192,1024]{2,1,0:T(8,128)} custom-call(bf16[10,192,256]{2,1,0:T(8,128)(2,1)} %get-tuple-element.72.refs_0_, bf16[10,192,256]{2,1,0:T(8,128)(2,1)} %collective-permute-done.2.refs_1_, bf16[10,192,256]{2,1,0:T(8,128)(2,1)} %collective-permute-done.3.refs_2_, bf16[10,192,256]{2,1,0:T(8,128)(2,1)} %collective-permute-done.4.refs_3_), custom_call_target="tpu_custom_call" | custom-call | tf_op jit(solution)/shard_map/place_units/pallas_call | solution.py:1332
  539.9 1.0 copy-done.25
  541.0 0.8 add_convert_fusion
  541.8 0.8 copy.201
  544.6 1.2 fusion.4
  (154 shorter events, 14.2 us)
Async XLA Ops:
  60.2 4.5 copy-start.27
  61.4 127.6 %collective-permute-start = (bf16[10,192,256]{2,1,0:T(8,128)(2,1)}, bf16[10,192,256]{2,1,0:T(8,128)(2,1)}, u32[]{:S(2)}, u32[]{:S(2)}) collective-permute-start(bf16[10,192,256]{2,1,0:T(8,128)(2,1)} %pad_maximum_fusion.2), channel_id=1, source_target_pairs={{0,8},{8,0},{16,24},{24,16},{1,9},{9,1},{17,25},{25,17},{2,10},{10... | collective-permute-start | bytes 2949128 | tf_op jit(solution)/shard_map/ppermute | solution.py:1345
  63.6 125.4 %collective-permute-start.1 = (bf16[10,192,256]{2,1,0:T(8,128)(2,1)}, bf16[10,192,256]{2,1,0:T(8,128)(2,1)}, u32[]{:S(2)}, u32[]{:S(2)}) collective-permute-start(bf16[10,192,256]{2,1,0:T(8,128)(2,1)} %pad_maximum_fusion.3), channel_id=1, source_target_pairs={{0,16},{8,24},{16,0},{24,8},{1,17},{9,25},{17,1},{25,9},{2,18},{10... | collective-permute-start | bytes 2949128 | tf_op jit(solution)/shard_map/ppermute | solution.py:1345
  67.7 2.0 copy-start.11
  74.2 2.3 copy-start.20
  76.5 2.8 copy-start.31
  76.5 2.8 copy-start.33
  79.3 0.7 copy-start.29
  79.3 0.7 copy-start.28
  79.7 2.4 copy-start.30
  79.7 2.6 copy-start.22
  80.0 3.2 copy-start.5
  82.1 1.1 copy-start.1
  82.1 1.1 copy-start.4
  83.2 97.4 %copy-start = (bf16[2,2,3,256,64]{4,3,2,1,0:T(8,128)(2,1)}, bf16[2,2,3,256,64]{4,3,2,1,0:T(8,128)(2,1)S(1)}, u32[]{:S(2)}) copy-start(bf16[2,2,3,256,64]{4,3,2,1,0:T(8,128)(2,1)S(1)} %copy.166) | copy-start | bytes 1179652
  83.3 97.4 %copy-start.9 = (bf16[2,64,1536]{2,1,0:T(8,128)(2,1)S(1)}, bf16[2,64,1536]{2,1,0:T(8,128)(2,1)}, u32[]{:S(2)}) copy-start(bf16[2,64,1536]{2,1,0:T(8,128)(2,1)} %refs_0_.1) | copy-start | bytes 1179652
  179.5 0.9 copy-start.3
  180.4 3.6 copy-start.6
  180.6 3.4 copy-start.14
  184.0 3.9 copy-start.16
  184.0 3.9 copy-start.17
  184.2 4.8 copy-start.13
  348.1 4.4 copy-start.2
  352.8 4.3 copy-start.7
  352.8 4.3 copy-start.15
  460.3 2.0 copy-start.24
  462.9 3.0 copy-start.12
  466.0 4.0 copy-start.36
  466.0 4.6 copy-start.35
  466.0 6.7 %copy-start.34 = (bf16[10,192,256]{2,1,0:T(8,128)(2,1)S(1)}, bf16[10,192,256]{2,1,0:T(8,128)(2,1)}, u32[]{:S(2)}) copy-start(bf16[10,192,256]{2,1,0:T(8,128)(2,1)} %get-tuple-element.67) | copy-start | bytes 2949124
  466.0 8.1 %copy-start.21 = (bf16[1536,1]{1,0:T(8,128)(2,1)S(1)}, bf16[1536,1]{1,0:T(8,128)(2,1)}, u32[]{:S(2)}) copy-start(bf16[1536,1]{1,0:T(8,128)(2,1)} %broadcast_in_dim.95) | copy-start | bytes 9220
  466.0 8.1 %copy-start.23 = (bf16[1536,40]{1,0:T(8,128)(2,1)S(1)}, bf16[1536,40]{1,0:T(8,128)(2,1)}, u32[]{:S(2)}) copy-start(bf16[1536,40]{1,0:T(8,128)(2,1)} %copy.188) | copy-start | bytes 368644
  469.9 63.2 %collective-permute-start.2 = (bf16[10,192,256]{2,1,0:T(8,128)(2,1)S(1)}, bf16[10,192,256]{2,1,0:T(8,128)(2,1)}, u32[]{:S(2)}, u32[]{:S(2)}) collective-permute-start(bf16[10,192,256]{2,1,0:T(8,128)(2,1)S(1)} %copy-done.36), channel_id=1, source_target_pairs={{0,8},{8,0},{16,24},{24,16},{1,9},{9,1},{17,25},{25,17},{2,10},{10... | collective-permute-start | bytes 2949128 | tf_op jit(solution)/shard_map/ppermute | solution.py:1345
  470.6 62.6 %collective-permute-start.3 = (bf16[10,192,256]{2,1,0:T(8,128)(2,1)S(1)}, bf16[10,192,256]{2,1,0:T(8,128)(2,1)}, u32[]{:S(2)}, u32[]{:S(2)}) collective-permute-start(bf16[10,192,256]{2,1,0:T(8,128)(2,1)S(1)} %copy-done.35), channel_id=1, source_target_pairs={{0,16},{8,24},{16,0},{24,8},{1,17},{9,25},{17,1},{25,9},{2,18},{10... | collective-permute-start | bytes 2949128 | tf_op jit(solution)/shard_map/ppermute | solution.py:1345
  472.6 60.5 %collective-permute-start.4 = (bf16[10,192,256]{2,1,0:T(8,128)(2,1)S(1)}, bf16[10,192,256]{2,1,0:T(8,128)(2,1)}, u32[]{:S(2)}, u32[]{:S(2)}) collective-permute-start(bf16[10,192,256]{2,1,0:T(8,128)(2,1)S(1)} %copy-done.34), channel_id=1, source_target_pairs={{0,24},{8,16},{16,8},{24,0},{1,25},{9,17},{17,9},{25,1},{2,26},{10... | collective-permute-start | bytes 2949128 | tf_op jit(solution)/shard_map/ppermute | solution.py:1345
  474.5 56.1 %copy-start.18 = (bf16[10,64,1536]{2,1,0:T(8,128)(2,1)S(1)}, bf16[10,64,1536]{2,1,0:T(8,128)(2,1)}, u32[]{:S(2)}) copy-start(bf16[10,64,1536]{2,1,0:T(8,128)(2,1)} %get-tuple-element.79) | copy-start | bytes 5898244
  474.5 56.1 %copy-start.19 = (bf16[10,64,1536]{2,1,0:T(8,128)(2,1)S(1)}, bf16[10,64,1536]{2,1,0:T(8,128)(2,1)}, u32[]{:S(2)}) copy-start(bf16[10,64,1536]{2,1,0:T(8,128)(2,1)} %get-tuple-element.80) | copy-start | bytes 5898244
  539.8 1.1 copy-start.25
  541.8 2.4 copy-start.10
  541.8 2.8 copy-start.8
  541.8 2.8 copy-start.32
  544.2 1.6 copy-start.26

commit v7 on v6

--- a/solution.py
+++ b/solution.py
@@ -1307,7 +1307,7 @@
             collective_id=number, has_side_effects=True, vmem_limit_bytes=40 << 20
         ),
         cost_estimate=pl.CostEstimate(
-            flops=50_000_000_000, bytes_accessed=150_000_000, transcendentals=0
+            flops=2000000000, bytes_accessed=1_000_000, transcendentals=0
         ),
         name="end",
     )(first, left, right, extra)
@@ -2390,6 +2390,9 @@
         axis=1,
     ).astype(bf16)
     if fused:
+        x_again, gain_again, grad_qkv = lax.optimization_barrier((x_line, gain_attn, grad_qkv))
+        scale_again = lax.rsqrt(jnp.mean(x_again * x_again, axis=1, keepdims=True) + epsilon)
+        first_line = (x_again * scale_again * gain_again).astype(bf16)
         grad_first, sums = end(
             grad_first_part.astype(bf16).reshape(sequence_batch, head_number, token_rows, width),
             first_line,

time: 556 us -> 547 us (0.984)
  Pallas kernels: 464 us -> 453 us
    pallas_call x1, Pallas kernels: 56.1 us -> 42.8 us  [end(): pl.pallas_call(functools.partial(end_kernel, cube, heads), out_shape=(jax...]
  transfers between devices with their start and end apart: 5 -> 5, of which waited for: 0 -> 0; matrix products, arithmetic and copies ran while one was open for 6% -> 7% of each run, Pallas kernels for 28% -> 26%
where the time goes in v7:
time: 547 us; the launch traced here: 538 us
  Pallas kernels  453 us (83%)
  local copies, waits for them, and re-layouts  36.3 us (7%)
  other arithmetic  23.1 us (4%)
  matrix products  18.9 us (3%)
    pallas_call x1, Pallas kernels, expert_turn(): pl.pallas_call(functools.partial(turn_kernel, cube, heads, hidden), out_s...  159 us
    pallas_call x1, Pallas kernels, attend(): pl.pallas_call(functools.partial(attend_kernel, cube, heads, group, [core...  98.9 us
    pallas_call x1, Pallas kernels, attend_back(): pl.pallas_call(functools.partial(attend_back_kernel, cube, heads, group,...  96.7 us
    pallas_call x1, Pallas kernels, start(): pl.pallas_call(functools.partial(start_kernel, cube, heads), out_shape=(j...  49.1 us
    pallas_call x1, Pallas kernels, end(): pl.pallas_call(functools.partial(end_kernel, cube, heads), out_shape=(jax...  42.8 us
  transfers between devices with their start and end apart: 5, of which 0 were waited for; matrix products, arithmetic and copies ran while one was open for 7% of the time, Pallas kernels for 26%

profile of v7, /device:TPU:0, one launch (start us, length us, event | category | flops | bytes accessed | tf_op | source)
XLA Modules:
  0.0 537.9 jit_solution(1133863495555353634)
XLA Ops:
  1.5 1.0 broadcast_in_dim_reshape.9.refs_3_
  3.1 0.7 pad_maximum_fusion.9
  4.0 1.0 copy.204
  5.7 1.3 constant_dynamic-slice_fusion.8
  7.0 1.1 pad_maximum_fusion.refs_2_
  8.1 49.1 %start.1 = (bf16[2,4,64,1536]{3,2,1,0:T(8,128)(2,1)}, bf16[4,2,4,48,768]{4,3,2,1,0:T(8,128)(2,1)}, bf16[10,192,256]{2,1,0:T(8,128)(2,1)}, s32[1,1024]{1,0:T(1,128)}) custom-call(bf16[2,64,1536]{2,1,0:T(8,128)(2,1)} %refs_0_.1, bf16[4,48,768]{2,1,0:T(8,128)(2,1)} %pad_maximum_fusion.5.refs_1_, bf16[10,192,256]{2,1,0:T(8,128)(2,1)} %pad_maximum_fusion.refs_2_, ...), custom_call_target="tpu_custom_call" | custom-call | tf_op jit(solution)/shard_map/start/pallas_call | solution.py:1154
  57.2 3.0 constant_dynamic-slice_fusion.1
  60.2 1.1 pad_maximum_fusion.2
  61.3 1.1 collective-permute-start
  62.4 1.1 pad_maximum_fusion.3
  63.5 1.2 fusion.22
  65.4 1.2 copy.197
  67.0 2.3 copy.165
  69.7 1.1 copy-done.27
  70.8 1.2 fusion.23
  73.9 2.0 copy.168.refs_2_
  75.9 98.9 %attend.1 = (bf16[4,128,384]{2,1,0:T(8,128)(2,1)S(1)}, bf16[4,2,2,256,256]{4,3,2,1,0:T(8,128)(2,1)}, f32[4,64,768]{2,1,0:T(8,128)S(1)}, f32[4,1,768]{2,1,0:T(1,1...) custom-call(bf16[4,768,64]{2,1,0:T(8,128)(2,1)S(1)} %bitcast.82, ...), custom_call_target="tpu_custom_call" | custom-call | tf_op jit(solution)/shard_map/attend/pallas_call | solution.py:1821
  174.8 0.9 copy-done.3
  176.0 3.4 multiply_reduce_fusion.7
  180.1 1.4 fusion.13
  182.7 0.9 concatenate.43.refs_0_
  183.7 2.1 pad_maximum_fusion.1.refs_3_
  185.8 2.2 bitcast_convert_fusion
  188.0 158.8 %expert_turn.1 = (f32[128,1664]{1,0:T(8,128)}, bf16[2048,1536]{1,0:T(8,128)(2,1)}, bf16[4,10,192,256]{3,2,1,0:T(8,128)(2,1)}, bf16[4,10,192,256]{3,2,1,0:T(8,128...) custom-call(bf16[128,1664]{1,0:T(8,128)(2,1)} %concatenate.43.refs_0_, bf16[2048,1536]{1,0:T(8,128)(2,1)} %bitcast.91, ...), custom_call_target="tpu_custom_call" | custom-call | tf_op jit(solution)/shard_map/expert_turn/pallas_call | solution.py:959
  346.8 0.9 slice.78
  347.9 2.0 multiply_reduce_fusion.5
  350.3 4.3 convolution_convert_fusion.1
  354.6 3.6 convolution_convert_fusion
  358.6 0.9 copy.180
  359.6 96.7 %attend_back.1 = (bf16[4,768,64]{2,1,0:T(8,128)(2,1)}, f32[512,256]{1,0:T(8,128)}, f32[128,1536]{1,0:T(8,128)}, f32[48,1536]{1,0:T(8,128)}, bf16[10,192,256]{2,1...) custom-call(bf16[4,768,64]{2,1,0:T(8,128)(2,1)} %bitcast.83, ...), custom_call_target="tpu_custom_call" | custom-call | tf_op jit(solution)/shard_map/attend_back/pallas_call | solution.py:2056
  456.7 1.7 collective-permute-start.3
  458.4 1.4 collective-permute-start.4
  459.9 1.1 convert_element_type.161
  464.3 2.7 multiply_reduce_fusion
  467.9 0.9 copy.188
  468.8 2.3 multiply_convert_fusion.left_ref
  471.5 1.1 copy.191.right_ref
  472.5 1.1 copy-done.4
  473.6 1.4 copy-done.10
  475.0 42.8 %end.1 = (bf16[4,2,64,1536]{3,2,1,0:T(8,128)(2,1)S(1)}, bf16[4,48,768]{2,1,0:T(8,128)(2,1)S(1)}) custom-call(bf16[2,4,64,1536]{3,2,1,0:T(8,128)(2,1)S(1)} %bitcast.86, bf16[512,1536]{1,0:T(8,128)(2,1)S(1)} %multiply_convert_fusion.left_ref, bf16[512,640]{1,0:T(8,128)(2,1)S(1)} %copy-done.4, bf16[1536,128]{1,0:T(8,128)(2,1)S(1)} %maximum_maximum_fusion.extra_ref), custom_call_target="tpu_custom_call" | custom-call | flops 2000000000 | bytes 1000000 | tf_op jit(solution)/shard_map/end/pallas_call | solution.py:1285
  517.9 2.5 convert_add_fusion
  520.4 6.7 %place_units.1 = f32[10,192,1024]{2,1,0:T(8,128)} custom-call(bf16[10,192,256]{2,1,0:T(8,128)(2,1)} %get-tuple-element.78.refs_0_, bf16[10,192,256]{2,1,0:T(8,128)(2,1)} %collective-permute-done.2.refs_1_, bf16[10,192,256]{2,1,0:T(8,128)(2,1)} %collective-permute-done.3.refs_2_, bf16[10,192,256]{2,1,0:T(8,128)(2,1)} %collective-permute-done.4.refs_3_), custom_call_target="tpu_custom_call" | custom-call | tf_op jit(solution)/shard_map/place_units/pallas_call | solution.py:1332
  527.2 0.8 slice_bitcast_fusion.1
  528.7 0.8 add_convert_fusion
  530.1 1.8 copy.201
  532.0 1.5 slice_reduce_fusion.1
  533.5 1.4 copy.193
  534.9 1.9 fusion.4
  (164 shorter events, 15.7 us)
Async XLA Ops:
  60.2 3.3 copy-start.23
  61.3 126.7 %collective-permute-start = (bf16[10,192,256]{2,1,0:T(8,128)(2,1)}, bf16[10,192,256]{2,1,0:T(8,128)(2,1)}, u32[]{:S(2)}, u32[]{:S(2)}) collective-permute-start(bf16[10,192,256]{2,1,0:T(8,128)(2,1)} %pad_maximum_fusion.2), channel_id=1, source_target_pairs={{0,8},{8,0},{16,24},{24,16},{1,9},{9,1},{17,25},{25,17},{2,10},{10... | collective-permute-start | bytes 2949128 | tf_op jit(solution)/shard_map/ppermute | solution.py:1345
  63.5 124.5 %collective-permute-start.1 = (bf16[10,192,256]{2,1,0:T(8,128)(2,1)}, bf16[10,192,256]{2,1,0:T(8,128)(2,1)}, u32[]{:S(2)}, u32[]{:S(2)}) collective-permute-start(bf16[10,192,256]{2,1,0:T(8,128)(2,1)} %pad_maximum_fusion.3), channel_id=1, source_target_pairs={{0,16},{8,24},{16,0},{24,8},{1,17},{9,25},{17,1},{25,9},{2,18},{10... | collective-permute-start | bytes 2949128 | tf_op jit(solution)/shard_map/ppermute | solution.py:1345
  64.7 1.9 copy-start.14
  69.3 1.5 copy-start.27
  70.8 1.3 copy-start.39
  72.0 0.7 copy-start.36
  72.0 1.0 copy-start.19
  72.4 1.4 copy-start.37
  73.3 2.6 copy-start.1
  73.3 2.6 copy-start.7
  73.7 101.1 %copy-start = (bf16[2,2,3,256,64]{4,3,2,1,0:T(8,128)(2,1)}, bf16[2,2,3,256,64]{4,3,2,1,0:T(8,128)(2,1)S(1)}, u32[]{:S(2)}) copy-start(bf16[2,2,3,256,64]{4,3,2,1,0:T(8,128)(2,1)S(1)} %copy.166) | copy-start | bytes 1179652
  75.9 103.5 %copy-start.8 = (s32[2,1,768]{2,1,0:T(1,128)}, s32[2,1,768]{2,1,0:T(1,128)S(1)}, u32[]{:S(2)}) copy-start(s32[2,1,768]{2,1,0:T(1,128)S(1)} %tile.10.refs_3_) | copy-start | bytes 18436
  174.8 0.9 copy-start.3
  175.7 3.7 copy-start.9
  176.0 3.4 copy-start.25
  176.0 3.5 copy-start.31
  176.0 3.7 copy-start.38
  179.4 170.5 %copy-start.12 = (f32[128,1536]{1,0:T(8,128)}, f32[128,1536]{1,0:T(8,128)S(1)}, u32[]{:S(2)}) copy-start(f32[128,1536]{1,0:T(8,128)S(1)} %get-tuple-element.153) | copy-start | bytes 2359300
  179.4 4.3 copy-start.28
  180.1 7.9 %copy-start.21 = (bf16[128,1536]{1,0:T(8,128)(2,1)}, bf16[128,1536]{1,0:T(8,128)(2,1)S(1)}, u32[]{:S(2)}) copy-start(bf16[128,1536]{1,0:T(8,128)(2,1)S(1)} %multiply_convert_fusion.2) | copy-start | bytes 1179652
  180.1 5.7 %copy-start.15 = (bf16[2,4,64,1536]{3,2,1,0:T(8,128)(2,1)S(1)}, bf16[2,4,64,1536]{3,2,1,0:T(8,128)(2,1)}, u32[]{:S(2)}) copy-start(bf16[2,4,64,1536]{3,2,1,0:T(8,128)(2,1)} %get-tuple-element.52) | copy-start | bytes 4718596
  346.8 3.1 copy-start.2
  350.2 4.3 copy-start.17
  350.2 4.3 copy-start.26
  354.6 3.6 copy-start.22
  456.3 5.5 %copy-start.33 = (bf16[4,768,64]{2,1,0:T(8,128)(2,1)S(1)}, bf16[4,768,64]{2,1,0:T(8,128)(2,1)}, u32[]{:S(2)}) copy-start(bf16[4,768,64]{2,1,0:T(8,128)(2,1)} %get-tuple-element.71) | copy-start | bytes 1179652
  456.3 64.1 %collective-permute-start.2 = (bf16[10,192,256]{2,1,0:T(8,128)(2,1)}, bf16[10,192,256]{2,1,0:T(8,128)(2,1)}, u32[]{:S(2)}, u32[]{:S(2)}) collective-permute-start(bf16[10,192,256]{2,1,0:T(8,128)(2,1)} %get-tuple-element.68), channel_id=1, source_target_pairs={{0,8},{8,0},{16,24},{24,16},{1,9},{9,1},{17,25},{25,17},{2,10},{10... | collective-permute-start | bytes 2949128 | tf_op jit(solution)/shard_map/ppermute | solution.py:1345
  456.7 63.7 %collective-permute-start.3 = (bf16[10,192,256]{2,1,0:T(8,128)(2,1)}, bf16[10,192,256]{2,1,0:T(8,128)(2,1)}, u32[]{:S(2)}, u32[]{:S(2)}) collective-permute-start(bf16[10,192,256]{2,1,0:T(8,128)(2,1)} %get-tuple-element.69), channel_id=1, source_target_pairs={{0,16},{8,24},{16,0},{24,8},{1,17},{9,25},{17,1},{25,9},{2,18},{10... | collective-permute-start | bytes 2949128 | tf_op jit(solution)/shard_map/ppermute | solution.py:1345
  458.4 62.0 %collective-permute-start.4 = (bf16[10,192,256]{2,1,0:T(8,128)(2,1)}, bf16[10,192,256]{2,1,0:T(8,128)(2,1)}, u32[]{:S(2)}, u32[]{:S(2)}) collective-permute-start(bf16[10,192,256]{2,1,0:T(8,128)(2,1)} %get-tuple-element.70), channel_id=1, source_target_pairs={{0,24},{8,16},{16,8},{24,0},{1,25},{9,17},{17,9},{25,1},{2,26},{10... | collective-permute-start | bytes 2949128 | tf_op jit(solution)/shard_map/ppermute | solution.py:1345
  462.1 1.4 copy-start.16
  462.1 2.1 copy-start.24
  464.3 2.7 copy-start.11
  468.8 2.3 copy-start.32
  472.5 1.1 copy-start.4
  473.6 1.4 copy-start.10
  475.0 42.8 %copy-start.29 = (bf16[10,64,1536]{2,1,0:T(8,128)(2,1)S(1)}, bf16[10,64,1536]{2,1,0:T(8,128)(2,1)}, u32[]{:S(2)}) copy-start(bf16[10,64,1536]{2,1,0:T(8,128)(2,1)} %get-tuple-element.85) | copy-start | bytes 5898244
  475.0 42.8 %copy-start.30 = (bf16[10,64,1536]{2,1,0:T(8,128)(2,1)S(1)}, bf16[10,64,1536]{2,1,0:T(8,128)(2,1)}, u32[]{:S(2)}) copy-start(bf16[10,64,1536]{2,1,0:T(8,128)(2,1)} %get-tuple-element.86) | copy-start | bytes 5898244
  517.8 2.6 copy-start.5
  520.4 6.7 %copy-start.6 = (bf16[4,48,768]{2,1,0:T(8,128)(2,1)S(1)}, bf16[4,48,768]{2,1,0:T(8,128)(2,1)}, u32[]{:S(2)}) copy-start(bf16[4,48,768]{2,1,0:T(8,128)(2,1)} %copy-done.5) | copy-start | bytes 884740
  527.1 1.5 copy-start.13
  527.1 1.5 copy-start.34
  528.0 1.7 copy-start.20
  529.5 5.4 %copy-start.18 = (f32[128,1536]{1,0:T(8,128)S(1)}, f32[128,1536]{1,0:T(8,128)}, u32[]{:S(2)}) copy-start(f32[128,1536]{1,0:T(8,128)} %copy-done.17) | copy-start | bytes 2359300
  529.8 7.0 %copy-start.35 = (f32[48,1536]{1,0:T(8,128)S(1)}, f32[48,1536]{1,0:T(8,128)}, u32[]{:S(2)}) copy-start(f32[48,1536]{1,0:T(8,128)} %get-tuple-element.168) | copy-start | bytes 884740

commit v8 on v7

--- a/solution.py
+++ b/solution.py
@@ -1652,6 +1652,10 @@
 TN = (((0,), (0,)), ((), ()))
 
 
+def column_of(row):
+    return jnp.broadcast_to(row, (8, row.shape[1])).T[:, :1]
+
+
 def allowed(key_segments, query_segments, block, rows, seq):
     columns = query_segments.shape[1]
     key_place = block * rows + lax.broadcasted_iota(jnp.int32, (rows, columns), 0)
@@ -1728,7 +1732,7 @@
         place = (block // 2, block % 2)
         for b in range(batch):
             mask = allowed(
-                key_seg[b, pl.ds(pl.multiple_of(block * rows, rows), rows), :],
+                column_of(key_seg[b, :, pl.ds(pl.multiple_of(block * rows, rows), rows)]),
                 query_seg[b],
                 block,
                 rows,
@@ -1943,7 +1947,7 @@
         place = (block // 2, block % 2)
         for b in range(batch):
             mask = allowed(
-                key_seg[b, pl.ds(pl.multiple_of(block * rows, rows), rows), :],
+                column_of(key_seg[b, :, pl.ds(pl.multiple_of(block * rows, rows), rows)]),
                 query_seg[b],
                 block,
                 rows,
@@ -2243,9 +2247,9 @@
         .transpose(0, 2, 3, 1, 4)
         .reshape(pairs_here, query_group * blk, HEAD_WIDTH)
     )
-    key_seg = segments[:, :, None]
+    key_seg = segments[:, None, :].astype(f32)
     q_seg = lax.dynamic_slice_in_dim(segments, q_start, blk, 1)
-    query_seg = jnp.tile(q_seg[:, None, :], (1, 1, query_group))
+    query_seg = jnp.tile(q_seg[:, None, :].astype(f32), (1, 1, query_group))
     lines, kv_all, out_turned, lse, *beside = attend(
         queries,
         keys_values.reshape(sequence_batch, blk, kv_columns),

time: 547 us -> 549 us (level)
    unnamed x88 -> x110, local copies, waits for them, and re-layouts: 10.8 us -> 12.7 us
  transfers between devices with their start and end apart: 5 -> 5, of which waited for: 0 -> 0; matrix products, arithmetic and copies ran while one was open for 7% -> 7% of each run, Pallas kernels for 26% -> 27%
where the time goes in v8:
time: 549 us; the launch traced here: 540 us
  Pallas kernels  455 us (83%)
  local copies, waits for them, and re-layouts  37.3 us (7%)
  other arithmetic  22.4 us (4%)
  matrix products  18.9 us (3%)
    pallas_call x1, Pallas kernels, expert_turn(): pl.pallas_call(functools.partial(turn_kernel, cube, heads, hidden), out_s...  159 us
    pallas_call x1, Pallas kernels, attend(): pl.pallas_call(functools.partial(attend_kernel, cube, heads, group, [core...  101 us
    pallas_call x1, Pallas kernels, attend_back(): pl.pallas_call(functools.partial(attend_back_kernel, cube, heads, group,...  96.4 us
    pallas_call x1, Pallas kernels, start(): pl.pallas_call(functools.partial(start_kernel, cube, heads), out_shape=(j...  49.1 us
    pallas_call x1, Pallas kernels, end(): pl.pallas_call(functools.partial(end_kernel, cube, heads), out_shape=(jax...  42.7 us
    unnamed x110, local copies, waits for them, and re-layouts  12.7 us
  transfers between devices with their start and end apart: 5, of which 0 were waited for; matrix products, arithmetic and copies ran while one was open for 7% of the time, Pallas kernels for 27%

profile of v8, /device:TPU:0, one launch (start us, length us, event | category | flops | bytes accessed | tf_op | source)
XLA Modules:
  0.0 540.0 jit_solution(5293635174453348784)
XLA Ops:
  1.5 1.0 broadcast_in_dim_reshape.9.refs_3_
  3.1 0.7 pad_maximum_fusion.9
  4.0 1.0 copy.194
  5.7 1.3 constant_dynamic-slice_fusion.8
  7.0 1.1 pad_maximum_fusion.refs_2_
  8.1 49.1 %start.1 = (bf16[2,4,64,1536]{3,2,1,0:T(8,128)(2,1)}, bf16[4,2,4,48,768]{4,3,2,1,0:T(8,128)(2,1)}, bf16[10,192,256]{2,1,0:T(8,128)(2,1)}, s32[1,1024]{1,0:T(1,128)}) custom-call(bf16[2,64,1536]{2,1,0:T(8,128)(2,1)} %refs_0_.1, bf16[4,48,768]{2,1,0:T(8,128)(2,1)} %pad_maximum_fusion.5.refs_1_, bf16[10,192,256]{2,1,0:T(8,128)(2,1)} %pad_maximum_fusion.refs_2_, ...), custom_call_target="tpu_custom_call" | custom-call | tf_op jit(solution)/shard_map/start/pallas_call | solution.py:1154
  57.2 3.0 constant_dynamic-slice_fusion.1
  60.2 1.1 pad_maximum_fusion.2
  61.3 1.1 collective-permute-start
  62.4 1.1 pad_maximum_fusion.3
  63.5 1.2 fusion.23
  65.4 1.2 copy.187
  67.0 2.3 copy.157
  69.7 1.1 copy-done.28
  70.8 1.2 fusion.24
  74.0 100.8 %attend.1 = (bf16[4,128,384]{2,1,0:T(8,128)(2,1)S(1)}, bf16[4,2,2,256,256]{4,3,2,1,0:T(8,128)(2,1)}, f32[4,64,768]{2,1,0:T(8,128)S(1)}, f32[4,1,768]{2,1,0:T(1,1...) custom-call(bf16[4,768,64]{2,1,0:T(8,128)(2,1)S(1)} %bitcast.81, ...), custom_call_target="tpu_custom_call" | custom-call | tf_op jit(solution)/shard_map/attend/pallas_call | solution.py:1825
  174.9 0.9 copy-done.3
  176.0 3.4 multiply_reduce_fusion.7
  179.5 1.5 copy.188
  181.4 1.4 fusion.13
  185.2 0.9 concatenate.43.refs_0_
  186.7 2.1 pad_maximum_fusion.1.refs_3_
  188.8 2.2 bitcast_convert_fusion
  191.1 158.8 %expert_turn.1 = (f32[128,1664]{1,0:T(8,128)}, bf16[2048,1536]{1,0:T(8,128)(2,1)}, bf16[4,10,192,256]{3,2,1,0:T(8,128)(2,1)}, bf16[4,10,192,256]{3,2,1,0:T(8,128...) custom-call(bf16[128,1664]{1,0:T(8,128)(2,1)} %concatenate.43.refs_0_, bf16[2048,1536]{1,0:T(8,128)(2,1)} %bitcast.90, ...), custom_call_target="tpu_custom_call" | custom-call | tf_op jit(solution)/shard_map/expert_turn/pallas_call | solution.py:959
  349.9 0.9 slice.78
  351.0 2.0 multiply_reduce_fusion.5
  353.4 4.3 convolution_convert_fusion.1
  357.7 3.6 convolution_convert_fusion
  361.7 0.9 copy.171
  362.7 96.4 %attend_back.1 = (bf16[4,768,64]{2,1,0:T(8,128)(2,1)}, f32[512,256]{1,0:T(8,128)}, f32[128,1536]{1,0:T(8,128)}, f32[48,1536]{1,0:T(8,128)}, bf16[10,192,256]{2,1...) custom-call(bf16[4,768,64]{2,1,0:T(8,128)(2,1)} %bitcast.82, ...), custom_call_target="tpu_custom_call" | custom-call | tf_op jit(solution)/shard_map/attend_back/pallas_call | solution.py:2060
  459.3 1.9 collective-permute-start.3
  461.2 1.5 collective-permute-start.4
  462.7 1.1 convert_element_type.173
  467.1 2.7 multiply_reduce_fusion
  470.7 0.9 copy.178
  471.6 2.3 multiply_convert_fusion.left_ref
  474.3 1.1 copy.181.right_ref
  475.4 1.1 copy-done.4
  476.5 1.4 copy-done.11
  477.9 42.7 %end.1 = (bf16[4,2,64,1536]{3,2,1,0:T(8,128)(2,1)S(1)}, bf16[4,48,768]{2,1,0:T(8,128)(2,1)S(1)}) custom-call(bf16[2,4,64,1536]{3,2,1,0:T(8,128)(2,1)S(1)} %bitcast.85, bf16[512,1536]{1,0:T(8,128)(2,1)S(1)} %multiply_convert_fusion.left_ref, bf16[512,640]{1,0:T(8,128)(2,1)S(1)} %copy-done.4, bf16[1536,128]{1,0:T(8,128)(2,1)S(1)} %maximum_maximum_fusion.extra_ref), custom_call_target="tpu_custom_call" | custom-call | flops 2000000000 | bytes 1000000 | tf_op jit(solution)/shard_map/end/pallas_call | solution.py:1285
  520.6 2.5 convert_add_fusion
  523.2 6.7 %place_units.1 = f32[10,192,1024]{2,1,0:T(8,128)} custom-call(bf16[10,192,256]{2,1,0:T(8,128)(2,1)} %get-tuple-element.78.refs_0_, bf16[10,192,256]{2,1,0:T(8,128)(2,1)} %collective-permute-done.2.refs_1_, bf16[10,192,256]{2,1,0:T(8,128)(2,1)} %collective-permute-done.3.refs_2_, bf16[10,192,256]{2,1,0:T(8,128)(2,1)} %collective-permute-done.4.refs_3_), custom_call_target="tpu_custom_call" | custom-call | tf_op jit(solution)/shard_map/place_units/pallas_call | solution.py:1332
  529.9 0.8 slice_bitcast_fusion.1
  531.4 0.8 add_convert_fusion
  532.9 1.8 copy.191
  534.7 1.5 slice_reduce_fusion.1
  536.2 1.4 copy.183
  537.6 1.2 fusion.4
  (187 shorter events, 17.0 us)
Async XLA Ops:
  60.2 3.4 copy-start.24
  61.3 129.7 %collective-permute-start = (bf16[10,192,256]{2,1,0:T(8,128)(2,1)}, bf16[10,192,256]{2,1,0:T(8,128)(2,1)}, u32[]{:S(2)}, u32[]{:S(2)}) collective-permute-start(bf16[10,192,256]{2,1,0:T(8,128)(2,1)} %pad_maximum_fusion.2), channel_id=1, source_target_pairs={{0,8},{8,0},{16,24},{24,16},{1,9},{9,1},{17,25},{25,17},{2,10},{10... | collective-permute-start | bytes 2949128 | tf_op jit(solution)/shard_map/ppermute | solution.py:1345
  63.5 127.5 %collective-permute-start.1 = (bf16[10,192,256]{2,1,0:T(8,128)(2,1)}, bf16[10,192,256]{2,1,0:T(8,128)(2,1)}, u32[]{:S(2)}, u32[]{:S(2)}) collective-permute-start(bf16[10,192,256]{2,1,0:T(8,128)(2,1)} %pad_maximum_fusion.3), channel_id=1, source_target_pairs={{0,16},{8,24},{16,0},{24,8},{1,17},{9,25},{17,1},{25,9},{2,18},{10... | collective-permute-start | bytes 2949128 | tf_op jit(solution)/shard_map/ppermute | solution.py:1345
  64.7 1.9 copy-start.15
  69.3 1.5 copy-start.28
  72.5 1.4 copy-start.37
  72.5 1.5 copy-start.1
  72.5 1.5 copy-start.7
  73.7 105.7 %copy-start = (bf16[2,2,3,256,64]{4,3,2,1,0:T(8,128)(2,1)}, bf16[2,2,3,256,64]{4,3,2,1,0:T(8,128)(2,1)S(1)}, u32[]{:S(2)}) copy-start(bf16[2,2,3,256,64]{4,3,2,1,0:T(8,128)(2,1)S(1)} %copy.158) | copy-start | bytes 1179652
  73.9 105.5 %copy-start.8 = (f32[2,1,2048]{2,1,0:T(1,128)}, f32[2,1,2048]{2,1,0:T(1,128)S(1)}, u32[]{:S(2)}) copy-start(f32[2,1,2048]{2,1,0:T(1,128)S(1)} %convert_element_type.161.refs_2_) | copy-start | bytes 49156
  74.0 105.4 %copy-start.9 = (f32[2,1,768]{2,1,0:T(1,128)}, f32[2,1,768]{2,1,0:T(1,128)S(1)}, u32[]{:S(2)}) copy-start(f32[2,1,768]{2,1,0:T(1,128)S(1)} %tile.11.refs_3_) | copy-start | bytes 18436
  175.8 3.7 copy-start.10
  176.0 3.4 copy-start.26
  176.0 5.0 copy-start.46
  179.5 173.6 %copy-start.13 = (f32[128,1536]{1,0:T(8,128)}, f32[128,1536]{1,0:T(8,128)S(1)}, u32[]{:S(2)}) copy-start(f32[128,1536]{1,0:T(8,128)S(1)} %get-tuple-element.153) | copy-start | bytes 2359300
  179.5 7.2 %copy-start.29 = (bf16[10,192,128]{2,1,0:T(8,128)(2,1)S(1)}, bf16[10,192,128]{2,1,0:T(8,128)(2,1)}, u32[]{:S(2)}) copy-start(bf16[10,192,128]{2,1,0:T(8,128)(2,1)} %get-tuple-element.137) | copy-start | bytes 1474564
  179.5 1.7 copy-start.42
  181.4 9.6 %copy-start.22 = (bf16[128,1536]{1,0:T(8,128)(2,1)}, bf16[128,1536]{1,0:T(8,128)(2,1)S(1)}, u32[]{:S(2)}) copy-start(bf16[128,1536]{1,0:T(8,128)(2,1)S(1)} %multiply_convert_fusion.2) | copy-start | bytes 1179652
  181.4 7.4 %copy-start.16 = (bf16[2,4,64,1536]{3,2,1,0:T(8,128)(2,1)S(1)}, bf16[2,4,64,1536]{3,2,1,0:T(8,128)(2,1)}, u32[]{:S(2)}) copy-start(bf16[2,4,64,1536]{3,2,1,0:T(8,128)(2,1)} %get-tuple-element.52) | copy-start | bytes 4718596
  183.5 7.5 %copy-start.44 = (f32[2,64]{1,0:T(2,128)}, f32[2,64]{1,0:T(2,128)S(1)}, u32[]{:S(2)}) copy-start(f32[2,64]{1,0:T(2,128)S(1)} %add_rsqrt_fusion.2) | copy-start | bytes 1540
  191.0 159.9 %copy-start.39 = (f32[128]{0:T(128)S(1)}, f32[128]{0:T(128)}, u32[]{:S(2)}) copy-start(f32[128]{0:T(128)} %copy-done.38) | copy-start | bytes 1540
  191.0 159.9 %copy-start.41 = (f32[128]{0:T(128)S(1)}, f32[128]{0:T(128)}, u32[]{:S(2)}) copy-start(f32[128]{0:T(128)} %copy-done.40) | copy-start | bytes 1540
  191.1 159.9 %copy-start.43 = (f32[128]{0:T(128)S(1)}, f32[128]{0:T(128)}, u32[]{:S(2)}) copy-start(f32[128]{0:T(128)} %copy-done.42) | copy-start | bytes 1540
  349.9 3.2 copy-start.2
  353.3 4.3 copy-start.18
  353.3 4.3 copy-start.27
  357.7 3.6 copy-start.23
  459.1 5.5 %copy-start.33 = (bf16[4,768,64]{2,1,0:T(8,128)(2,1)S(1)}, bf16[4,768,64]{2,1,0:T(8,128)(2,1)}, u32[]{:S(2)}) copy-start(bf16[4,768,64]{2,1,0:T(8,128)(2,1)} %get-tuple-element.71) | copy-start | bytes 1179652
  459.1 64.0 %collective-permute-start.2 = (bf16[10,192,256]{2,1,0:T(8,128)(2,1)}, bf16[10,192,256]{2,1,0:T(8,128)(2,1)}, u32[]{:S(2)}, u32[]{:S(2)}) collective-permute-start(bf16[10,192,256]{2,1,0:T(8,128)(2,1)} %get-tuple-element.68), channel_id=1, source_target_pairs={{0,8},{8,0},{16,24},{24,16},{1,9},{9,1},{17,25},{25,17},{2,10},{10... | collective-permute-start | bytes 2949128 | tf_op jit(solution)/shard_map/ppermute | solution.py:1345
  459.3 63.8 %collective-permute-start.3 = (bf16[10,192,256]{2,1,0:T(8,128)(2,1)}, bf16[10,192,256]{2,1,0:T(8,128)(2,1)}, u32[]{:S(2)}, u32[]{:S(2)}) collective-permute-start(bf16[10,192,256]{2,1,0:T(8,128)(2,1)} %get-tuple-element.69), channel_id=1, source_target_pairs={{0,16},{8,24},{16,0},{24,8},{1,17},{9,25},{17,1},{25,9},{2,18},{10... | collective-permute-start | bytes 2949128 | tf_op jit(solution)/shard_map/ppermute | solution.py:1345
  461.2 61.9 %collective-permute-start.4 = (bf16[10,192,256]{2,1,0:T(8,128)(2,1)}, bf16[10,192,256]{2,1,0:T(8,128)(2,1)}, u32[]{:S(2)}, u32[]{:S(2)}) collective-permute-start(bf16[10,192,256]{2,1,0:T(8,128)(2,1)} %get-tuple-element.70), channel_id=1, source_target_pairs={{0,24},{8,16},{16,8},{24,0},{1,25},{9,17},{17,9},{25,1},{2,26},{10... | collective-permute-start | bytes 2949128 | tf_op jit(solution)/shard_map/ppermute | solution.py:1345
  464.9 1.4 copy-start.17
  465.0 2.1 copy-start.25
  465.0 2.1 copy-start.47
  467.1 2.8 copy-start.12
  471.6 2.3 copy-start.32
  471.6 2.3 copy-start.49
  477.9 42.7 %copy-start.30 = (bf16[10,64,1536]{2,1,0:T(8,128)(2,1)S(1)}, bf16[10,64,1536]{2,1,0:T(8,128)(2,1)}, u32[]{:S(2)}) copy-start(bf16[10,64,1536]{2,1,0:T(8,128)(2,1)} %get-tuple-element.85) | copy-start | bytes 5898244
  477.9 42.7 %copy-start.31 = (bf16[10,64,1536]{2,1,0:T(8,128)(2,1)S(1)}, bf16[10,64,1536]{2,1,0:T(8,128)(2,1)}, u32[]{:S(2)}) copy-start(bf16[10,64,1536]{2,1,0:T(8,128)(2,1)} %get-tuple-element.86) | copy-start | bytes 5898244
  520.6 2.6 copy-start.5
  523.1 6.7 %copy-start.6 = (bf16[4,48,768]{2,1,0:T(8,128)(2,1)S(1)}, bf16[4,48,768]{2,1,0:T(8,128)(2,1)}, u32[]{:S(2)}) copy-start(bf16[4,48,768]{2,1,0:T(8,128)(2,1)} %copy-done.5) | copy-start | bytes 884740
  529.9 1.5 copy-start.14
  529.9 1.5 copy-start.34
  530.7 1.7 copy-start.21
  530.8 1.7 copy-start.45
  532.3 5.4 copy-start.19
  532.3 5.4 copy-start.48
  532.5 6.3 %copy-start.35 = (f32[48,1536]{1,0:T(8,128)S(1)}, f32[48,1536]{1,0:T(8,128)}, u32[]{:S(2)}) copy-start(f32[48,1536]{1,0:T(8,128)} %get-tuple-element.168) | copy-start | bytes 884740
  (8 other events, 7.4 us)
